TPU v7x, 32 devices: a whole 2x2x4 slice. The times are simulated.
32 devices in a mesh: gx: 8 (over y, x, core), gy: 4 (over z).
Axes of the slice: x: 2, y: 2, z: 4, core: 2. Of those that a mesh axis runs over, the one named last changes fastest.
Arguments:
- density: float32 [256, 512, 256], P('gx', 'gy'), as said below
- reaction_rates: float32 [6], replicated, may hold values from 0.3 to 3
- state_changes: int32 [6, 3], replicated, may hold values from -2 to 2, as said below
- target_box: int32 [2, 3], replicated, may hold values from 0 to 512, as said below
- truncation: int32 [2], replicated, may hold values from 5 to 16
Outputs:
- occupancy: float32 [256, 512, 256], P('gx', 'gy')
- summary: float32 [2], replicated
Inputs may be any that keep to these rules, and one draw needn't show every extreme that they name: density is positive. `state_changes`: each row is one reaction's change of the three counts; for each of the first two species, some reaction changes it by 2 and some by -2. For each species, target_box[0, d] < target_box[1, d], and target_box[1, d] is at most that species' number of counts; along the species with the most counts the box reaches the lattice's end.
All inputs are finite; a program needn't handle non-finite values.
Results may differ from a plain program's by a relative error of at most 0.0001.
Values sent between devices are 32-bit elements; how exact they have to be, the bound alone decides.
No kernel may reach another device: no remote copies, remote signals or barrier semaphores. Data moves between devices by JAX's collectives and lax.ppermute only.
A program may use at most 256 MiB of HBM per device.

v0:
```python
import math

import jax
import jax.numpy as jnp
from jax import lax
from jax.sharding import PartitionSpec as P

STEPS = 4


mean_jumps = 8.0
headroom = 1.05
series_length = 40


def extended_2(cells, sides, width):
    for axis, dim in sides:
        count = lax.axis_size(axis)
        ends = count - 1
        head = lax.slice_in_dim(cells, 0, width, axis=dim)
        tail = lax.slice_in_dim(cells, cells.shape[dim] - width, cells.shape[dim], axis=dim)
        cells = jnp.concatenate(
            [
                lax.ppermute(tail, axis, [(i, (i + 1) % count) for i in range(ends)]),
                cells,
                lax.ppermute(head, axis, [((i + 1) % count, i) for i in range(ends)]),
            ],
            axis=dim,
        )
    return cells


def propensity_factor(counts, reactant_order, extent):
    values = counts.astype(jnp.float32)
    linear = values / extent
    square = values * (values - 1.0) / (extent * extent)
    return jnp.where(
        reactant_order == 0, jnp.ones_like(values), jnp.where(reactant_order == 1, linear, square)
    )


def box_indicator(counts, target_box, axis_number):
    return ((counts >= target_box[0, axis_number]) & (counts < target_box[1, axis_number])).astype(
        jnp.float32
    )


def outer_three(along_first, along_second, along_third):
    return along_first[:, None, None] * along_second[None, :, None] * along_third[None, None, :]


def jump_weights(truncation):
    table = [
        math.exp(-mean_jumps) * mean_jumps**jump_index / math.factorial(jump_index)
        for jump_index in range(series_length)
    ]
    weights = [jnp.float32(table[jump_index]) for jump_index in range(STEPS + 1)]
    tails = []
    for which in range(2):
        tail_weight = jnp.float32(0.0)
        for jump_index in range(STEPS + 1, series_length):
            taken = (jump_index <= truncation[which]).astype(jnp.float32)
            tail_weight = tail_weight + taken * jnp.float32(table[jump_index])
        tails.append(tail_weight)
    return (weights, tails[0], tails[1])


def body(density, reaction_rates, state_changes, target_box, truncation):
    block_first, block_second, species_third = density.shape
    extent_first = block_first * lax.axis_size("gx")
    extent_second = block_second * lax.axis_size("gy")
    anchor_first = lax.axis_index("gx") * block_first
    anchor_second = lax.axis_index("gy") * block_second
    extents = (extent_first, extent_second, species_third)
    reactant_orders = jnp.maximum(-state_changes, 0)
    reaction_total = state_changes.shape[0]
    corner = None
    for reaction in range(reaction_total):
        corner_term = reaction_rates[reaction]
        for axis_number in range(3):
            last_count = jnp.full((1,), extents[axis_number] - 1, jnp.int32)
            corner_term = (
                corner_term
                * propensity_factor(
                    last_count, reactant_orders[reaction, axis_number], float(extents[axis_number])
                )[0]
            )
        corner = corner_term if corner is None else corner + corner_term
    uniform_rate = headroom * corner

    def advance(extended, margin):
        length_first = extended.shape[0]
        length_second = extended.shape[1]
        counts_first = anchor_first - margin + jnp.arange(length_first, dtype=jnp.int32)
        counts_second = anchor_second - margin + jnp.arange(length_second, dtype=jnp.int32)
        counts_third = jnp.arange(-2, species_third + 2, dtype=jnp.int32)
        count_grids = (counts_first, counts_second, counts_third)
        free = 1.0 - outer_three(
            box_indicator(counts_first, target_box, 0),
            box_indicator(counts_second, target_box, 1),
            box_indicator(counts_third, target_box, 2),
        )
        padded = jnp.pad(extended, ((0, 0), (0, 0), (2, 2)))
        scaled = padded * free / uniform_rate
        coefficients = []
        for reaction in range(reaction_total):
            factors = [
                propensity_factor(
                    count_grids[axis_number],
                    reactant_orders[reaction, axis_number],
                    float(extents[axis_number]),
                )
                for axis_number in range(3)
            ]
            coefficients.append(
                outer_three(reaction_rates[reaction] * factors[0], factors[1], factors[2])
            )
        total_rate = coefficients[0]
        for reaction in range(1, reaction_total):
            total_rate = total_rate + coefficients[reaction]
        advanced = extended[2:-2, 2:-2, :] - total_rate[2:-2, 2:-2, 2:-2] * scaled[2:-2, 2:-2, 2:-2]
        for reaction in range(reaction_total):
            flux_term = scaled * coefficients[reaction]
            start = [2 - state_changes[reaction, axis_number] for axis_number in range(3)]
            arrival = lax.dynamic_slice(
                flux_term, start, (length_first - 4, length_second - 4, species_third)
            )
            advanced = advanced + arrival
        return advanced

    interior_box = outer_three(
        box_indicator(anchor_first + jnp.arange(block_first, dtype=jnp.int32), target_box, 0),
        box_indicator(anchor_second + jnp.arange(block_second, dtype=jnp.int32), target_box, 1),
        box_indicator(jnp.arange(species_third, dtype=jnp.int32), target_box, 2),
    )
    mass_sums = []
    hit_sums = []

    def record(current):
        local_sums = (jnp.sum(current), jnp.sum(current * interior_box))
        local_sums = lax.psum((local_sums[0], local_sums[1]), ("gx", "gy"))
        mass_sums.append(local_sums[0])
        hit_sums.append(local_sums[1])

    weights, tail_density, tail_totals = jump_weights(truncation)
    current = density
    record(current)
    accumulated = weights[0] * density
    for jump_index in range(1, STEPS + 1):
        extended = extended_2(current, (("gx", 0), ("gy", 1)), 2)
        current = advance(extended, 2)
        record(current)
        accumulated = accumulated + weights[jump_index] * current
    occupancy = accumulated + tail_density * current
    reached = weights[0] * hit_sums[0]
    retained = weights[0] * mass_sums[0]
    for jump_index in range(1, STEPS + 1):
        reached = reached + weights[jump_index] * hit_sums[jump_index]
        retained = retained + weights[jump_index] * mass_sums[jump_index]
    cell_total = float(extent_first * extent_second * species_third)
    reached = (reached + tail_totals * hit_sums[STEPS]) / cell_total
    retained = (retained + tail_totals * mass_sums[STEPS]) / cell_total
    return (occupancy, jnp.stack([reached, retained]))


def solution(mesh):
    placed = (P("gx", "gy", None), P(), P(), P(), P())
    return jax.shard_map(
        body, mesh=mesh, in_specs=placed, out_specs=(P("gx", "gy", None), P()), check_vma=False
    )
```

profile of v0, /device:TPU:0, one launch (start us, length us, event | category | flops | bytes accessed | tf_op | source)
XLA Modules:
  0.0 452.9 jit_solution(1418222518418801072)
XLA Ops:
  1.7 2.4 collective-permute-start
  4.1 1.3 collective-permute-start.1
  28.8 2.1 fusion.61
  30.8 1.5 fusion.65
  32.4 1.5 fusion.63
  33.9 1.3 and_convert_fusion.3
  35.3 1.3 fusion.53
  36.7 3.4 broadcast_multiply_fusion
  40.2 3.5 broadcast_multiply_fusion.1
  44.9 3.5 broadcast_multiply_fusion.2
  48.5 3.5 broadcast_multiply_fusion.3
  52.0 1.3 fusion.49
  53.3 3.5 broadcast_multiply_fusion.4
  57.0 3.4 broadcast_multiply_fusion.5
  60.4 1.3 and_convert_fusion.4
  87.8 3.1 constant_dynamic-update-slice_fusion.1
  91.0 4.3 collective-permute-start.2
  95.3 1.3 collective-permute-start.3
  97.8 3.8 collective-permute-done.3
  101.6 4.5 fusion.7
  106.1 31.7 %fusion.35 = (f32[32,128,256]{2,1,0:T(8,128)S(1)}, f32[32,128,256]{2,1,0:T(8,128)}) fusion(f32[36,132,260]{2,1,0:T(8,128)S(1)} %fusion.7, s32[]{:T(128)S(6)} %select_n.1085, s32[]{:T(128)S(6)} %select_n.1086, s32[]{:T(128)S(6)} %select_n.1087, s32[]{:T(128)S(6)} %select_n.1082, s32[]{:T(128)S(6)} %select_n.1083, s32[]{:T(128)S(6)} %select_n.1084, ...), kind=kLoop, calls=%fused_computation.79 | loop fusion | flops 19922944 | bytes 92274760 | tf_op jit(solution)/shard_map/add | solution.py:128
  137.8 2.9 collective-permute-start.4
  140.7 1.3 collective-permute-start.5
  142.0 4.8 %collective-permute-done.5 = f32[2,128,256]{2,1,0:T(8,128)S(1)} collective-permute-done((f32[2,128,256]{2,1,0:T(8,128)S(1)}, f32[2,128,256]{2,1,0:T(8,128)S(1)}, u32[]{:S(2)}, u32[]{:S(2)}) %collective-permute-start.5) | collective-permute-done | bytes 262176 | tf_op jit(solution)/shard_map/ppermute | solution.py:26
  146.9 3.5 collective-permute-start.6
  150.3 1.5 collective-permute-start.7
  152.3 4.3 collective-permute-done.7
  156.6 8.8 %fusion.5 = f32[36,132,260]{2,1,0:T(8,128)} fusion(f32[36,2,256]{2,1,0:T(2,128)S(1)} %collective-permute-done.7, f32[36,2,256]{2,1,0:T(2,128)S(1)} %collective-permute-done.6, f32[2,128,256]{2,1,0:T(8,128)S(1)} %collective-permute-done.5, f32[32,128,256]{2,1,0:T(8,128)S(1)} %get-tuple-element.31, f32[2,128,256]{2,1,0:T(8,128)S(1)} %collective-permute-done.4, ...), kind=kLoop, calls=%fused_computation.21 | loop fusion | flops 19768320 | bytes 9828180 | tf_op jit(solution)/shard_map/div | solution.py:104
  165.4 39.4 %fusion.28 = f32[32,128,256]{2,1,0:T(8,128)} fusion(f32[36,132,260]{2,1,0:T(8,128)} %fusion.5, s32[]{:T(128)S(6)} %select_n.1085, s32[]{:T(128)S(6)} %select_n.1086, s32[]{:T(128)S(6)} %select_n.1087, s32[]{:T(128)S(6)} %select_n.1082, s32[]{:T(128)S(6)} %select_n.1083, s32[]{:T(128)S(6)} %select_n.1084, s32[]{:T(128)S(6)} %select_n.1079, ...), kind=kLoop, calls=%fused_computation.65 | loop fusion | flops 14680064 | bytes 67108936 | tf_op jit(solution)/shard_map/add | solution.py:128
  206.1 6.6 %collective-permute-start.8 = (f32[2,128,256]{2,1,0:T(8,128)S(1)}, f32[2,128,256]{2,1,0:T(8,128)S(1)}, u32[]{:S(2)}, u32[]{:S(2)}) collective-permute-start(f32[2,128,256]{2,1,0:T(8,128)S(1)} %get-tuple-element.43), channel_id=1, source_target_pairs={{0,4},{4,8},{8,12},{12,16},{16,20},{20,24},{24,28},{1,5},{5,9},{9,... | collective-permute-start | bytes 786440 | tf_op jit(solution)/shard_map/ppermute | solution.py:24
  212.8 1.3 collective-permute-start.9
  214.7 2.0 collective-permute-done.9
  217.7 3.5 collective-permute-start.10
  221.2 1.3 collective-permute-start.11
  222.5 1.3 and_convert_fusion.2
  223.8 3.6 collective-permute-done.11
  227.5 8.8 %fusion.3 = f32[36,132,260]{2,1,0:T(8,128)} fusion(f32[36,2,256]{2,1,0:T(2,128)S(1)} %collective-permute-done.11, f32[36,2,256]{2,1,0:T(2,128)S(1)} %collective-permute-done.10, f32[2,128,256]{2,1,0:T(8,128)S(1)} %collective-permute-done.9, f32[32,128,256]{2,1,0:T(8,128)S(1)} %copy-done.1, f32[2,128,256]{2,1,0:T(8,128)S(1)} %collective-permute-done.8, ...), kind=kLoop, calls=%fused_computation.15 | loop fusion | flops 19768320 | bytes 9828180 | tf_op jit(solution)/shard_map/div | solution.py:104
  236.3 39.4 %fusion.21 = f32[32,128,256]{2,1,0:T(8,128)} fusion(f32[36,132,260]{2,1,0:T(8,128)} %fusion.3, s32[]{:T(128)S(6)} %select_n.1085, s32[]{:T(128)S(6)} %select_n.1086, s32[]{:T(128)S(6)} %select_n.1087, s32[]{:T(128)S(6)} %select_n.1082, s32[]{:T(128)S(6)} %select_n.1083, s32[]{:T(128)S(6)} %select_n.1084, s32[]{:T(128)S(6)} %select_n.1079, ...), kind=kLoop, calls=%fused_computation.51 | loop fusion | flops 14680064 | bytes 67108936 | tf_op jit(solution)/shard_map/add | solution.py:128
  276.8 6.1 %collective-permute-start.12 = (f32[2,128,256]{2,1,0:T(8,128)S(1)}, f32[2,128,256]{2,1,0:T(8,128)S(1)}, u32[]{:S(2)}, u32[]{:S(2)}) collective-permute-start(f32[2,128,256]{2,1,0:T(8,128)S(1)} %get-tuple-element.41), channel_id=1, source_target_pairs={{0,4},{4,8},{8,12},{12,16},{16,20},{20,24},{24,28},{1,5},{5,9},{9,... | collective-permute-start | bytes 786440 | tf_op jit(solution)/shard_map/ppermute | solution.py:24
  283.0 1.5 collective-permute-start.13
  284.5 1.3 and_convert_fusion.1
  333.4 2.3 collective-permute-start.14
  335.8 1.3 collective-permute-start.15
  338.2 4.3 collective-permute-done.15
  342.5 8.8 %fusion.1 = f32[36,132,260]{2,1,0:T(8,128)} fusion(f32[36,2,256]{2,1,0:T(2,128)S(1)} %collective-permute-done.15, f32[36,2,256]{2,1,0:T(2,128)S(1)} %collective-permute-done.14, f32[2,128,256]{2,1,0:T(8,128)S(1)} %collective-permute-done.13, f32[32,128,256]{2,1,0:T(8,128)S(1)} %copy-done.2, f32[2,128,256]{2,1,0:T(8,128)S(1)} %collective-permute-done.12, ...), kind=kLoop, calls=%fused_computation.9 | loop fusion | flops 19768320 | bytes 9828180 | tf_op jit(solution)/shard_map/div | solution.py:104
  351.4 42.4 %fusion.13 = (f32[]{:T(128)}, f32[]{:T(128)}, f32[]{:T(128)}, f32[]{:T(128)}, f32[]{:T(128)}, /*index=5*/f32[]{:T(128)}, f32[]{:T(128)}, f32[]{:T(128)}, f32[]{:T(128)}, f32[]{:T(128)}, /*index=10*/f32[32,128,256]{2,1,0:T(8,128)}) fusion(f32[256]{0:T(256)S(1)} %and_convert_fusion, f32[32,128]{1,0:T(8,128)S(1)} %broadcast_multiply_fusion.13, ...), kind=kLoop, calls=%fused_computation.35 | loop fusion | flops 31457280 | bytes 79709296 | tf_op jit(solution)/shard_map/reduce_sum | solution.py:140
  393.8 40.8 %all-reduce.4 = (f32[]{:T(128)}, f32[]{:T(128)}, f32[]{:T(128)}, f32[]{:T(128)}, f32[]{:T(128)}, /*index=5*/f32[]{:T(128)}, f32[]{:T(128)}, f32[]{:T(128)}, f32[]{:T(128)}, f32[]{:T(128)}) all-reduce(f32[]{:T(128)} %get-tuple-element.18, f32[]{:T(128)} %get-tuple-element.16, ...), channel_id=1, replica_groups=mesh['gx'=8,'gy'=4] {'gx','gy'}, use_global_device_ids=true, to_apply=%region_11.12 | all-reduce | flops 10 | bytes 80 | tf_op jit(solution)/shard_map/psum | solution.py:141
  442.6 10.3 %multiply_add_fusion = f32[32,128,256]{2,1,0:T(8,128)} fusion(f32[32,128,256]{2,1,0:T(8,128)} %get-tuple-element.30, f32[32,128,256]{2,1,0:T(8,128)} %fusion.21, f32[32,128,256]{2,1,0:T(8,128)} %fusion.28, f32[32,128,256]{2,1,0:T(8,128)} %copy-done, f32[32,128,256]{2,1,0:T(8,128)} %param.5, f32[]{:T(128)S(6)} %add.881), kind=kLoop, calls=%fused_computation.97 | loop fusion | flops 11534336 | bytes 25165828 | tf_op jit(solution)/shard_map/add | solution.py:154
  (57 shorter events, 13.0 us)
Async XLA Ops:
  1.7 86.1 %collective-permute-start = (f32[2,128,256]{2,1,0:T(8,128)S(1)}, f32[2,128,256]{2,1,0:T(8,128)S(1)}, u32[]{:S(2)}, u32[]{:S(2)}) collective-permute-start(f32[2,128,256]{2,1,0:T(8,128)S(1)} %get-tuple-element.48), channel_id=1, source_target_pairs={{0,4},{4,8},{8,12},{12,16},{16,20},{20,24},{24,28},{1,5},{5,9},{9,... | collective-permute-start | bytes 786440 | tf_op jit(solution)/shard_map/ppermute | solution.py:24
  4.1 86.8 %collective-permute-start.1 = (f32[2,128,256]{2,1,0:T(8,128)S(1)}, f32[2,128,256]{2,1,0:T(8,128)S(1)}, u32[]{:S(2)}, u32[]{:S(2)}) collective-permute-start(f32[2,128,256]{2,1,0:T(8,128)S(1)} %get-tuple-element.47), channel_id=1, source_target_pairs={{4,0},{8,4},{12,8},{16,12},{20,16},{24,20},{28,24},{5,1},{9,5},{13... | collective-permute-start | bytes 786440 | tf_op jit(solution)/shard_map/ppermute | solution.py:26
  87.8 18.2 %slice-start = ((s8[7520256]{0:T(1024)(128)(4,1)}), s8[4194304]{0:T(1024)(128)(4,1)S(1)}, s32[]{:S(2)}) async-start(s8[7520256]{0:T(1024)(128)(4,1)} %bitcast.182), calls=%async_computation | async-start | bytes 8388608
  91.0 6.8 %collective-permute-start.2 = (f32[36,2,256]{2,1,0:T(2,128)S(1)}, f32[36,2,256]{2,1,0:T(2,128)S(1)}, u32[]{:S(2)}, u32[]{:S(2)}) collective-permute-start(f32[36,2,256]{2,1,0:T(2,128)S(1)} %get-tuple-element.39), channel_id=1, source_target_pairs={{0,1},{1,2},{2,3},{4,5},{5,6},{6,7},{8,9},{9,10},{10,11},{12,13},{... | collective-permute-start | bytes 221192 | tf_op jit(solution)/shard_map/ppermute | solution.py:24
  95.3 6.2 %collective-permute-start.3 = (f32[36,2,256]{2,1,0:T(2,128)S(1)}, f32[36,2,256]{2,1,0:T(2,128)S(1)}, u32[]{:S(2)}, u32[]{:S(2)}) collective-permute-start(f32[36,2,256]{2,1,0:T(2,128)S(1)} %get-tuple-element.40), channel_id=1, source_target_pairs={{1,0},{2,1},{3,2},{5,4},{6,5},{7,6},{9,8},{10,9},{11,10},{13,12},{... | collective-permute-start | bytes 221192 | tf_op jit(solution)/shard_map/ppermute | solution.py:26
  97.8 8.3 %slice-start.1 = ((s8[7520256]{0:T(1024)(128)(4,1)}), s8[3325952]{0:T(1024)(128)(4,1)S(1)}, s32[]{:S(2)}) async-start(s8[7520256]{0:T(1024)(128)(4,1)} %bitcast.182), calls=%async_computation.1 | async-start | bytes 6651904
  137.8 27.7 %copy-start = (f32[32,128,256]{2,1,0:T(8,128)}, f32[32,128,256]{2,1,0:T(8,128)S(1)}, u32[]{:S(2)}) copy-start(f32[32,128,256]{2,1,0:T(8,128)S(1)} %get-tuple-element.31) | copy-start | bytes 12582916
  137.8 4.2 collective-permute-start.4
  140.7 6.1 %collective-permute-start.5 = (f32[2,128,256]{2,1,0:T(8,128)S(1)}, f32[2,128,256]{2,1,0:T(8,128)S(1)}, u32[]{:S(2)}, u32[]{:S(2)}) collective-permute-start(f32[2,128,256]{2,1,0:T(8,128)S(1)} %get-tuple-element.46), channel_id=1, source_target_pairs={{4,0},{8,4},{12,8},{16,12},{20,16},{24,20},{28,24},{5,1},{9,5},{13... | collective-permute-start | bytes 786440 | tf_op jit(solution)/shard_map/ppermute | solution.py:26
  146.9 5.5 %collective-permute-start.6 = (f32[36,2,256]{2,1,0:T(2,128)S(1)}, f32[36,2,256]{2,1,0:T(2,128)S(1)}, u32[]{:S(2)}, u32[]{:S(2)}) collective-permute-start(f32[36,2,256]{2,1,0:T(2,128)S(1)} %get-tuple-element.37), channel_id=1, source_target_pairs={{0,1},{1,2},{2,3},{4,5},{5,6},{6,7},{8,9},{9,10},{10,11},{12,13},{... | collective-permute-start | bytes 221192 | tf_op jit(solution)/shard_map/ppermute | solution.py:24
  150.3 6.2 %collective-permute-start.7 = (f32[36,2,256]{2,1,0:T(2,128)S(1)}, f32[36,2,256]{2,1,0:T(2,128)S(1)}, u32[]{:S(2)}, u32[]{:S(2)}) collective-permute-start(f32[36,2,256]{2,1,0:T(2,128)S(1)} %get-tuple-element.38), channel_id=1, source_target_pairs={{1,0},{2,1},{3,2},{5,4},{6,5},{7,6},{9,8},{10,9},{11,10},{13,12},{... | collective-permute-start | bytes 221192 | tf_op jit(solution)/shard_map/ppermute | solution.py:26
  165.4 48.6 %copy-start.3 = (s32[2]{0:T(128)S(1)}, s32[2]{0:T(128)}, u32[]{:S(2)}) copy-start(s32[2]{0:T(128)} %param.9) | copy-start | bytes 28
  204.9 22.6 %copy-start.1 = (f32[32,128,256]{2,1,0:T(8,128)S(1)}, f32[32,128,256]{2,1,0:T(8,128)}, u32[]{:S(2)}) copy-start(f32[32,128,256]{2,1,0:T(8,128)} %fusion.28) | copy-start | bytes 12582916
  206.1 8.6 %collective-permute-start.8 = (f32[2,128,256]{2,1,0:T(8,128)S(1)}, f32[2,128,256]{2,1,0:T(8,128)S(1)}, u32[]{:S(2)}, u32[]{:S(2)}) collective-permute-start(f32[2,128,256]{2,1,0:T(8,128)S(1)} %get-tuple-element.43), channel_id=1, source_target_pairs={{0,4},{4,8},{8,12},{12,16},{16,20},{20,24},{24,28},{1,5},{5,9},{9,... | collective-permute-start | bytes 786440 | tf_op jit(solution)/shard_map/ppermute | solution.py:24
  212.8 3.9 collective-permute-start.9
  217.7 6.1 %collective-permute-start.10 = (f32[36,2,256]{2,1,0:T(2,128)S(1)}, f32[36,2,256]{2,1,0:T(2,128)S(1)}, u32[]{:S(2)}, u32[]{:S(2)}) collective-permute-start(f32[36,2,256]{2,1,0:T(2,128)S(1)} %get-tuple-element.35), channel_id=1, source_target_pairs={{0,1},{1,2},{2,3},{4,5},{5,6},{6,7},{8,9},{9,10},{10,11},{12,13},{... | collective-permute-start | bytes 221192 | tf_op jit(solution)/shard_map/ppermute | solution.py:24
  221.2 6.2 %collective-permute-start.11 = (f32[36,2,256]{2,1,0:T(2,128)S(1)}, f32[36,2,256]{2,1,0:T(2,128)S(1)}, u32[]{:S(2)}, u32[]{:S(2)}) collective-permute-start(f32[36,2,256]{2,1,0:T(2,128)S(1)} %get-tuple-element.36), channel_id=1, source_target_pairs={{1,0},{2,1},{3,2},{5,4},{6,5},{7,6},{9,8},{10,9},{11,10},{13,12},{... | collective-permute-start | bytes 221192 | tf_op jit(solution)/shard_map/ppermute | solution.py:26
  276.8 55.4 %collective-permute-start.12 = (f32[2,128,256]{2,1,0:T(8,128)S(1)}, f32[2,128,256]{2,1,0:T(8,128)S(1)}, u32[]{:S(2)}, u32[]{:S(2)}) collective-permute-start(f32[2,128,256]{2,1,0:T(8,128)S(1)} %get-tuple-element.41), channel_id=1, source_target_pairs={{0,4},{4,8},{8,12},{12,16},{16,20},{20,24},{24,28},{1,5},{5,9},{9,... | collective-permute-start | bytes 786440 | tf_op jit(solution)/shard_map/ppermute | solution.py:24
  283.0 49.2 %collective-permute-start.13 = (f32[2,128,256]{2,1,0:T(8,128)S(1)}, f32[2,128,256]{2,1,0:T(8,128)S(1)}, u32[]{:S(2)}, u32[]{:S(2)}) collective-permute-start(f32[2,128,256]{2,1,0:T(8,128)S(1)} %get-tuple-element.42), channel_id=1, source_target_pairs={{4,0},{8,4},{12,8},{16,12},{20,16},{24,20},{28,24},{5,1},{9,5},{13... | collective-permute-start | bytes 786440 | tf_op jit(solution)/shard_map/ppermute | solution.py:26
  332.1 10.4 %copy-start.2 = (f32[32,128,256]{2,1,0:T(8,128)S(1)}, f32[32,128,256]{2,1,0:T(8,128)}, u32[]{:S(2)}) copy-start(f32[32,128,256]{2,1,0:T(8,128)} %fusion.21) | copy-start | bytes 12582916
  333.4 4.8 %collective-permute-start.14 = (f32[36,2,256]{2,1,0:T(2,128)S(1)}, f32[36,2,256]{2,1,0:T(2,128)S(1)}, u32[]{:S(2)}, u32[]{:S(2)}) collective-permute-start(f32[36,2,256]{2,1,0:T(2,128)S(1)} %get-tuple-element.33), channel_id=1, source_target_pairs={{0,1},{1,2},{2,3},{4,5},{5,6},{6,7},{8,9},{9,10},{10,11},{12,13},{... | collective-permute-start | bytes 221192 | tf_op jit(solution)/shard_map/ppermute | solution.py:24
  335.8 6.8 %collective-permute-start.15 = (f32[36,2,256]{2,1,0:T(2,128)S(1)}, f32[36,2,256]{2,1,0:T(2,128)S(1)}, u32[]{:S(2)}, u32[]{:S(2)}) collective-permute-start(f32[36,2,256]{2,1,0:T(2,128)S(1)} %get-tuple-element.34), channel_id=1, source_target_pairs={{1,0},{2,1},{3,2},{5,4},{6,5},{7,6},{9,8},{10,9},{11,10},{13,12},{... | collective-permute-start | bytes 221192 | tf_op jit(solution)/shard_map/ppermute | solution.py:26
where the time goes:
time: 456 us; the launch traced here: 453 us
  other arithmetic  230 us (50%)
  between operations  103 us (23%)
  starting transfers between devices  42.4 us (9%)
  blocking collectives  40.8 us (9%)
  waiting for transfers between devices  23.3 us (5%)
  local copies, waits for them, and re-layouts  13 us (3%)
    add x3, other arithmetic, advance(): advanced = advanced + arrival  111 us
    reduce_sum x1, other arithmetic, record(): local_sums = (jnp.sum(current), jnp.sum(current * interior_box))  42.4 us
    psum x1, blocking collectives, record(): local_sums = lax.psum((local_sums[0], local_sums[1]), ('gx', 'gy'))  40.8 us
    ppermute x8, starting transfers between devices, extended_2(): lax.ppermute(tail, axis, [(i, (i + 1) % count) for i in range(ends)])  31.7 us
    div x4, other arithmetic, advance(): scaled = padded * free / uniform_rate  31 us
    ppermute x8, waiting for transfers between devices, extended_2(): lax.ppermute(head, axis, [((i + 1) % count, i) for i in range(ends)])  22.8 us
    mul x14, other arithmetic, outer_three(): along_first[:, None, None] * along_second[None, :, None]  21.4 us
    ppermute x8, starting transfers between devices, extended_2(): lax.ppermute(head, axis, [((i + 1) % count, i) for i in range(ends)])  10.7 us
  transfers between devices with their start and end apart: 16, of which 7 were waited for; matrix products, arithmetic and copies ran while one was open for 9% of the time, Pallas kernels for 0%

commit v1 on v0

v1 whole, which is shorter than its diff:
```python
import functools
import math

import jax
import jax.numpy as jnp
from jax import lax
from jax.experimental import pallas as pl
from jax.experimental.pallas import tpu as pltpu
from jax.sharding import PartitionSpec as P

STEPS = 4
REACTIONS = 6
HALO = 2 * STEPS
LANES = 128
ROWS = 16
PAD = 8

mean_jumps = 8.0
headroom = 1.05
series_length = 40

VMEM_LIMIT = 62 << 20


def largest_divisor(number, limit):
    return max(u for u in range(1, limit + 1) if number % u == 0)


def counts_factor(values, order, extent):
    linear = values * (1.0 / extent)
    square = values * (values - 1.0) * (1.0 / (extent * extent))
    return jnp.where(order == 0, 1.0, jnp.where(order == 1, linear, square))


def tables_kernel(
    dims, rates, changes, box, truncation, stay, weights, free, itab, ftab, plain
):
    block_first, block_second, extents, kernel_layers = dims
    rows = block_second + 2 * HALO
    plane = 2 * rows
    layers = block_first + 2 * HALO
    anchor_first = lax.axis_index("gx") * block_first - HALO
    anchor_second = lax.axis_index("gy") * block_second - HALO
    step = pl.program_id(0)

    def order(r, d):
        return jnp.maximum(-changes[r, d], 0)

    @pl.when(step == 0)
    def _():
        corner = jnp.float32(0.0)
        for r in range(REACTIONS):
            term = rates[r]
            for d in range(3):
                e = float(extents[d])
                s = order(r, d)
                term = term * jnp.where(
                    s == 0,
                    1.0,
                    jnp.where(s == 1, (e - 1.0) / e, (e - 1.0) * (e - 2.0) / (e * e)),
                )
            corner = corner + term
        inverse = 1.0 / jnp.full((rows, LANES), headroom * corner, jnp.float32)
        row = lax.broadcasted_iota(jnp.int32, (rows, LANES), 0) + anchor_second
        lane = lax.broadcasted_iota(jnp.int32, (rows, LANES), 1)
        real_row = (row >= 0) & (row < extents[1])
        box_row = (row >= box[0, 1]) & (row < box[1, 1])
        for h in range(2):
            third = 2 * lane + h
            box_here = box_row & (third >= box[0, 2]) & (third < box[1, 2])
            for v in range(3):
                at = pl.ds((v * 2 + h) * rows, rows)
                if v == 2:
                    free[at, :] = jnp.zeros((rows, LANES), jnp.float32)
                elif v == 1:
                    free[at, :] = jnp.where(real_row & ~box_here, 1.0, 0.0)
                else:
                    free[at, :] = jnp.where(real_row, 1.0, 0.0)

            def coefficient(r, carry):
                scale = inverse * rates[r]
                at = pl.ds(pl.multiple_of((r * 2 + h) * rows, 8), rows)
                s1 = order(r, 1)
                s2 = order(r, 2)
                plain[at, :] = (
                    scale
                    * counts_factor(row.astype(jnp.float32), s1, float(extents[1]))
                    * counts_factor(third.astype(jnp.float32), s2, float(extents[2]))
                )
                from_row = row - changes[r, 1]
                from_third = third - changes[r, 2]
                inside = (from_third >= 0) & (from_third < extents[2])
                moved = (
                    scale
                    * counts_factor(from_row.astype(jnp.float32), s1, float(extents[1]))
                    * counts_factor(from_third.astype(jnp.float32), s2, float(extents[2]))
                )
                weights[at, :] = jnp.where(inside, moved, 0.0)
                return carry

            lax.fori_loop(0, REACTIONS, coefficient, 0)
        for which in range(2):
            for r in range(REACTIONS):
                for h in range(2):
                    source = h - changes[r, 2]
                    parity = source & 1
                    turn = source >> 1
                    itab[which * 12 + r * 2 + h] = (
                        PAD
                        + ((turn + 1) * kernel_layers[which] - changes[r, 0]) * plane
                        + parity * rows
                        - changes[r, 1]
                    )

        def layer_scalars(i, carry):
            n0 = anchor_first + i
            real = (n0 >= 0) & (n0 < extents[0])
            in_box = (n0 >= box[0, 0]) & (n0 < box[1, 0])
            itab[24 + i] = jnp.where(real, jnp.where(in_box, 1, 0), 2)
            for r in range(REACTIONS):
                source = (n0 - changes[r, 0]).astype(jnp.float32)
                ftab[i * REACTIONS + r] = counts_factor(source, order(r, 0), float(extents[0]))
            return carry

        lax.fori_loop(0, layers, layer_scalars, 0)
        table = [
            math.exp(-mean_jumps) * mean_jumps**j / math.factorial(j) for j in range(series_length)
        ]
        tails = []
        for which in range(2):
            tail = jnp.float32(0.0)
            for j in range(STEPS + 1, series_length):
                tail = tail + jnp.where(j <= truncation[which], jnp.float32(table[j]), 0.0)
            tails.append(tail)
        base = layers * REACTIONS
        for j in range(STEPS):
            ftab[base + j] = jnp.float32(table[j])
        ftab[base + STEPS] = jnp.float32(table[STEPS]) + tails[0]
        ftab[base + STEPS + 1] = jnp.float32(table[STEPS]) + tails[1]

    chunk = stay.shape[0]

    def group(g, carry):
        row0 = pl.multiple_of(g * ROWS, ROWS)
        terms = [
            [plain[pl.ds((r * 2 + h) * rows + row0, ROWS), :] for h in range(2)]
            for r in range(REACTIONS)
        ]
        for i in range(chunk):
            n0 = anchor_first + step * chunk + i
            kind = itab[24 + step * chunk + i]
            firsts = [
                counts_factor(n0.astype(jnp.float32), order(r, 0), float(extents[0]))
                for r in range(REACTIONS)
            ]
            for h in range(2):
                total = terms[0][h] * firsts[0]
                for r in range(1, REACTIONS):
                    total = total + terms[r][h] * firsts[r]
                mask = free[pl.ds(pl.multiple_of(kind * plane + h * rows + row0, 8), ROWS), :]
                stay[i, h, pl.ds(row0, ROWS), :] = 1.0 - mask * total
        return carry

    lax.fori_loop(0, rows // ROWS, group, 0)


def split_product(values, matrix):
    high = values.astype(jnp.bfloat16)
    low = (values - high.astype(jnp.float32)).astype(jnp.bfloat16)
    return jnp.dot(high, matrix, preferred_element_type=jnp.float32) + jnp.dot(
        low, matrix, preferred_element_type=jnp.float32
    )


def parity_matrix(transposed):
    size = 2 * LANES
    third = lax.broadcasted_iota(jnp.int32, (size, size), 1 if transposed else 0)
    place = lax.broadcasted_iota(jnp.int32, (size, size), 0 if transposed else 1)
    return jnp.where(place == (third & 1) * LANES + (third >> 1), 1.0, 0.0).astype(jnp.bfloat16)


class Lattice:
    def __init__(self, layers, rows, which, itab, ftab, total_layers, weights, free, stay, p, acc, q):
        self.layers, self.rows, self.plane = layers, rows, 2 * rows
        self.which, self.itab, self.ftab = which, itab, ftab
        self.weights, self.free, self.stay = weights, free, stay
        self.p, self.acc, self.q = p, acc, q
        self.weight_base = total_layers * REACTIONS
        self.never = jnp.full((ROWS, LANES), itab[24], jnp.int32) < 0

    def moved(self, turn, row):
        return PAD + (turn + 1) * self.layers * self.plane + row

    def ingest(self, values, local, table_layer, row0, count):
        w0 = self.ftab[self.weight_base]
        kind = self.itab[24 + table_layer]
        for h in range(2):
            part = values[:, h * LANES : (h + 1) * LANES]
            at = pl.multiple_of(local * self.plane + h * self.rows + row0, 8)
            self.p[pl.ds(at, count), :] = part
            self.acc[pl.ds(at, count), :] = part * w0
            mask = self.free[
                pl.ds(pl.multiple_of(kind * self.plane + h * self.rows + row0, 8), count), :
            ]
            masked = part * mask
            self.q[0][pl.ds(pl.multiple_of(self.moved(0, at), 8), count), :] = masked
            self.q[0][pl.ds(pl.multiple_of(self.moved(-1, at), 8), count), :] = pltpu.roll(
                masked, 1, 1
            )
            self.q[0][pl.ds(pl.multiple_of(self.moved(1, at), 8), count), :] = pltpu.roll(
                masked, LANES - 1, 1
            )

    def arrivals(self, source, local0, u, row0, h, start, coefficients, firsts):
        total = start
        shift = local0 * self.plane + row0
        for r in range(REACTIONS):
            at = self.itab[self.which * 12 + r * 2 + h] + shift + u * self.plane
            total = total + source[pl.ds(at, ROWS), :] * coefficients[r][h] * firsts[r]
        return total

    def coefficients(self, row0):
        return [
            [
                self.weights[pl.ds(pl.multiple_of((r * 2 + h) * self.rows + row0, 8), ROWS), :]
                for h in range(2)
            ]
            for r in range(REACTIONS)
        ]

    def advance(self, k, unroll, blocks, block_start):
        source, target = self.q[(k - 1) % 2], self.q[k % 2]
        weight = self.ftab[self.weight_base + k]
        plane, rows = self.plane, self.rows

        def roll_block(before, u, h):
            at = pl.multiple_of(before + u * plane + h * rows, 8)
            values = target[pl.ds(pl.multiple_of(self.moved(0, at), 8), ROWS), :]
            return (pltpu.roll(values, 1, 1), pltpu.roll(values, LANES - 1, 1))

        def store_block(before, u, h, pair):
            at = pl.multiple_of(before + u * plane + h * rows, 8)
            target[pl.ds(pl.multiple_of(self.moved(-1, at), 8), ROWS), :] = pair[0]
            target[pl.ds(pl.multiple_of(self.moved(1, at), 8), ROWS), :] = pair[1]

        def group(g, before):
            row0 = pl.multiple_of(g * ROWS, ROWS)
            coefficients = self.coefficients(row0)

            def block(b, before):
                local0, table0 = block_start(b)
                rolled = [[roll_block(before, u, h) for h in range(2)] for u in range(unroll)]
                results = []
                for u in range(unroll):
                    kind = self.itab[24 + table0 + u]
                    firsts = [self.ftab[(table0 + u) * REACTIONS + r] for r in range(REACTIONS)]
                    for h in range(2):
                        at = pl.multiple_of((local0 + u) * plane + h * rows + row0, 8)
                        value = self.p[pl.ds(at, ROWS), :]
                        if u > 0:
                            value = jnp.where(self.never, rolled[u - 1][h][0], value)
                        value = value * self.stay[pl.ds(at, ROWS), :]
                        value = self.arrivals(
                            source, local0, u, row0, h, value, coefficients, firsts
                        )
                        mask = self.free[
                            pl.ds(pl.multiple_of(kind * plane + h * rows + row0, 8), ROWS), :
                        ]
                        total = self.acc[pl.ds(at, ROWS), :] + value * weight
                        results.append((at, value, value * mask, total))
                for at, value, masked, total in results:
                    self.p[pl.ds(at, ROWS), :] = value
                    self.acc[pl.ds(at, ROWS), :] = total
                    target[pl.ds(pl.multiple_of(self.moved(0, at), 8), ROWS), :] = masked
                for u in range(unroll):
                    for h in range(2):
                        store_block(before, u, h, rolled[u][h])
                return pl.multiple_of(local0 * plane + row0, 8)

            return lax.fori_loop(0, blocks, block, before)

        first = pl.multiple_of(block_start(0)[0] * plane, 8)
        last = lax.fori_loop(0, rows // ROWS, group, first)
        pairs = [[roll_block(last, u, h) for h in range(2)] for u in range(unroll)]
        for u in range(unroll):
            for h in range(2):
                store_block(last, u, h, pairs[u][h])

    def finish(self, unroll, blocks, block_start):
        source = self.q[(STEPS - 1) % 2]
        weight_density = self.ftab[self.weight_base + STEPS]
        weight_totals = self.ftab[self.weight_base + STEPS + 1]
        plane, rows = self.plane, self.rows

        def group(g, sums):
            row0 = pl.multiple_of(g * ROWS + HALO, 8)
            coefficients = self.coefficients(row0)

            def block(b, sums):
                mass, hit = sums
                local0, table0 = block_start(b)
                results = []
                for u in range(unroll):
                    kind = self.itab[24 + table0 + u]
                    firsts = [self.ftab[(table0 + u) * REACTIONS + r] for r in range(REACTIONS)]
                    for h in range(2):
                        at = pl.multiple_of((local0 + u) * plane + h * rows + row0, 8)
                        value = self.p[pl.ds(at, ROWS), :] * self.stay[pl.ds(at, ROWS), :]
                        value = self.arrivals(
                            source, local0, u, row0, h, value, coefficients, firsts
                        )
                        mask = self.free[
                            pl.ds(pl.multiple_of(kind * plane + h * rows + row0, 8), ROWS), :
                        ]
                        so_far = self.acc[pl.ds(at, ROWS), :]
                        totals = so_far + value * weight_totals
                        mass = mass + totals
                        hit = hit + totals * (1.0 - mask)
                        results.append((at, so_far + value * weight_density))
                for at, total in results:
                    self.acc[pl.ds(at, ROWS), :] = total
                return mass, hit

            return lax.fori_loop(0, blocks, block, sums)

        zero = jnp.zeros((ROWS, LANES), jnp.float32)
        return lax.fori_loop(0, (rows - 2 * HALO) // ROWS, group, (zero, zero))

    def restore(self, local, out, index, matrix):
        own = self.rows - 2 * HALO
        even = self.acc[pl.ds(pl.multiple_of(local * self.plane + HALO, 8), own), :]
        odd = self.acc[pl.ds(pl.multiple_of(local * self.plane + self.rows + HALO, 8), own), :]
        out[index] = split_product(jnp.concatenate([even, odd], axis=1), matrix)


def copy_all(copies):
    for copy in copies:
        copy.start()
    return copies


def wait_all(copies):
    for copy in copies:
        copy.wait()


def interior_kernel(
    dims,
    density, below, above, stay_all, weights, free, itab, ftab,
    occupancy, q_edges, p_edges, acc_edges, sums,
    p, acc, q0, q1, stay, block, staged, sem_in, sem_stay, sem_edges, sem_out,
):
    block_first, block_second, _, _ = dims
    rows = block_second + 2 * HALO
    plane = 2 * rows
    chunk = 8
    chunks = block_first // chunk
    lattice = Lattice(
        block_first, rows, 0, itab, ftab, block_first + 2 * HALO, weights, free, stay, p, acc, (q0, q1)
    )
    loads = copy_all(
        [
            pltpu.make_async_copy(
                density.at[pl.ds(c * chunk, chunk)], block.at[pl.ds(c * chunk, chunk)], sem_in.at[c]
            )
            for c in range(chunks)
        ]
    )
    stay_copy = pltpu.make_async_copy(
        stay_all.at[pl.ds(HALO * plane, block_first * plane)], stay, sem_stay
    )
    stay_copy.start()
    spread = parity_matrix(False)
    for c in range(chunks):
        loads[c].wait()

        def layer(i, carry):
            local = c * chunk + i
            for part, row0, count in (
                (below[local], 0, HALO),
                (block[local], HALO, block_second),
                (above[local], HALO + block_second, HALO),
            ):
                lattice.ingest(split_product(part, spread), local, local + HALO, row0, count)
            return carry

        lax.fori_loop(0, chunk, layer, 0)
    stay_copy.wait()

    edges = []

    def export(k):
        q = (q0, q1)[k % 2]
        for side in range(2):
            layer = 2 * k if side == 0 else block_first - 2 * k - 4
            for turn in (-1, 0, 1):
                edges.append(
                    pltpu.make_async_copy(
                        q.at[pl.ds(lattice.moved(turn, layer * plane), 4 * plane)],
                        q_edges.at[k, side, turn + 1],
                        sem_edges.at[(k * 2 + side) * 4 + turn + 1],
                    )
                )
                edges[-1].start()
            layer = 2 * k if side == 0 else block_first - 2 * k - 2
            edges.append(
                pltpu.make_async_copy(
                    p.at[pl.ds(layer * plane, 2 * plane)],
                    p_edges.at[k, side],
                    sem_edges.at[(k * 2 + side) * 4 + 3],
                )
            )
            edges[-1].start()

    export(0)
    for k in range(1, STEPS):
        low, high = 2 * k, block_first - 2 * k
        unroll = largest_divisor(high - low, 10)

        def block_start(b, low=low, unroll=unroll):
            return low + b * unroll, low + b * unroll + HALO

        lattice.advance(k, unroll, (high - low) // unroll, block_start)
        export(k)
    for side in range(2):
        layer = 0 if side == 0 else block_first - HALO
        edges.append(
            pltpu.make_async_copy(
                acc.at[pl.ds(layer * plane, HALO * plane)], acc_edges.at[side], sem_edges.at[32 + side]
            )
        )
        edges[-1].start()
    inner = block_first - 2 * HALO
    unroll = largest_divisor(inner, 8)
    mass, hit = lattice.finish(
        unroll, inner // unroll, lambda b: (HALO + b * unroll, 2 * HALO + b * unroll)
    )
    sums[pl.ds(0, ROWS), :] = mass
    sums[pl.ds(ROWS, ROWS), :] = hit
    gather = parity_matrix(True)

    def layer(i, carry):
        lattice.restore(HALO + i, staged, i, gather)
        return carry

    lax.fori_loop(0, inner, layer, 0)
    out = pltpu.make_async_copy(staged, occupancy.at[pl.ds(HALO, inner)], sem_out)
    out.start()
    out.wait()
    wait_all(edges)


def edges_kernel(
    dims, devices,
    halo_low, halo_high, corner_low, corner_high, stay_all, q_edges, p_edges, acc_edges, sums_in,
    weights, free, itab, ftab, occupancy_in,
    occupancy, row_out,
    p, acc, q0, q1, stay, staged, sem_q, sem_p, sem_other, sem_out,
):
    block_first, block_second, _, _ = dims
    rows = block_second + 2 * HALO
    plane = 2 * rows
    side_layers = 2 * HALO + 2
    right_table = block_first - 2
    lattice = Lattice(
        2 * side_layers, rows, 1, itab, ftab, block_first + 2 * HALO, weights, free, stay, p, acc,
        (q0, q1),
    )
    copies = []
    for side in range(2):
        table = 0 if side == 0 else right_table
        copies.append(
            pltpu.make_async_copy(
                stay_all.at[pl.ds(table * plane, side_layers * plane)],
                stay.at[pl.ds(side * side_layers * plane, side_layers * plane)],
                sem_other.at[side],
            )
        )
        layer = HALO if side == 0 else side_layers + 2
        copies.append(
            pltpu.make_async_copy(
                acc_edges.at[side], acc.at[pl.ds(layer * plane, HALO * plane)], sem_other.at[2 + side]
            )
        )
        for k in range(STEPS):
            layer = 2 * k + HALO if side == 0 else side_layers + 6 - 2 * k
            for turn in (-1, 0, 1):
                copies.append(
                    pltpu.make_async_copy(
                        q_edges.at[k, side, turn + 1],
                        (q0, q1)[k % 2].at[pl.ds(lattice.moved(turn, layer * plane), 4 * plane)],
                        sem_q.at[(k * 2 + side) * 3 + turn + 1],
                    )
                )
            layer = 2 * k + HALO if side == 0 else side_layers + 8 - 2 * k
            copies.append(
                pltpu.make_async_copy(
                    p_edges.at[k, side], p.at[pl.ds(layer * plane, 2 * plane)], sem_p.at[k * 2 + side]
                )
            )
    copy_all(copies)
    spread = parity_matrix(False)
    for side, main, corner in ((0, halo_low, corner_low), (1, halo_high, corner_high)):

        def layer(i, carry, side=side, main=main, corner=corner):
            local = i if side == 0 else side_layers + 10 + i
            table = i if side == 0 else block_first + HALO + i
            for part, row0, count in (
                (corner[i, pl.ds(0, HALO)], 0, HALO),
                (main[i], HALO, block_second),
                (corner[i, pl.ds(HALO, HALO)], HALO + block_second, HALO),
            ):
                lattice.ingest(split_product(part, spread), local, table, row0, count)
            return carry

        lax.fori_loop(0, HALO, layer, 0)
    wait_all(copies)

    def starts(k):
        def block_start(b):
            return (
                2 * k + b * (side_layers + 10 - 4 * k),
                2 * k + b * (block_first + HALO - 4 * k),
            )

        return block_start

    for k in range(1, STEPS):
        lattice.advance(k, HALO, 2, starts(k))
    mass, hit = lattice.finish(HALO, 2, starts(STEPS))
    gather = parity_matrix(True)
    outs = []
    for side in range(2):

        def layer(i, carry, side=side):
            local = HALO + i if side == 0 else side_layers + 2 + i
            lattice.restore(local, staged, side * HALO + i, gather)
            return carry

        lax.fori_loop(0, HALO, layer, 0)
        outs.append(
            pltpu.make_async_copy(
                staged.at[pl.ds(side * HALO, HALO)],
                occupancy.at[pl.ds(0 if side == 0 else block_first - HALO, HALO)],
                sem_out.at[side],
            )
        )
        outs[-1].start()
    mass = jnp.sum(mass + sums_in[pl.ds(0, ROWS), :])
    hit = jnp.sum(hit + sums_in[pl.ds(ROWS, ROWS), :])
    lane = lax.broadcasted_iota(jnp.int32, (devices, LANES), 1)
    row_out[...] = jnp.where(lane == 0, hit, jnp.where(lane == 1, mass, 0.0))
    wait_all(outs)


def body(density, reaction_rates, state_changes, target_box, truncation):
    block_first, block_second, species_third = density.shape
    extents = (
        block_first * lax.axis_size("gx"),
        block_second * lax.axis_size("gy"),
        species_third,
    )
    count_first, count_second = lax.axis_size("gx"), lax.axis_size("gy")
    devices = count_first * count_second
    rows = block_second + 2 * HALO
    plane = 2 * rows
    layers = block_first + 2 * HALO
    side_layers = 2 * HALO + 2
    dims = (block_first, block_second, extents, (block_first, 2 * side_layers))

    def to_next(x, axis, count):
        return lax.ppermute(x, axis, [(i, i + 1) for i in range(count - 1)])

    def to_previous(x, axis, count):
        return lax.ppermute(x, axis, [(i + 1, i) for i in range(count - 1)])

    below = to_next(density[:, -HALO:], "gy", count_second)
    above = to_previous(density[:, :HALO], "gy", count_second)
    halo_low = to_next(density[-HALO:], "gx", count_first)
    halo_high = to_previous(density[:HALO], "gx", count_first)
    corner_low = to_next(
        jnp.concatenate([below[-HALO:], above[-HALO:]], axis=1), "gx", count_first
    )
    corner_high = to_previous(
        jnp.concatenate([below[:HALO], above[:HALO]], axis=1), "gx", count_first
    )

    f32 = jnp.float32
    smem = pl.BlockSpec(memory_space=pltpu.SMEM)
    vmem = pl.BlockSpec(memory_space=pltpu.VMEM)
    hbm = pl.BlockSpec(memory_space=pl.ANY)
    params = pltpu.CompilerParams(vmem_limit_bytes=VMEM_LIMIT)
    chunk = largest_divisor(layers, 8)

    stay, weights, free, itab, ftab = pl.pallas_call(
        functools.partial(tables_kernel, dims),
        grid=(layers // chunk,),
        out_shape=(
            jax.ShapeDtypeStruct((layers, 2, rows, LANES), f32),
            jax.ShapeDtypeStruct((12 * rows, LANES), f32),
            jax.ShapeDtypeStruct((6 * rows, LANES), f32),
            jax.ShapeDtypeStruct((24 + layers,), jnp.int32),
            jax.ShapeDtypeStruct((layers * REACTIONS + 8,), f32),
        ),
        in_specs=[smem] * 4,
        out_specs=(
            pl.BlockSpec((chunk, 2, rows, LANES), lambda i: (i, 0, 0, 0)),
            pl.BlockSpec((12 * rows, LANES), lambda i: (0, 0)),
            pl.BlockSpec((6 * rows, LANES), lambda i: (0, 0)),
            smem,
            smem,
        ),
        scratch_shapes=[pltpu.VMEM((12 * rows, LANES), f32)],
        compiler_params=params,
        name="tables",
    )(reaction_rates, state_changes, target_box, truncation)
    stay = stay.reshape(layers * plane, LANES)

    def scratch(local_layers):
        return [
            pltpu.VMEM((local_layers * plane, LANES), f32),
            pltpu.VMEM((local_layers * plane, LANES), f32),
            pltpu.VMEM((3 * local_layers * plane + 2 * PAD, LANES), f32),
            pltpu.VMEM((3 * local_layers * plane + 2 * PAD, LANES), f32),
            pltpu.VMEM((local_layers * plane, LANES), f32),
        ]

    chunks = block_first // 8
    occupancy, q_edges, p_edges, acc_edges, sums = pl.pallas_call(
        functools.partial(interior_kernel, dims),
        out_shape=(
            jax.ShapeDtypeStruct(density.shape, f32),
            jax.ShapeDtypeStruct((STEPS, 2, 3, 4 * plane, LANES), f32),
            jax.ShapeDtypeStruct((STEPS, 2, 2 * plane, LANES), f32),
            jax.ShapeDtypeStruct((2, HALO * plane, LANES), f32),
            jax.ShapeDtypeStruct((2 * ROWS, LANES), f32),
        ),
        in_specs=[hbm, vmem, vmem, hbm, vmem, vmem, smem, smem],
        out_specs=(hbm, hbm, hbm, hbm, vmem),
        scratch_shapes=scratch(block_first)
        + [
            pltpu.VMEM((block_first, block_second, species_third), f32),
            pltpu.VMEM((block_first - 2 * HALO, block_second, species_third), f32),
            pltpu.SemaphoreType.DMA((chunks,)),
            pltpu.SemaphoreType.DMA,
            pltpu.SemaphoreType.DMA((34,)),
            pltpu.SemaphoreType.DMA,
        ],
        compiler_params=params,
        cost_estimate=pl.CostEstimate(flops=400_000_000, bytes_accessed=40_000_000, transcendentals=0),
        name="interior",
    )(density, below, above, stay, weights, free, itab, ftab)

    occupancy, row = pl.pallas_call(
        functools.partial(edges_kernel, dims, devices),
        out_shape=(
            jax.ShapeDtypeStruct(density.shape, f32),
            jax.ShapeDtypeStruct((devices, LANES), f32),
        ),
        in_specs=[vmem] * 4 + [hbm] * 4 + [vmem] * 3 + [smem] * 2 + [hbm],
        out_specs=(hbm, vmem),
        scratch_shapes=scratch(2 * side_layers)
        + [
            pltpu.VMEM((2 * HALO, block_second, species_third), f32),
            pltpu.SemaphoreType.DMA((24,)),
            pltpu.SemaphoreType.DMA((8,)),
            pltpu.SemaphoreType.DMA((4,)),
            pltpu.SemaphoreType.DMA((2,)),
        ],
        input_output_aliases={13: 0},
        compiler_params=params,
        name="edges",
    )(
        halo_low, halo_high, corner_low, corner_high, stay, q_edges, p_edges, acc_edges, sums,
        weights, free, itab, ftab, occupancy,
    )
    rows_in = lax.all_to_all(row, ("gx", "gy"), 0, 0, tiled=True)
    summary = jnp.sum(rows_in[:, :2], axis=0) * (1.0 / math.prod(extents))
    return occupancy, summary


def solution(mesh):
    placed = (P("gx", "gy", None), P(), P(), P(), P())
    return jax.shard_map(
        body, mesh=mesh, in_specs=placed, out_specs=(P("gx", "gy", None), P()), check_vma=False
    )
```

time: 456 us -> 123 us (0.27)
  other arithmetic: 230 us -> 1.22 us
  between operations: 103 us -> 0.82 us
  Pallas kernels: 0 us -> 76.9 us
  starting transfers between devices: 42.4 us -> 14.1 us
  blocking collectives: 40.8 us -> 14.9 us
  waiting for transfers between devices: 23.3 us -> 8.94 us
  local copies, waits for them, and re-layouts: 13 us -> 5.81 us
    add x4 -> x0, other arithmetic: 121 us -> none  [the longest x3 111 us: advance(): advanced = advanced + arrival]
    pallas_call x0 -> x3, Pallas kernels: none -> 76.9 us  [the longest x1 37.6 us: body(): pl.pallas_call(functools.partial(interior_kernel, dims), out_shape=(jax.S...]
    reduce_sum x1, other arithmetic: 42.4 us -> 0.02 us  [body(): summary = jnp.sum(rows_in[:, :2], axis=0) * (1.0 / math.prod(extents))]
    psum x1 -> x0, blocking collectives: 40.8 us -> none  [record(): local_sums = lax.psum((local_sums[0], local_sums[1]), ('gx', 'gy'))]
    div x4 -> x0, other arithmetic: 31 us -> none  [advance(): scaled = padded * free / uniform_rate]
    ppermute x16 -> x6, starting transfers between devices: 42.4 us -> 14.1 us  [the longest x3 10.2 us: to_next(): return lax.ppermute(x, axis, [(i, i + 1) for i in range(count - 1)])]
    mul x17 -> x1, other arithmetic: 25.1 us -> 0.52 us  [body(): summary = jnp.sum(rows_in[:, :2], axis=0) * (1.0 / math.prod(extents))]
    all_to_all x0 -> x1, blocking collectives: none -> 14.9 us  [body(): rows_in = lax.all_to_all(row, ('gx', 'gy'), 0, 0, tiled=True)]
  transfers between devices with their start and end apart: 16 -> 6, of which waited for: 7 -> 1; matrix products, arithmetic and copies ran while one was open for 9% -> 4% of each run, Pallas kernels for 0% -> 39%
where the time goes in v1:
time: 123 us
  Pallas kernels  76.9 us (63%)
  blocking collectives  14.9 us (12%)
  starting transfers between devices  14.1 us (11%)
  waiting for transfers between devices  8.94 us (7%)
  local copies, waits for them, and re-layouts  5.81 us (5%)
    pallas_call x1, Pallas kernels, body(): pl.pallas_call(functools.partial(interior_kernel, dims), out_shape=(jax.S...  37.6 us
    pallas_call x1, Pallas kernels, body(): pl.pallas_call(functools.partial(edges_kernel, dims, devices), out_shape=...  28.8 us
    all_to_all x1, blocking collectives, body(): rows_in = lax.all_to_all(row, ('gx', 'gy'), 0, 0, tiled=True)  14.9 us
    pallas_call x1, Pallas kernels, body(): pl.pallas_call(functools.partial(tables_kernel, dims), grid=(layers // ch...  10.5 us
    ppermute x3, starting transfers between devices, to_next(): return lax.ppermute(x, axis, [(i, i + 1) for i in range(count - 1)])  10.2 us
    ppermute x3, waiting for transfers between devices, to_previous(): return lax.ppermute(x, axis, [(i + 1, i) for i in range(count - 1)])  8.93 us
    ppermute x3, starting transfers between devices, to_previous(): return lax.ppermute(x, axis, [(i + 1, i) for i in range(count - 1)])  3.84 us
    slice x1, local copies, waits for them, and re-layouts, body(): halo_high = to_previous(density[:HALO], 'gx', count_first)  3.03 us
  transfers between devices with their start and end apart: 6, of which 1 were waited for; matrix products, arithmetic and copies ran while one was open for 4% of the time, Pallas kernels for 39%

profile of v1, /device:TPU:0, one launch (start us, length us, event | category | flops | bytes accessed | tf_op | source)
XLA Modules:
  0.0 122.6 jit_solution(15186022635559644351)
XLA Ops:
  0.6 0.0 copy-start.5
  0.6 1.1 fusion
  1.7 4.9 %collective-permute-start.2 = (f32[32,8,256]{2,1,0:T(8,128)S(1)}, f32[32,8,256]{2,1,0:T(8,128)S(1)}, u32[]{:S(2)}, u32[]{:S(2)}) collective-permute-start(f32[32,8,256]{2,1,0:T(8,128)S(1)} %get-tuple-element.26), channel_id=1, source_target_pairs={{0,1},{1,2},{2,3},{4,5},{5,6},{6,7},{8,9},{9,10},{10,11},{12,13},{... | collective-permute-start | bytes 786440 | tf_op jit(solution)/shard_map/ppermute | solution.py:572
  6.7 3.0 %fusion.1 = (f32[8,128,256]{2,1,0:T(8,128)}, f32[8,128,256]{2,1,0:T(8,128)}) fusion(f32[32,128,256]{2,1,0:T(8,128)} %density.1), kind=kLoop, calls=%fused_computation.5 | loop fusion | bytes 4194304 | tf_op jit(solution)/shard_map/slice | solution.py:580
  9.7 1.3 %collective-permute-start.1 = (f32[8,128,256]{2,1,0:T(8,128)}, f32[8,128,256]{2,1,0:T(8,128)S(1)}, u32[]{:S(2)}, u32[]{:S(2)}) collective-permute-start(f32[8,128,256]{2,1,0:T(8,128)} %get-tuple-element.28), channel_id=1, source_target_pairs={{4,0},{8,4},{12,8},{16,12},{20,16},{24,20},{28,24},{5,1},{9,5},{13... | collective-permute-start | bytes 3145736 | tf_op jit(solution)/shard_map/ppermute | solution.py:575
  11.0 4.0 %collective-permute-start = (f32[8,128,256]{2,1,0:T(8,128)}, f32[8,128,256]{2,1,0:T(8,128)}, u32[]{:S(2)}, u32[]{:S(2)}) collective-permute-start(f32[8,128,256]{2,1,0:T(8,128)} %get-tuple-element.29), channel_id=1, source_target_pairs={{0,4},{4,8},{8,12},{12,16},{16,20},{20,24},{24,28},{1,5},{5,9},{9,... | collective-permute-start | bytes 3145736 | tf_op jit(solution)/shard_map/ppermute | solution.py:572
  15.0 1.3 %collective-permute-start.3 = (f32[32,8,256]{2,1,0:T(8,128)S(1)}, f32[32,8,256]{2,1,0:T(8,128)S(1)}, u32[]{:S(2)}, u32[]{:S(2)}) collective-permute-start(f32[32,8,256]{2,1,0:T(8,128)S(1)} %get-tuple-element.27), channel_id=1, source_target_pairs={{1,0},{2,1},{3,2},{5,4},{6,5},{7,6},{9,8},{10,9},{11,10},{13,12},{... | collective-permute-start | bytes 786440 | tf_op jit(solution)/shard_map/ppermute | solution.py:575
  16.3 0.0 collective-permute-done.2.below
  16.3 0.0 copy-start.1
  16.3 8.9 %collective-permute-done.3.above = f32[32,8,256]{2,1,0:T(8,128)S(1)} collective-permute-done((f32[32,8,256]{2,1,0:T(8,128)S(1)}, f32[32,8,256]{2,1,0:T(8,128)S(1)}, u32[]{:S(2)}, u32[]{:S(2)}) %collective-permute-start.3) | collective-permute-done | bytes 262176 | tf_op jit(solution)/shard_map/ppermute | solution.py:575
  25.2 0.0 copy-start.2
  25.3 1.3 %collective-permute-start.4 = (f32[8,16,256]{2,1,0:T(8,128)S(1)}, f32[8,16,256]{2,1,0:T(8,128)S(1)}, u32[]{:S(2)}, u32[]{:S(2)}) collective-permute-start(f32[8,16,256]{2,1,0:T(8,128)S(1)} %pad_maximum_fusion), channel_id=1, source_target_pairs={{0,4},{4,8},{8,12},{12,16},{16,20},{20,24},{24,28},{1,5},{5,9},{9,... | collective-permute-start | bytes 393224 | tf_op jit(solution)/shard_map/ppermute | solution.py:572
  26.6 0.7 pad_maximum_fusion.1
  27.2 1.3 %collective-permute-start.5 = (f32[8,16,256]{2,1,0:T(8,128)}, f32[8,16,256]{2,1,0:T(8,128)S(1)}, u32[]{:S(2)}, u32[]{:S(2)}) collective-permute-start(f32[8,16,256]{2,1,0:T(8,128)} %pad_maximum_fusion.1), channel_id=1, source_target_pairs={{4,0},{8,4},{12,8},{16,12},{20,16},{24,20},{28,24},{5,1},{9,5},{13... | collective-permute-start | bytes 393224 | tf_op jit(solution)/shard_map/ppermute | solution.py:575
  28.5 0.0 copy-done.5
  28.5 0.7 copy.9.changes
  29.2 10.5 %tables.1 = (f32[48,2,144,128]{3,2,1,0:T(8,128)}, f32[1728,128]{1,0:T(8,128)}, f32[864,128]{1,0:T(8,128)}, s32[72]{0:T(128)}, f32[296]{0:T(512)}) custom-call(f32[6]{0:T(128)} %rates.1, s32[6,3]{1,0:T(8,128)} %copy.9.changes, s32[2,3]{1,0:T(2,128)} %box.1, s32[2]{0:T(128)} %truncation.1), custom_call_target="tpu_custom_call" | custom-call | tf_op jit(solution)/shard_map/tables/pallas_call | solution.py:595
  39.7 0.0 copy-done.1
  39.8 0.0 copy-done.2
  39.8 37.6 %interior.1 = (f32[32,128,256]{2,1,0:T(8,128)}, f32[4,2,3,1152,128]{4,3,2,1,0:T(8,128)}, f32[4,2,576,128]{3,2,1,0:T(8,128)}, f32[2,2304,128]{2,1,0:T(8,128)}, f32[32,128]{1,0:T(8,128)}) custom-call(f32[32,128,256]{2,1,0:T(8,128)} %density.1, f32[32,8,256]{2,1,0:T(8,128)} %copy-done.1, f32[32,8,256]{2,1,0:T(8,128)} %copy-done.2, f32[13824,128]{1,0:T(8,128)} %bitcast.5, ...), custom_call_target="tpu_custom_call" | custom-call | flops 400000000 | bytes 40000000 | tf_op jit(solution)/shard_map/interior/pallas_call | solution.py:629
  77.4 0.0 collective-permute-done.4.corner_low
  77.4 0.0 copy-start.3
  77.4 0.0 collective-permute-done.5.corner_high
  77.4 0.0 copy-start.4
  77.4 0.0 collective-permute-done.1.halo_high
  77.4 0.0 copy-start
  77.4 0.0 collective-permute-done.halo_low
  77.4 0.6 copy-done.3
  78.0 0.0 copy-done.4
  78.1 0.4 copy-done
  78.4 28.8 %edges.1 = (f32[32,128,256]{2,1,0:T(8,128)}, f32[32,128]{1,0:T(8,128)}) custom-call(f32[8,128,256]{2,1,0:T(8,128)} %collective-permute-done.halo_low, f32[8,128,256]{2,1,0:T(8,128)} %copy-done, f32[8,16,256]{2,1,0:T(8,128)} %copy-done.3, f32[8,16,256]{2,1,0:T(8,128)} %copy-done.4, f32[13824,128]{1,0:T(8,128)} %bitcast.6, ...), custom_call_target="tpu_custom_call", output_to_operand_aliasing={{0}: (13, {})} | custom-call | tf_op jit(solution)/shard_map/edges/pallas_call | solution.py:654
  107.2 14.9 %all_to_all.12 = f32[32,1,128]{2,1,0:T(1,128)S(1)} all-to-all(f32[32,1,128]{2,1,0:T(1,128)} %bitcast.8), channel_id=1, replica_groups=mesh['gx'=8,'gy'=4] {'gx','gy'}, dimensions={0} | all-to-all | bytes 32768 | tf_op jit(solution)/shard_map/all_to_all | solution.py:677
  122.1 0.5 broadcast_multiply_fusion
  (4 shorter events, 0.1 us)
Async XLA Ops:
  0.6 27.9 %copy-start.5 = (s32[6,3]{0,1:T(4,128)S(1)}, s32[6,3]{0,1:T(4,128)}, u32[]{:S(2)}) copy-start(s32[6,3]{0,1:T(4,128)} %param.7) | copy-start | bytes 220
  1.7 14.6 %collective-permute-start.2 = (f32[32,8,256]{2,1,0:T(8,128)S(1)}, f32[32,8,256]{2,1,0:T(8,128)S(1)}, u32[]{:S(2)}, u32[]{:S(2)}) collective-permute-start(f32[32,8,256]{2,1,0:T(8,128)S(1)} %get-tuple-element.26), channel_id=1, source_target_pairs={{0,1},{1,2},{2,3},{4,5},{5,6},{6,7},{8,9},{9,10},{10,11},{12,13},{... | collective-permute-start | bytes 786440 | tf_op jit(solution)/shard_map/ppermute | solution.py:572
  9.7 67.7 %collective-permute-start.1 = (f32[8,128,256]{2,1,0:T(8,128)}, f32[8,128,256]{2,1,0:T(8,128)S(1)}, u32[]{:S(2)}, u32[]{:S(2)}) collective-permute-start(f32[8,128,256]{2,1,0:T(8,128)} %get-tuple-element.28), channel_id=1, source_target_pairs={{4,0},{8,4},{12,8},{16,12},{20,16},{24,20},{28,24},{5,1},{9,5},{13... | collective-permute-start | bytes 3145736 | tf_op jit(solution)/shard_map/ppermute | solution.py:575
  11.0 66.4 %collective-permute-start = (f32[8,128,256]{2,1,0:T(8,128)}, f32[8,128,256]{2,1,0:T(8,128)}, u32[]{:S(2)}, u32[]{:S(2)}) collective-permute-start(f32[8,128,256]{2,1,0:T(8,128)} %get-tuple-element.29), channel_id=1, source_target_pairs={{0,4},{4,8},{8,12},{12,16},{16,20},{20,24},{24,28},{1,5},{5,9},{9,... | collective-permute-start | bytes 3145736 | tf_op jit(solution)/shard_map/ppermute | solution.py:572
  15.0 10.2 %collective-permute-start.3 = (f32[32,8,256]{2,1,0:T(8,128)S(1)}, f32[32,8,256]{2,1,0:T(8,128)S(1)}, u32[]{:S(2)}, u32[]{:S(2)}) collective-permute-start(f32[32,8,256]{2,1,0:T(8,128)S(1)} %get-tuple-element.27), channel_id=1, source_target_pairs={{1,0},{2,1},{3,2},{5,4},{6,5},{7,6},{9,8},{10,9},{11,10},{13,12},{... | collective-permute-start | bytes 786440 | tf_op jit(solution)/shard_map/ppermute | solution.py:575
  16.3 23.5 %copy-start.1 = (f32[32,8,256]{2,1,0:T(8,128)}, f32[32,8,256]{2,1,0:T(8,128)S(1)}, u32[]{:S(2)}) copy-start(f32[32,8,256]{2,1,0:T(8,128)S(1)} %collective-permute-done.2.below) | copy-start | bytes 786436
  25.2 14.5 %copy-start.2 = (f32[32,8,256]{2,1,0:T(8,128)}, f32[32,8,256]{2,1,0:T(8,128)S(1)}, u32[]{:S(2)}) copy-start(f32[32,8,256]{2,1,0:T(8,128)S(1)} %collective-permute-done.3.above) | copy-start | bytes 786436
  25.3 52.1 %collective-permute-start.4 = (f32[8,16,256]{2,1,0:T(8,128)S(1)}, f32[8,16,256]{2,1,0:T(8,128)S(1)}, u32[]{:S(2)}, u32[]{:S(2)}) collective-permute-start(f32[8,16,256]{2,1,0:T(8,128)S(1)} %pad_maximum_fusion), channel_id=1, source_target_pairs={{0,4},{4,8},{8,12},{12,16},{16,20},{20,24},{24,28},{1,5},{5,9},{9,... | collective-permute-start | bytes 393224 | tf_op jit(solution)/shard_map/ppermute | solution.py:572
  27.2 50.1 %collective-permute-start.5 = (f32[8,16,256]{2,1,0:T(8,128)}, f32[8,16,256]{2,1,0:T(8,128)S(1)}, u32[]{:S(2)}, u32[]{:S(2)}) collective-permute-start(f32[8,16,256]{2,1,0:T(8,128)} %pad_maximum_fusion.1), channel_id=1, source_target_pairs={{4,0},{8,4},{12,8},{16,12},{20,16},{24,20},{28,24},{5,1},{9,5},{13... | collective-permute-start | bytes 393224 | tf_op jit(solution)/shard_map/ppermute | solution.py:575
  77.4 0.6 copy-start.3
  77.4 0.7 copy-start.4
  77.4 1.0 copy-start

commit v2 on v1

v2 whole, which is shorter than its diff:
```python
import functools
import math

import jax
import jax.numpy as jnp
from jax import lax
from jax.experimental import pallas as pl
from jax.experimental.pallas import tpu as pltpu
from jax.sharding import PartitionSpec as P

STEPS = 4
REACTIONS = 6
HALO = 2 * STEPS
LANES = 128
ROWS = 16
PAD = 8
BODY_LAYERS = 14

mean_jumps = 8.0
headroom = 1.05
series_length = 40

VMEM_LIMIT = 62 << 20


KINDS = 24


def largest_divisor(number, limit):
    return max(u for u in range(1, limit + 1) if number % u == 0)


def counts_factor(values, order, extent):
    linear = values * (1.0 / extent)
    square = values * (values - 1.0) * (1.0 / (extent * extent))
    return jnp.where(order == 0, 1.0, jnp.where(order == 1, linear, square))


def tables_kernel(
    dims, rates, changes, box, truncation, stay, weights, free, itab, ftab, plain
):
    block_first, block_second, extents, kernel_layers = dims
    rows = block_second + 2 * HALO
    plane = 2 * rows
    layers = block_first + 2 * HALO
    anchor_first = lax.axis_index("gx") * block_first - HALO
    anchor_second = lax.axis_index("gy") * block_second - HALO
    step = pl.program_id(0)

    def order(r, d):
        return jnp.maximum(-changes[r, d], 0)

    @pl.when(step == 0)
    def _():
        corner = jnp.float32(0.0)
        for r in range(REACTIONS):
            term = rates[r]
            for d in range(3):
                e = float(extents[d])
                s = order(r, d)
                term = term * jnp.where(
                    s == 0,
                    1.0,
                    jnp.where(s == 1, (e - 1.0) / e, (e - 1.0) * (e - 2.0) / (e * e)),
                )
            corner = corner + term
        inverse = 1.0 / jnp.full((rows, LANES), headroom * corner, jnp.float32)
        row = lax.broadcasted_iota(jnp.int32, (rows, LANES), 0) + anchor_second
        lane = lax.broadcasted_iota(jnp.int32, (rows, LANES), 1)
        real_row = (row >= 0) & (row < extents[1])
        box_row = (row >= box[0, 1]) & (row < box[1, 1])
        for h in range(2):
            third = 2 * lane + h
            box_here = box_row & (third >= box[0, 2]) & (third < box[1, 2])
            for v in range(3):
                at = pl.ds((v * 2 + h) * rows, rows)
                if v == 2:
                    free[at, :] = jnp.zeros((rows, LANES), jnp.float32)
                elif v == 1:
                    free[at, :] = jnp.where(real_row & ~box_here, 1.0, 0.0)
                else:
                    free[at, :] = jnp.where(real_row, 1.0, 0.0)

            def coefficient(r, carry):
                scale = inverse * rates[r]
                at = pl.ds(pl.multiple_of((r * 2 + h) * rows, 8), rows)
                s1 = order(r, 1)
                s2 = order(r, 2)
                plain[at, :] = (
                    scale
                    * counts_factor(row.astype(jnp.float32), s1, float(extents[1]))
                    * counts_factor(third.astype(jnp.float32), s2, float(extents[2]))
                )
                from_row = row - changes[r, 1]
                from_third = third - changes[r, 2]
                inside = (from_third >= 0) & (from_third < extents[2])
                moved = (
                    scale
                    * counts_factor(from_row.astype(jnp.float32), s1, float(extents[1]))
                    * counts_factor(from_third.astype(jnp.float32), s2, float(extents[2]))
                )
                weights[at, :] = jnp.where(inside, moved, 0.0)
                return carry

            lax.fori_loop(0, REACTIONS, coefficient, 0)
        for which in range(2):
            for r in range(REACTIONS):
                for h in range(2):
                    source = h - changes[r, 2]
                    parity = source & 1
                    turn = source >> 1
                    itab[which * 12 + r * 2 + h] = (
                        PAD
                        + ((turn + 1) * kernel_layers[which] - changes[r, 0]) * plane
                        + parity * rows
                        - changes[r, 1]
                    )

        def layer_scalars(i, carry):
            n0 = anchor_first - 2 + i
            real = (n0 >= 0) & (n0 < extents[0])
            in_box = (n0 >= box[0, 0]) & (n0 < box[1, 0])
            itab[KINDS + i] = jnp.where(real, jnp.where(in_box, 1, 0), 2)
            for r in range(REACTIONS):
                source = (n0 - changes[r, 0]).astype(jnp.float32)
                ftab[i * REACTIONS + r] = counts_factor(source, order(r, 0), float(extents[0]))
            return carry

        lax.fori_loop(0, layers + 4, layer_scalars, 0)
        table = [
            math.exp(-mean_jumps) * mean_jumps**j / math.factorial(j) for j in range(series_length)
        ]
        tails = []
        for which in range(2):
            tail = jnp.float32(0.0)
            for j in range(STEPS + 1, series_length):
                tail = tail + jnp.where(j <= truncation[which], jnp.float32(table[j]), 0.0)
            tails.append(tail)
        base = (layers + 4) * REACTIONS
        for j in range(STEPS):
            ftab[base + j] = jnp.float32(table[j])
        ftab[base + STEPS] = jnp.float32(table[STEPS]) + tails[0]
        ftab[base + STEPS + 1] = jnp.float32(table[STEPS]) + tails[1]

    chunk = stay.shape[0]

    def group(g, carry):
        row0 = pl.multiple_of(g * ROWS, ROWS)
        terms = [
            [plain[pl.ds((r * 2 + h) * rows + row0, ROWS), :] for h in range(2)]
            for r in range(REACTIONS)
        ]
        for i in range(chunk):
            entry = step * chunk + i + 2
            kind = itab[KINDS + entry]
            firsts = [
                ftab[(entry + changes[r, 0]) * REACTIONS + r] for r in range(REACTIONS)
            ]
            for h in range(2):
                total = terms[0][h] * firsts[0]
                for r in range(1, REACTIONS):
                    total = total + terms[r][h] * firsts[r]
                mask = free[pl.ds(pl.multiple_of(kind * plane + h * rows + row0, 8), ROWS), :]
                stay[i, h, pl.ds(row0, ROWS), :] = 1.0 - mask * total
        return carry

    lax.fori_loop(0, rows // ROWS, group, 0)


def split_product(values, matrix):
    high = values.astype(jnp.bfloat16)
    low = (values - high.astype(jnp.float32)).astype(jnp.bfloat16)
    return jnp.dot(high, matrix, preferred_element_type=jnp.float32) + jnp.dot(
        low, matrix, preferred_element_type=jnp.float32
    )


def parity_matrix(transposed):
    size = 2 * LANES
    third = lax.broadcasted_iota(jnp.int32, (size, size), 1 if transposed else 0)
    place = lax.broadcasted_iota(jnp.int32, (size, size), 0 if transposed else 1)
    return jnp.where(place == (third & 1) * LANES + (third >> 1), 1.0, 0.0).astype(jnp.bfloat16)


class Segment:
    def __init__(self, count, own, table, source, target, totals):
        self.count, self.own, self.table = count, own, table
        self.source, self.target, self.totals = source, target, totals


class Lattice:
    def __init__(self, rows, which, itab, ftab, table_layers, weights, free, stay, p, acc, moved_layers):
        self.rows, self.plane = rows, 2 * rows
        self.which, self.itab, self.ftab = which, itab, ftab
        self.weights, self.free, self.stay = weights, free, stay
        self.p, self.acc, self.moved_layers = p, acc, moved_layers
        self.weight_base = (table_layers + 4) * REACTIONS
        self.never = jnp.full((ROWS, LANES), itab[KINDS], jnp.int32) < 0

    def moved(self, turn, row):
        return PAD + (turn + 1) * self.moved_layers * self.plane + row

    def kind(self, table):
        return self.itab[KINDS + 2 + table]

    def first(self, table, r):
        return self.ftab[(table + 2) * REACTIONS + r]

    def mask(self, kind, h, row0, count):
        at = pl.multiple_of(kind * self.plane + h * self.rows + row0, 8)
        return self.free[pl.ds(at, count), :]

    def ingest(self, q, values, local, table, target, totals):
        kind = self.kind(table)
        rows = self.rows
        for h in range(2):
            part = values[:, h * LANES : (h + 1) * LANES]
            at = pl.multiple_of(local * self.plane + h * rows, 8)
            self.p[pl.ds(at, rows), :] = part
            if totals is not None:
                at = pl.multiple_of(totals * self.plane + h * rows, 8)
                self.acc[pl.ds(at, rows), :] = part * self.ftab[self.weight_base]
            masked = part * self.mask(kind, h, 0, rows)
            at = target * self.plane + h * rows
            for turn in (0, -1, 1):
                lanes = masked if turn == 0 else pltpu.roll(masked, 1 if turn < 0 else LANES - 1, 1)
                q[pl.ds(pl.multiple_of(self.moved(turn, at), 8), rows), :] = lanes

    def coefficients(self, row0):
        return [
            [
                self.weights[pl.ds(pl.multiple_of((r * 2 + h) * self.rows + row0, 8), ROWS), :]
                for h in range(2)
            ]
            for r in range(REACTIONS)
        ]

    def places(self, segments, row0):
        found = []
        for segment in segments:
            own = segment.own * self.plane + row0
            target = segment.target * self.plane + row0
            totals = None if segment.totals is None else segment.totals * self.plane + row0
            shift = segment.source * self.plane + row0
            sources = [
                [self.itab[self.which * 12 + r * 2 + h] + shift for h in range(2)]
                for r in range(REACTIONS)
            ]
            for u in range(segment.count):
                found.append((segment, u, own, target, totals, sources))
        return found

    def value(self, source, place, h, coefficients, firsts, rolled=None):
        segment, u, own, _, _, sources = place
        at = pl.multiple_of(own + u * self.plane + h * self.rows, 8)
        value = self.p[pl.ds(at, ROWS), :]
        if rolled is not None:
            value = jnp.where(self.never, rolled, value)
        value = value * self.stay[pl.ds(at, ROWS), :]
        for r in range(REACTIONS):
            arriving = source[pl.ds(sources[r][h] + u * self.plane, ROWS), :]
            value = value + arriving * coefficients[r][h] * firsts[r]
        return at, value

    def advance(self, k, source, target, blocks, layout, has_totals=None):
        weight = self.ftab[self.weight_base + k]
        plane, rows = self.plane, self.rows
        counts = [segment.count for segment in layout(0)]
        size = sum(counts)
        offsets = [(s, u) for s, count in enumerate(counts) for u in range(count)]
        lag = min(5, size // 3)

        def center_row(before, index, h):
            s, u = offsets[index]
            return before[s] + u * plane + h * rows

        def roll_layer(before, index):
            pairs = []
            for h in range(2):
                at = self.moved(0, center_row(before, index, h))
                values = target[pl.ds(pl.multiple_of(at, 8), ROWS), :]
                pairs.append((pltpu.roll(values, 1, 1), pltpu.roll(values, LANES - 1, 1)))
            return pairs

        def store_layer(before, index, pairs):
            for h in range(2):
                row = center_row(before, index, h)
                for side, turn in enumerate((-1, 1)):
                    at = pl.multiple_of(self.moved(turn, row), 8)
                    target[pl.ds(at, ROWS), :] = pairs[h][side]

        def group(g, before):
            row0 = pl.multiple_of(g * ROWS, ROWS)
            coefficients = self.coefficients(row0)

            def block(b, before):
                places = self.places(layout(b), row0)
                rolled = [roll_layer(before, index) for index in range(size)]
                stored = 0
                for index, place in enumerate(places):
                    segment, u, own, target0, totals0, _ = place
                    table = segment.table + u
                    kind = self.kind(table)
                    firsts = [self.first(table, r) for r in range(REACTIONS)]
                    ready = -1
                    if index >= lag:
                        ready = ((index - lag + 1) * size + size - lag - 1) // (size - lag) - 1
                    for h in range(2):
                        at, value = self.value(
                            source, place, h, coefficients, firsts,
                            rolled[ready][1][h] if ready >= 0 else None,
                        )
                        self.p[pl.ds(at, ROWS), :] = value
                        masked = value * self.mask(kind, h, row0, ROWS)
                        row = target0 + u * plane + h * rows
                        target[pl.ds(pl.multiple_of(self.moved(0, row), 8), ROWS), :] = masked
                        if has_totals is None or has_totals[index]:
                            row = pl.multiple_of(totals0 + u * plane + h * rows, 8)
                            self.acc[pl.ds(row, ROWS), :] = (
                                self.acc[pl.ds(row, ROWS), :] + value * weight
                            )
                    while stored <= ready:
                        store_layer(before, stored, rolled[stored])
                        stored += 1
                while stored < size:
                    store_layer(before, stored, rolled[stored])
                    stored += 1
                return tuple(
                    pl.multiple_of(jnp.int32(segment.target * plane) + row0, 8)
                    for segment in layout(b)
                )

            return lax.fori_loop(0, blocks, block, before)

        before = tuple(jnp.int32(segment.target * plane) for segment in layout(jnp.int32(0)))
        last = lax.fori_loop(0, rows // ROWS, group, before)
        for index in range(size):
            store_layer(last, index, roll_layer(last, index))

    def finish(self, source, blocks, layout):
        weight_density = self.ftab[self.weight_base + STEPS]
        weight_totals = self.ftab[self.weight_base + STEPS + 1]

        def group(g, sums):
            row0 = pl.multiple_of(g * ROWS + HALO, 8)
            coefficients = self.coefficients(row0)

            def block(b, sums):
                mass, hit = sums
                for place in self.places(layout(b), row0):
                    segment, u, _, _, totals0, _ = place
                    table = segment.table + u
                    kind = self.kind(table)
                    firsts = [self.first(table, r) for r in range(REACTIONS)]
                    for h in range(2):
                        _, value = self.value(source, place, h, coefficients, firsts)
                        row = pl.multiple_of(totals0 + u * self.plane + h * self.rows, 8)
                        so_far = self.acc[pl.ds(row, ROWS), :]
                        totals = so_far + value * weight_totals
                        mass = mass + totals
                        hit = hit + totals * (1.0 - self.mask(kind, h, row0, ROWS))
                        self.acc[pl.ds(row, ROWS), :] = so_far + value * weight_density
                return mass, hit

            return lax.fori_loop(0, blocks, block, sums)

        zero = jnp.zeros((ROWS, LANES), jnp.float32)
        return lax.fori_loop(0, (self.rows - 2 * HALO) // ROWS, group, (zero, zero))

    def restore(self, local, out, index, matrix):
        own = self.rows - 2 * HALO
        even = self.acc[pl.ds(pl.multiple_of(local * self.plane + HALO, 8), own), :]
        odd = self.acc[pl.ds(pl.multiple_of(local * self.plane + self.rows + HALO, 8), own), :]
        out[index] = split_product(jnp.concatenate([even, odd], axis=1), matrix)


def copy_all(copies):
    for copy in copies:
        copy.start()
    return copies


def wait_all(copies):
    for copy in copies:
        copy.wait()


def in_groups(count, limit, function):
    size = largest_divisor(count, limit)

    def several(g, carry):
        for i in range(size):
            function(g * size + i)
        return carry

    lax.fori_loop(0, count // size, several, 0)


def sends_kernel(axis, dim, source, *refs):
    first, second, stage, sems = refs[-4:]
    odd = lax.axis_index(axis) & 1
    last = source.shape[dim] - HALO
    copies = []
    for i, start in enumerate(((1 - odd) * last, odd * last)):
        at = pl.ds(pl.multiple_of(start, HALO), HALO)
        piece = source.at[at] if dim == 0 else source.at[:, at]
        copies.append(pltpu.make_async_copy(piece, stage.at[i], sems.at[i]))
    copy_all(copies)
    outs = []
    for i, out in enumerate((first, second)):
        copies[i].wait()
        outs.append(pltpu.make_async_copy(stage.at[i], out, sems.at[2 + i]))
        outs[-1].start()
    wait_all(outs)


def corners_kernel(first_in, second_in, itab, first, second):
    odd = lax.axis_index("gx") & 1
    last = first_in.shape[0] - HALO
    swapped = (lax.axis_index("gy") & 1) == 0
    for out, start in ((first, (1 - odd) * last), (second, odd * last)):
        at = pl.ds(pl.multiple_of(start, HALO), HALO)
        low, high = first_in[at], second_in[at]
        out[:, pl.ds(0, HALO)] = jnp.where(swapped, high, low)
        out[:, pl.ds(HALO, HALO)] = jnp.where(swapped, low, high)


def interior_kernel(
    dims,
    density, first_side, second_side, stay_all, weights, free, itab, ftab,
    occupancy, q_edges, p_edges, acc_edges, sums,
    p, acc, q0, q1, stay, block, staged, sem_in, sem_stay, sem_edges, sem_out,
):
    block_first, block_second, _, _ = dims
    rows = block_second + 2 * HALO
    plane = 2 * rows
    chunk = 8
    chunks = block_first // chunk
    even = (lax.axis_index("gy") & 1) == 0
    lattice = Lattice(
        rows, 0, itab, ftab, block_first + 2 * HALO, weights, free, stay, p, acc, block_first
    )
    loads = copy_all(
        [
            pltpu.make_async_copy(
                density.at[pl.ds(c * chunk, chunk)], block.at[pl.ds(c * chunk, chunk)], sem_in.at[c]
            )
            for c in range(chunks)
        ]
    )
    stay_copy = pltpu.make_async_copy(
        stay_all.at[pl.ds(HALO * plane, block_first * plane)], stay, sem_stay
    )
    stay_copy.start()
    spread = parity_matrix(False)
    for c in range(chunks):
        loads[c].wait()

        def layer(i, c=c):
            local = c * chunk + i
            first, second = first_side[local], second_side[local]
            below = jnp.where(even, second, first)
            above = jnp.where(even, first, second)
            values = jnp.concatenate([below, block[local], above], axis=0)
            lattice.ingest(
                q0, split_product(values, spread), local, local + HALO, local, local
            )

        in_groups(chunk, 4, layer)
    stay_copy.wait()

    edges = []

    def export(k):
        q = (q0, q1)[k % 2]
        for side in range(2):
            layer = 2 * k if side == 0 else block_first - 2 * k - 4
            for turn in (-1, 0, 1):
                edges.append(
                    pltpu.make_async_copy(
                        q.at[pl.ds(lattice.moved(turn, layer * plane), 4 * plane)],
                        q_edges.at[k, side, turn + 1],
                        sem_edges.at[(k * 2 + side) * 4 + turn + 1],
                    )
                )
                edges[-1].start()
            layer = 2 * k if side == 0 else block_first - 2 * k - 2
            edges.append(
                pltpu.make_async_copy(
                    p.at[pl.ds(layer * plane, 2 * plane)],
                    p_edges.at[k, side],
                    sem_edges.at[(k * 2 + side) * 4 + 3],
                )
            )
            edges[-1].start()

    def layout_of(low, unroll):
        def layout(b):
            local = low + b * unroll
            return [Segment(unroll, local, local + HALO, local, local, local)]

        return layout

    export(0)
    for k in range(1, STEPS):
        low, high = 2 * k, block_first - 2 * k
        unroll = largest_divisor(high - low, BODY_LAYERS)
        lattice.advance(
            k, (q0, q1)[(k - 1) % 2], (q0, q1)[k % 2], (high - low) // unroll, layout_of(low, unroll)
        )
        export(k)
    for side in range(2):
        layer = 0 if side == 0 else block_first - HALO
        edges.append(
            pltpu.make_async_copy(
                acc.at[pl.ds(layer * plane, HALO * plane)], acc_edges.at[side], sem_edges.at[32 + side]
            )
        )
        edges[-1].start()
    inner = block_first - 2 * HALO
    unroll = largest_divisor(inner, 8)
    mass, hit = lattice.finish((q0, q1)[(STEPS - 1) % 2], inner // unroll, layout_of(HALO, unroll))
    sums[pl.ds(0, ROWS), :] = mass
    sums[pl.ds(ROWS, ROWS), :] = hit
    gather = parity_matrix(True)
    in_groups(inner, 4, lambda i: lattice.restore(HALO + i, staged, i, gather))
    out = pltpu.make_async_copy(staged, occupancy.at[pl.ds(HALO, inner)], sem_out)
    out.start()
    out.wait()
    wait_all(edges)


SIDE = 2 * HALO + 2
SIDE_MOVED = HALO + 4


def edges_kernel(
    dims, devices,
    first_halo, second_halo, first_corner, second_corner, stay_all, q_edges, p_edges, acc_edges, sums_in,
    weights, free, itab, ftab, occupancy_in,
    occupancy, row_out,
    p, acc, q0, q1, q2, q3, stay, staged, sem_q, sem_p, sem_other, sem_out,
):
    block_first, block_second, _, _ = dims
    rows = block_second + 2 * HALO
    plane = 2 * rows
    q = (q0, q1, q2, q3)
    right_table = block_first - 2
    lattice = Lattice(
        rows, 1, itab, ftab, block_first + 2 * HALO, weights, free, stay, p, acc, 2 * SIDE_MOVED
    )
    early, imports = [], []
    p_imports = [[] for _ in range(STEPS)]
    for side in range(2):
        first = 2
        early.append(
            pltpu.make_async_copy(
                stay_all.at[pl.ds(((0, right_table)[side] + first) * plane, (SIDE - 4) * plane)],
                stay.at[pl.ds((side * SIDE + first) * plane, (SIDE - 4) * plane)],
                sem_other.at[side],
            )
        )
        early.append(
            pltpu.make_async_copy(
                acc_edges.at[side],
                acc.at[pl.ds(side * HALO * plane, HALO * plane)],
                sem_other.at[2 + side],
            )
        )
        for k in range(STEPS):
            layer = 2 * k + HALO if side == 0 else SIDE + 8 - 2 * k
            p_imports[k].append(
                pltpu.make_async_copy(
                    p_edges.at[k, side], p.at[pl.ds(layer * plane, 2 * plane)], sem_p.at[k * 2 + side]
                )
            )
    for k in range(STEPS):
        imports.append([])
        for side in range(2):
            layer = HALO if side == 0 else SIDE_MOVED
            for turn in (-1, 0, 1):
                imports[k].append(
                    pltpu.make_async_copy(
                        q_edges.at[k, side, turn + 1],
                        q[k].at[pl.ds(lattice.moved(turn, layer * plane), 4 * plane)],
                        sem_q.at[(k * 2 + side) * 3 + turn + 1],
                    )
                )
    copy_all(imports[0])
    copy_all(early)
    copy_all(p_imports[0])
    for k in range(1, STEPS):
        copy_all(imports[k] + p_imports[k])
    spread = parity_matrix(False)
    even = (lax.axis_index("gx") & 1) == 0
    for side in range(2):

        def layer(i, side=side):
            take_first = even if side == 1 else ~even
            corner = jnp.where(take_first, first_corner[i], second_corner[i])
            main = jnp.where(take_first, first_halo[i], second_halo[i])
            values = jnp.concatenate([corner[:HALO], main, corner[HALO:]], axis=0)
            lattice.ingest(
                q0,
                split_product(values, spread),
                i if side == 0 else SIDE + 10 + i,
                i if side == 0 else block_first + HALO + i,
                i if side == 0 else SIDE_MOVED + 4 + i,
                None,
            )

        in_groups(HALO, 4, layer)
    wait_all(early)

    def layout_of(k):
        def layout(b):
            return [
                Segment(HALO, 2 * k, 2 * k, 2, 0, 2 * k - HALO),
                Segment(
                    HALO, SIDE + 10 - 2 * k, block_first + HALO - 2 * k,
                    SIDE_MOVED + 2, SIDE_MOVED + 4, 2 * HALO - 2 * k,
                ),
            ]

        return layout

    for k in range(1, STEPS):
        wait_all(imports[k - 1] + p_imports[k - 1])
        own = [u >= HALO - 2 * k for u in range(HALO)] + [u < 2 * k for u in range(HALO)]
        lattice.advance(k, q[k - 1], q[k], 1, layout_of(k), own)
    wait_all(imports[STEPS - 1] + p_imports[STEPS - 1])
    mass, hit = lattice.finish(q[STEPS - 1], 1, layout_of(STEPS))
    gather = parity_matrix(True)
    outs = []
    for side in range(2):
        in_groups(
            HALO,
            4,
            lambda i, side=side: lattice.restore(side * HALO + i, staged, side * HALO + i, gather),
        )
        outs.append(
            pltpu.make_async_copy(
                staged.at[pl.ds(side * HALO, HALO)],
                occupancy.at[pl.ds(0 if side == 0 else block_first - HALO, HALO)],
                sem_out.at[side],
            )
        )
        outs[-1].start()
    mass = jnp.sum(mass + sums_in[pl.ds(0, ROWS), :])
    hit = jnp.sum(hit + sums_in[pl.ds(ROWS, ROWS), :])
    lane = lax.broadcasted_iota(jnp.int32, (devices, LANES), 1)
    row_out[...] = jnp.where(lane == 0, hit, jnp.where(lane == 1, mass, 0.0))
    wait_all(outs)


def body(density, reaction_rates, state_changes, target_box, truncation):
    block_first, block_second, species_third = density.shape
    extents = (
        block_first * lax.axis_size("gx"),
        block_second * lax.axis_size("gy"),
        species_third,
    )
    count_first, count_second = lax.axis_size("gx"), lax.axis_size("gy")
    devices = count_first * count_second
    rows = block_second + 2 * HALO
    plane = 2 * rows
    layers = block_first + 2 * HALO
    dims = (block_first, block_second, extents, (block_first, 2 * SIDE_MOVED))

    def exchange(pieces, axis, count):
        received = []
        for start, piece in enumerate(pieces):
            pairs = [(i, i + 1) for i in range(start, count - 1, 2)]
            received.append(lax.ppermute(piece, axis, pairs + [(j, i) for i, j in pairs]))
        return received

    f32 = jnp.float32
    smem = pl.BlockSpec(memory_space=pltpu.SMEM)
    vmem = pl.BlockSpec(memory_space=pltpu.VMEM)
    hbm = pl.BlockSpec(memory_space=pl.ANY)
    params = pltpu.CompilerParams(vmem_limit_bytes=VMEM_LIMIT)
    chunk = largest_divisor(layers, 8)

    def sends(axis, dim, *after):
        shape = tuple(HALO if d == dim else size for d, size in enumerate(density.shape))
        return pl.pallas_call(
            functools.partial(sends_kernel, axis, dim),
            out_shape=(jax.ShapeDtypeStruct(shape, f32),) * 2,
            in_specs=[hbm] * (1 + len(after)),
            out_specs=(hbm, hbm),
            scratch_shapes=[pltpu.VMEM((2,) + shape, f32), pltpu.SemaphoreType.DMA((4,))],
            compiler_params=params,
            name="sends",
        )(density, *after)

    side_sends = sends("gy", 1)
    first_side, second_side = exchange(side_sends, "gy", count_second)
    first_halo, second_halo = exchange(sends("gx", 0, side_sends[0]), "gx", count_first)

    stay, weights, free, itab, ftab = pl.pallas_call(
        functools.partial(tables_kernel, dims),
        grid=(layers // chunk,),
        out_shape=(
            jax.ShapeDtypeStruct((layers, 2, rows, LANES), f32),
            jax.ShapeDtypeStruct((12 * rows, LANES), f32),
            jax.ShapeDtypeStruct((6 * rows, LANES), f32),
            jax.ShapeDtypeStruct((KINDS + layers + 4,), jnp.int32),
            jax.ShapeDtypeStruct(((layers + 4) * REACTIONS + 8,), f32),
        ),
        in_specs=[smem] * 4,
        out_specs=(
            pl.BlockSpec((chunk, 2, rows, LANES), lambda i: (i, 0, 0, 0)),
            pl.BlockSpec((12 * rows, LANES), lambda i: (0, 0)),
            pl.BlockSpec((6 * rows, LANES), lambda i: (0, 0)),
            smem,
            smem,
        ),
        scratch_shapes=[pltpu.VMEM((12 * rows, LANES), f32)],
        compiler_params=params,
        name="tables",
    )(reaction_rates, state_changes, target_box, truncation)
    stay = stay.reshape(layers * plane, LANES)

    corner = jax.ShapeDtypeStruct((HALO, 2 * HALO, species_third), f32)
    corner_sends = pl.pallas_call(
        corners_kernel,
        out_shape=(corner, corner),
        in_specs=[vmem, vmem, smem],
        out_specs=(vmem, vmem),
        compiler_params=params,
        name="corners",
    )(first_side, second_side, itab)
    first_corner, second_corner = exchange(corner_sends, "gx", count_first)

    def scratch(own, totals, moved, steps):
        return (
            [pltpu.VMEM((own * plane, LANES), f32), pltpu.VMEM((totals * plane, LANES), f32)]
            + [pltpu.VMEM((3 * moved * plane + 2 * PAD, LANES), f32) for _ in range(steps)]
            + [pltpu.VMEM((own * plane, LANES), f32)]
        )

    chunks = block_first // 8
    occupancy, q_edges, p_edges, acc_edges, sums = pl.pallas_call(
        functools.partial(interior_kernel, dims),
        out_shape=(
            jax.ShapeDtypeStruct(density.shape, f32),
            jax.ShapeDtypeStruct((STEPS, 2, 3, 4 * plane, LANES), f32),
            jax.ShapeDtypeStruct((STEPS, 2, 2 * plane, LANES), f32),
            jax.ShapeDtypeStruct((2, HALO * plane, LANES), f32),
            jax.ShapeDtypeStruct((2 * ROWS, LANES), f32),
        ),
        in_specs=[hbm, vmem, vmem, hbm, vmem, vmem, smem, smem],
        out_specs=(hbm, hbm, hbm, hbm, vmem),
        scratch_shapes=scratch(block_first, block_first, block_first, 2)
        + [
            pltpu.VMEM((block_first, block_second, species_third), f32),
            pltpu.VMEM((block_first - 2 * HALO, block_second, species_third), f32),
            pltpu.SemaphoreType.DMA((chunks,)),
            pltpu.SemaphoreType.DMA,
            pltpu.SemaphoreType.DMA((34,)),
            pltpu.SemaphoreType.DMA,
        ],
        compiler_params=params,
        cost_estimate=pl.CostEstimate(flops=400_000_000, bytes_accessed=40_000_000, transcendentals=0),
        name="interior",
    )(density, first_side, second_side, stay, weights, free, itab, ftab)

    occupancy, row = pl.pallas_call(
        functools.partial(edges_kernel, dims, devices),
        out_shape=(
            jax.ShapeDtypeStruct(density.shape, f32),
            jax.ShapeDtypeStruct((devices, LANES), f32),
        ),
        in_specs=[vmem] * 4 + [hbm] * 4 + [vmem] * 3 + [smem] * 2 + [hbm],
        out_specs=(hbm, vmem),
        scratch_shapes=scratch(2 * SIDE, 2 * HALO, 2 * SIDE_MOVED, STEPS)
        + [
            pltpu.VMEM((2 * HALO, block_second, species_third), f32),
            pltpu.SemaphoreType.DMA((24,)),
            pltpu.SemaphoreType.DMA((8,)),
            pltpu.SemaphoreType.DMA((4,)),
            pltpu.SemaphoreType.DMA((2,)),
        ],
        input_output_aliases={13: 0},
        compiler_params=params,
        name="edges",
    )(
        first_halo, second_halo, first_corner, second_corner, stay, q_edges, p_edges, acc_edges, sums,
        weights, free, itab, ftab, occupancy,
    )
    rows_in = lax.all_to_all(row, ("gx", "gy"), 0, 0, tiled=True)
    summary = jnp.sum(rows_in[:, :2], axis=0) * (1.0 / math.prod(extents))
    return occupancy, summary


def solution(mesh):
    placed = (P("gx", "gy", None), P(), P(), P(), P())
    return jax.shard_map(
        body, mesh=mesh, in_specs=placed, out_specs=(P("gx", "gy", None), P()), check_vma=False
    )
```

time: 123 us -> 98.7 us (0.80)
  waiting for transfers between devices: 8.94 us -> 0.02 us
  Pallas kernels: 76.9 us -> 71 us
  starting transfers between devices: 14.1 us -> 10.3 us
  local copies, waits for them, and re-layouts: 5.81 us -> 2.48 us
  blocking collectives: 14.9 us -> 13.1 us
    ppermute x6, waiting for transfers between devices: 8.94 us -> 0.02 us  [exchange(): lax.ppermute(piece, axis, pairs + [(j, i) for i, j in pairs])]
    pallas_call x1, Pallas kernels: 37.6 us -> 29.2 us  [body(): pl.pallas_call(functools.partial(interior_kernel, dims), out_shape=(jax.S...]
    pallas_call x0 -> x3, Pallas kernels: none -> 6.16 us  [the longest x2 4.39 us: sends(): pl.pallas_call(functools.partial(sends_kernel, axis, dim), out_shape=(jax...]
    slice x4 -> x0, local copies, waits for them, and re-layouts: 4.12 us -> none  [the longest x1 3.03 us: body(): halo_high = to_previous(density[:HALO], 'gx', count_first)]
    ppermute x6, starting transfers between devices: 14.1 us -> 10.3 us  [exchange(): lax.ppermute(piece, axis, pairs + [(j, i) for i, j in pairs])]
    pallas_call x1, Pallas kernels: 28.8 us -> 25.5 us  [body(): pl.pallas_call(functools.partial(edges_kernel, dims, devices), out_shape=...]
    all_to_all x1, blocking collectives: 14.9 us -> 13.1 us  [body(): rows_in = lax.all_to_all(row, ('gx', 'gy'), 0, 0, tiled=True)]
    unnamed x13 -> x15, local copies, waits for them, and re-layouts: 1.69 us -> 2.48 us
  transfers between devices with their start and end apart: 6 -> 6, of which waited for: 1 -> 0; matrix products, arithmetic and copies ran while one was open for 4% -> 1% of each run, Pallas kernels for 39% -> 42%
where the time goes in v2:
time: 98.7 us; the launch traced here: 98.3 us
  Pallas kernels  71 us (72%)
  blocking collectives  13.1 us (13%)
  starting transfers between devices  10.3 us (10%)
  local copies, waits for them, and re-layouts  2.48 us (3%)
    pallas_call x1, Pallas kernels, body(): pl.pallas_call(functools.partial(interior_kernel, dims), out_shape=(jax.S...  29.2 us
    pallas_call x1, Pallas kernels, body(): pl.pallas_call(functools.partial(edges_kernel, dims, devices), out_shape=...  25.5 us
    all_to_all x1, blocking collectives, body(): rows_in = lax.all_to_all(row, ('gx', 'gy'), 0, 0, tiled=True)  13.1 us
    ppermute x6, starting transfers between devices, exchange(): lax.ppermute(piece, axis, pairs + [(j, i) for i, j in pairs])  10.3 us
    pallas_call x1, Pallas kernels, body(): pl.pallas_call(functools.partial(tables_kernel, dims), grid=(layers // ch...  10.2 us
    pallas_call x2, Pallas kernels, sends(): pl.pallas_call(functools.partial(sends_kernel, axis, dim), out_shape=(jax...  4.39 us
    unnamed x15, local copies, waits for them, and re-layouts  2.48 us
  transfers between devices with their start and end apart: 6, of which 0 were waited for; matrix products, arithmetic and copies ran while one was open for 1% of the time, Pallas kernels for 42%

profile of v2, /device:TPU:0, one launch (start us, length us, event | category | flops | bytes accessed | tf_op | source)
XLA Modules:
  0.0 98.3 jit_solution(14036900671460288759)
XLA Ops:
  0.6 0.0 copy-start.6
  0.6 1.8 %sends.2 = (f32[32,8,256]{2,1,0:T(8,128)}, f32[32,8,256]{2,1,0:T(8,128)}) custom-call(f32[32,128,256]{2,1,0:T(8,128)} %density.1), custom_call_target="tpu_custom_call" | custom-call | tf_op jit(solution)/shard_map/sends/pallas_call | solution.py:686
  2.4 0.0 copy-start.3
  2.4 2.6 %sends.3 = (f32[8,128,256]{2,1,0:T(8,128)}, f32[8,128,256]{2,1,0:T(8,128)}) custom-call(f32[32,128,256]{2,1,0:T(8,128)} %density.1, f32[32,8,256]{2,1,0:T(8,128)} %get-tuple-element.20.refs_0_), custom_call_target="tpu_custom_call" | custom-call | tf_op jit(solution)/shard_map/sends/pallas_call | solution.py:686
  5.1 0.5 collective-permute-start
  5.6 1.6 %collective-permute-start.1 = (f32[8,128,256]{2,1,0:T(8,128)}, f32[8,128,256]{2,1,0:T(8,128)}, u32[]{:S(2)}, u32[]{:S(2)}) collective-permute-start(f32[8,128,256]{2,1,0:T(8,128)} %get-tuple-element.22), channel_id=1, source_target_pairs={{4,8},{12,16},{20,24},{8,4},{16,12},{24,20},{5,9},{13,17},{21,25},... | collective-permute-start | bytes 3145736 | tf_op jit(solution)/shard_map/ppermute | solution.py:674
  7.2 0.7 collective-permute-start.3
  7.9 0.0 copy-done.3
  7.9 5.5 %collective-permute-start.2 = (f32[32,8,256]{2,1,0:T(8,128)S(1)}, f32[32,8,256]{2,1,0:T(8,128)S(1)}, u32[]{:S(2)}, u32[]{:S(2)}) collective-permute-start(f32[32,8,256]{2,1,0:T(8,128)S(1)} %copy-done.3), channel_id=1, source_target_pairs={{0,1},{2,3},{1,0},{3,2},{4,5},{6,7},{5,4},{7,6},{8,9},{10,11},{9,8... | collective-permute-start | bytes 786440 | tf_op jit(solution)/shard_map/ppermute | solution.py:674
  13.4 0.0 copy-done.6
  13.4 0.7 copy.9.changes
  14.0 10.2 %tables.1 = (f32[48,2,144,128]{3,2,1,0:T(8,128)}, f32[1728,128]{1,0:T(8,128)}, f32[864,128]{1,0:T(8,128)}, s32[76]{0:T(128)}, f32[320]{0:T(512)}) custom-call(f32[6]{0:T(128)} %rates.1, s32[6,3]{1,0:T(8,128)} %copy.9.changes, s32[2,3]{1,0:T(2,128)} %box.1, s32[2]{0:T(128)} %truncation.1), custom_call_target="tpu_custom_call" | custom-call | tf_op jit(solution)/shard_map/tables/pallas_call | solution.py:700
  24.3 0.0 collective-permute-done.3.second_in.second_side
  24.3 0.0 copy-start.1
  24.3 0.0 collective-permute-done.2.first_in.first_side
  24.3 0.0 copy-start.2
  24.3 0.7 copy-done.1
  25.0 0.1 copy-done.2
  25.1 1.8 %corners.1 = (f32[8,16,256]{2,1,0:T(8,128)}, f32[8,16,256]{2,1,0:T(8,128)}) custom-call(f32[32,8,256]{2,1,0:T(8,128)} %copy-done.2, f32[32,8,256]{2,1,0:T(8,128)} %copy-done.1, s32[76]{0:T(128)} %get-tuple-element.24.itab), custom_call_target="tpu_custom_call" | custom-call | tf_op jit(solution)/shard_map/corners/pallas_call | solution.py:725
  26.9 1.3 %collective-permute-start.4 = (f32[8,16,256]{2,1,0:T(8,128)}, f32[8,16,256]{2,1,0:T(8,128)S(1)}, u32[]{:S(2)}, u32[]{:S(2)}) collective-permute-start(f32[8,16,256]{2,1,0:T(8,128)} %get-tuple-element.25), channel_id=1, source_target_pairs={{0,4},{8,12},{16,20},{24,28},{4,0},{12,8},{20,16},{28,24},{1,5},{9... | collective-permute-start | bytes 393224 | tf_op jit(solution)/shard_map/ppermute | solution.py:674
  28.2 0.7 collective-permute-start.5
  28.9 29.2 %interior.1 = (f32[32,128,256]{2,1,0:T(8,128)}, f32[4,2,3,1152,128]{4,3,2,1,0:T(8,128)}, f32[4,2,576,128]{3,2,1,0:T(8,128)}, f32[2,2304,128]{2,1,0:T(8,128)}, f32[32,128]{1,0:T(8,128)}) custom-call(f32[32,128,256]{2,1,0:T(8,128)} %density.1, f32[32,8,256]{2,1,0:T(8,128)} %copy-done.2, f32[32,8,256]{2,1,0:T(8,128)} %copy-done.1, f32[13824,128]{1,0:T(8,128)} %bitcast.5, ...), custom_call_target="tpu_custom_call" | custom-call | flops 400000000 | bytes 40000000 | tf_op jit(solution)/shard_map/interior/pallas_call | solution.py:743
  58.1 0.0 collective-permute-done.4.first_corner
  58.1 0.0 copy-start.4
  58.1 0.0 collective-permute-done.5.second_corner
  58.1 0.0 copy-start.5
  58.1 0.0 collective-permute-done.first_halo
  58.1 0.0 copy-start
  58.1 0.0 collective-permute-done.1.second_halo
  58.1 0.6 copy-done.4
  58.7 0.0 copy-done.5
  58.8 0.4 copy-done
  59.1 25.5 %edges.1 = (f32[32,128,256]{2,1,0:T(8,128)}, f32[32,128]{1,0:T(8,128)}) custom-call(f32[8,128,256]{2,1,0:T(8,128)} %copy-done, f32[8,128,256]{2,1,0:T(8,128)} %collective-permute-done.1.second_halo, f32[8,16,256]{2,1,0:T(8,128)} %copy-done.4, f32[8,16,256]{2,1,0:T(8,128)} %copy-done.5, f32[13824,128]{1,0:T(8,128)} %bitcast.6, ...), custom_call_target="tpu_custom_call", output_to_operand_aliasing={{0}: (13, {})} | custom-call | tf_op jit(solution)/shard_map/edges/pallas_call | solution.py:768
  84.6 13.1 %all_to_all.12 = f32[32,1,128]{2,1,0:T(1,128)S(1)} all-to-all(f32[32,1,128]{2,1,0:T(1,128)} %bitcast.8), channel_id=1, replica_groups=mesh['gx'=8,'gy'=4] {'gx','gy'}, dimensions={0} | all-to-all | bytes 32768 | tf_op jit(solution)/shard_map/all_to_all | solution.py:791
  97.8 0.5 broadcast_multiply_fusion
  (1 shorter events, 0.0 us)
Async XLA Ops:
  0.6 12.7 %copy-start.6 = (s32[6,3]{0,1:T(4,128)S(1)}, s32[6,3]{0,1:T(4,128)}, u32[]{:S(2)}) copy-start(s32[6,3]{0,1:T(4,128)} %param.7) | copy-start | bytes 220
  2.4 5.4 %copy-start.3 = (f32[32,8,256]{2,1,0:T(8,128)S(1)}, f32[32,8,256]{2,1,0:T(8,128)}, u32[]{:S(2)}) copy-start(f32[32,8,256]{2,1,0:T(8,128)} %get-tuple-element.20.refs_0_) | copy-start | bytes 786436
  5.1 53.0 %collective-permute-start = (f32[8,128,256]{2,1,0:T(8,128)}, f32[8,128,256]{2,1,0:T(8,128)S(1)}, u32[]{:S(2)}, u32[]{:S(2)}) collective-permute-start(f32[8,128,256]{2,1,0:T(8,128)} %get-tuple-element.21), channel_id=1, source_target_pairs={{0,4},{8,12},{16,20},{24,28},{4,0},{12,8},{20,16},{28,24},{1,5},{9... | collective-permute-start | bytes 3145736 | tf_op jit(solution)/shard_map/ppermute | solution.py:674
  5.6 52.5 %collective-permute-start.1 = (f32[8,128,256]{2,1,0:T(8,128)}, f32[8,128,256]{2,1,0:T(8,128)}, u32[]{:S(2)}, u32[]{:S(2)}) collective-permute-start(f32[8,128,256]{2,1,0:T(8,128)} %get-tuple-element.22), channel_id=1, source_target_pairs={{4,8},{12,16},{20,24},{8,4},{16,12},{24,20},{5,9},{13,17},{21,25},... | collective-permute-start | bytes 3145736 | tf_op jit(solution)/shard_map/ppermute | solution.py:674
  7.2 17.1 %collective-permute-start.3 = (f32[32,8,256]{2,1,0:T(8,128)}, f32[32,8,256]{2,1,0:T(8,128)S(1)}, u32[]{:S(2)}, u32[]{:S(2)}) collective-permute-start(f32[32,8,256]{2,1,0:T(8,128)} %get-tuple-element.23), channel_id=1, source_target_pairs={{1,2},{2,1},{5,6},{6,5},{9,10},{10,9},{13,14},{14,13},{17,18},{18,... | collective-permute-start | bytes 786440 | tf_op jit(solution)/shard_map/ppermute | solution.py:674
  7.9 16.4 %collective-permute-start.2 = (f32[32,8,256]{2,1,0:T(8,128)S(1)}, f32[32,8,256]{2,1,0:T(8,128)S(1)}, u32[]{:S(2)}, u32[]{:S(2)}) collective-permute-start(f32[32,8,256]{2,1,0:T(8,128)S(1)} %copy-done.3), channel_id=1, source_target_pairs={{0,1},{2,3},{1,0},{3,2},{4,5},{6,7},{5,4},{7,6},{8,9},{10,11},{9,8... | collective-permute-start | bytes 786440 | tf_op jit(solution)/shard_map/ppermute | solution.py:674
  24.3 0.7 copy-start.1
  24.3 0.8 copy-start.2
  26.9 31.2 %collective-permute-start.4 = (f32[8,16,256]{2,1,0:T(8,128)}, f32[8,16,256]{2,1,0:T(8,128)S(1)}, u32[]{:S(2)}, u32[]{:S(2)}) collective-permute-start(f32[8,16,256]{2,1,0:T(8,128)} %get-tuple-element.25), channel_id=1, source_target_pairs={{0,4},{8,12},{16,20},{24,28},{4,0},{12,8},{20,16},{28,24},{1,5},{9... | collective-permute-start | bytes 393224 | tf_op jit(solution)/shard_map/ppermute | solution.py:674
  28.2 29.9 %collective-permute-start.5 = (f32[8,16,256]{2,1,0:T(8,128)}, f32[8,16,256]{2,1,0:T(8,128)S(1)}, u32[]{:S(2)}, u32[]{:S(2)}) collective-permute-start(f32[8,16,256]{2,1,0:T(8,128)} %get-tuple-element.26), channel_id=1, source_target_pairs={{4,8},{12,16},{20,24},{8,4},{16,12},{24,20},{5,9},{13,17},{21,25},... | collective-permute-start | bytes 393224 | tf_op jit(solution)/shard_map/ppermute | solution.py:674
  58.1 0.6 copy-start.4
  58.1 0.7 copy-start.5
  58.1 1.0 %copy-start = (f32[8,128,256]{2,1,0:T(8,128)}, f32[8,128,256]{2,1,0:T(8,128)S(1)}, u32[]{:S(2)}) copy-start(f32[8,128,256]{2,1,0:T(8,128)S(1)} %collective-permute-done.first_halo) | copy-start | bytes 3145732

commit v3 on v2

--- a/solution.py
+++ b/solution.py
@@ -23,7 +23,7 @@
 VMEM_LIMIT = 62 << 20
 
 
-KINDS = 24
+ABOVE = 2
 
 
 def largest_divisor(number, limit):
@@ -37,7 +37,9 @@
 
 
 def tables_kernel(
-    dims, rates, changes, box, truncation, stay, weights, free, itab, ftab, plain
+    dims, rates, changes, box, truncation,
+    stay, weights, free, offsets, series, firsts, kinds,
+    staged, sem_stay,
 ):
     block_first, block_second, extents, kernel_layers = dims
     rows = block_second + 2 * HALO
@@ -45,126 +47,147 @@
     layers = block_first + 2 * HALO
     anchor_first = lax.axis_index("gx") * block_first - HALO
     anchor_second = lax.axis_index("gy") * block_second - HALO
-    step = pl.program_id(0)
 
     def order(r, d):
-        return jnp.maximum(-changes[r, d], 0)
-
-    @pl.when(step == 0)
-    def _():
-        corner = jnp.float32(0.0)
+        return jnp.maximum(-changes[d, r], 0)
+
+    def by_reaction(index, value, copies=1):
+        found = jnp.zeros(index.shape, jnp.float32)
         for r in range(REACTIONS):
-            term = rates[r]
-            for d in range(3):
-                e = float(extents[d])
-                s = order(r, d)
-                term = term * jnp.where(
-                    s == 0,
-                    1.0,
-                    jnp.where(s == 1, (e - 1.0) / e, (e - 1.0) * (e - 2.0) / (e * e)),
+            here = index == r
+            for c in range(1, copies):
+                here = here | (index == r + c * REACTIONS)
+            found = jnp.where(here, value(r), found)
+        return found
+
+    def orders_by_reaction(index, d, copies):
+        return by_reaction(index, lambda r: order(r, d).astype(jnp.float32), copies)
+
+    corner = jnp.float32(0.0)
+    for r in range(REACTIONS):
+        term = rates[r]
+        for d in range(3):
+            e = float(extents[d])
+            s = order(r, d)
+            term = term * jnp.where(
+                s == 0, 1.0, jnp.where(s == 1, (e - 1.0) / e, (e - 1.0) * (e - 2.0) / (e * e))
+            )
+        corner = corner + term
+    inverse = 1.0 / jnp.full((rows, LANES), headroom * corner, jnp.float32)
+    row = lax.broadcasted_iota(jnp.int32, (rows, LANES), 0) + anchor_second
+    lane = lax.broadcasted_iota(jnp.int32, (rows, LANES), 1)
+    real_row = (row >= 0) & (row < extents[1])
+    box_row = (row >= box[0, 1]) & (row < box[1, 1])
+    for h in range(2):
+        third = 2 * lane + h
+        box_here = box_row & (third >= box[0, 2]) & (third < box[1, 2])
+        free[pl.ds(h * rows, rows), :] = jnp.where(real_row, 1.0, 0.0)
+        free[pl.ds(plane + h * rows, rows), :] = jnp.where(real_row & ~box_here, 1.0, 0.0)
+        free[pl.ds(2 * plane + h * rows, rows), :] = jnp.zeros((rows, LANES), jnp.float32)
+
+    copies = 3
+    split_lane = lax.broadcasted_iota(jnp.int32, (1, LANES), 1)
+    first_order = orders_by_reaction(split_lane, 0, copies)
+    along_rows = jnp.where(
+        lane < copies * REACTIONS,
+        counts_factor(
+            row.astype(jnp.float32),
+            orders_by_reaction(split_lane, 1, copies),
+            float(extents[1]),
+        )
+        * by_reaction(split_lane, lambda r: rates[r], copies)
+        * inverse,
+        0.0,
+    )
+    term = lax.broadcasted_iota(jnp.int32, (LANES, 2 * LANES), 0)
+    place = lax.broadcasted_iota(jnp.int32, (LANES, 2 * LANES), 1)
+    third = 2 * (place & (LANES - 1)) + (place >> 7)
+    along_third = counts_factor(
+        third.astype(jnp.float32),
+        orders_by_reaction(term[:, :LANES], 2, copies)[:, :1],
+        float(extents[2]),
+    )
+    high = along_third.astype(jnp.bfloat16).astype(jnp.float32)
+    low = along_third - high
+    is_low = (term >= REACTIONS) & (term < 2 * REACTIONS)
+    along_third = jnp.where(
+        term < copies * REACTIONS, jnp.where(is_low, low, high), 0.0
+    ).astype(jnp.bfloat16)
+
+    stay_copies = []
+    chunk = largest_divisor(layers, 8)
+
+    def stay_layer(i):
+        n0 = anchor_first + i
+        real = (n0 >= 0) & (n0 < extents[0])
+        in_box = (n0 >= box[0, 0]) & (n0 < box[1, 0])
+        kind = jnp.where(real, jnp.where(in_box, 1, 0), 2)
+        along_first = counts_factor(
+            jnp.full((1, LANES), n0, jnp.int32).astype(jnp.float32), first_order, float(extents[0])
+        )
+        whole = along_rows * along_first
+        upper = whole.astype(jnp.bfloat16).astype(jnp.float32)
+        split = jnp.where(lane < 2 * REACTIONS, upper, whole - upper).astype(jnp.bfloat16)
+        total = jnp.dot(split, along_third, preferred_element_type=jnp.float32)
+        for h in range(2):
+            mask = free[pl.ds(pl.multiple_of(kind * plane + h * rows, 8), rows), :]
+            at = pl.multiple_of(i * plane + h * rows, 8)
+            staged[pl.ds(at, rows), :] = 1.0 - mask * total[:, h * LANES : (h + 1) * LANES]
+
+    for c in range(layers // chunk):
+        in_groups(chunk, 4, lambda i, c=c: stay_layer(c * chunk + i))
+        at = pl.ds(c * chunk * plane, chunk * plane)
+        stay_copies.append(pltpu.make_async_copy(staged.at[at], stay.at[at], sem_stay.at[c]))
+        stay_copies[-1].start()
+
+    for h in range(2):
+        third = 2 * lane + h
+
+        def coefficient(r, carry, h=h, third=third):
+            from_row = row - changes[1, r]
+            from_third = third - changes[2, r]
+            moved = (
+                inverse
+                * rates[r]
+                * counts_factor(from_row.astype(jnp.float32), order(r, 1), float(extents[1]))
+                * counts_factor(from_third.astype(jnp.float32), order(r, 2), float(extents[2]))
+            )
+            inside = (from_third >= 0) & (from_third < extents[2])
+            at = pl.ds(pl.multiple_of((r * 2 + h) * rows, 8), rows)
+            weights[at, :] = jnp.where(inside, moved, 0.0)
+            return carry
+
+        lax.fori_loop(0, REACTIONS, coefficient, 0)
+    for which in range(2):
+        for r in range(REACTIONS):
+            for h in range(2):
+                source = h - changes[2, r]
+                offsets[which * 12 + r * 2 + h] = (
+                    PAD
+                    + (((source >> 1) + 1) * kernel_layers[which] - changes[0, r]) * plane
+                    + (source & 1) * rows
+                    - changes[1, r]
                 )
-            corner = corner + term
-        inverse = 1.0 / jnp.full((rows, LANES), headroom * corner, jnp.float32)
-        row = lax.broadcasted_iota(jnp.int32, (rows, LANES), 0) + anchor_second
-        lane = lax.broadcasted_iota(jnp.int32, (rows, LANES), 1)
-        real_row = (row >= 0) & (row < extents[1])
-        box_row = (row >= box[0, 1]) & (row < box[1, 1])
-        for h in range(2):
-            third = 2 * lane + h
-            box_here = box_row & (third >= box[0, 2]) & (third < box[1, 2])
-            for v in range(3):
-                at = pl.ds((v * 2 + h) * rows, rows)
-                if v == 2:
-                    free[at, :] = jnp.zeros((rows, LANES), jnp.float32)
-                elif v == 1:
-                    free[at, :] = jnp.where(real_row & ~box_here, 1.0, 0.0)
-                else:
-                    free[at, :] = jnp.where(real_row, 1.0, 0.0)
-
-            def coefficient(r, carry):
-                scale = inverse * rates[r]
-                at = pl.ds(pl.multiple_of((r * 2 + h) * rows, 8), rows)
-                s1 = order(r, 1)
-                s2 = order(r, 2)
-                plain[at, :] = (
-                    scale
-                    * counts_factor(row.astype(jnp.float32), s1, float(extents[1]))
-                    * counts_factor(third.astype(jnp.float32), s2, float(extents[2]))
-                )
-                from_row = row - changes[r, 1]
-                from_third = third - changes[r, 2]
-                inside = (from_third >= 0) & (from_third < extents[2])
-                moved = (
-                    scale
-                    * counts_factor(from_row.astype(jnp.float32), s1, float(extents[1]))
-                    * counts_factor(from_third.astype(jnp.float32), s2, float(extents[2]))
-                )
-                weights[at, :] = jnp.where(inside, moved, 0.0)
-                return carry
-
-            lax.fori_loop(0, REACTIONS, coefficient, 0)
-        for which in range(2):
-            for r in range(REACTIONS):
-                for h in range(2):
-                    source = h - changes[r, 2]
-                    parity = source & 1
-                    turn = source >> 1
-                    itab[which * 12 + r * 2 + h] = (
-                        PAD
-                        + ((turn + 1) * kernel_layers[which] - changes[r, 0]) * plane
-                        + parity * rows
-                        - changes[r, 1]
-                    )
-
-        def layer_scalars(i, carry):
-            n0 = anchor_first - 2 + i
-            real = (n0 >= 0) & (n0 < extents[0])
-            in_box = (n0 >= box[0, 0]) & (n0 < box[1, 0])
-            itab[KINDS + i] = jnp.where(real, jnp.where(in_box, 1, 0), 2)
-            for r in range(REACTIONS):
-                source = (n0 - changes[r, 0]).astype(jnp.float32)
-                ftab[i * REACTIONS + r] = counts_factor(source, order(r, 0), float(extents[0]))
-            return carry
-
-        lax.fori_loop(0, layers + 4, layer_scalars, 0)
-        table = [
-            math.exp(-mean_jumps) * mean_jumps**j / math.factorial(j) for j in range(series_length)
-        ]
-        tails = []
-        for which in range(2):
-            tail = jnp.float32(0.0)
-            for j in range(STEPS + 1, series_length):
-                tail = tail + jnp.where(j <= truncation[which], jnp.float32(table[j]), 0.0)
-            tails.append(tail)
-        base = (layers + 4) * REACTIONS
-        for j in range(STEPS):
-            ftab[base + j] = jnp.float32(table[j])
-        ftab[base + STEPS] = jnp.float32(table[STEPS]) + tails[0]
-        ftab[base + STEPS + 1] = jnp.float32(table[STEPS]) + tails[1]
-
-    chunk = stay.shape[0]
-
-    def group(g, carry):
-        row0 = pl.multiple_of(g * ROWS, ROWS)
-        terms = [
-            [plain[pl.ds((r * 2 + h) * rows + row0, ROWS), :] for h in range(2)]
-            for r in range(REACTIONS)
-        ]
-        for i in range(chunk):
-            entry = step * chunk + i + 2
-            kind = itab[KINDS + entry]
-            firsts = [
-                ftab[(entry + changes[r, 0]) * REACTIONS + r] for r in range(REACTIONS)
-            ]
-            for h in range(2):
-                total = terms[0][h] * firsts[0]
-                for r in range(1, REACTIONS):
-                    total = total + terms[r][h] * firsts[r]
-                mask = free[pl.ds(pl.multiple_of(kind * plane + h * rows + row0, 8), ROWS), :]
-                stay[i, h, pl.ds(row0, ROWS), :] = 1.0 - mask * total
-        return carry
-
-    lax.fori_loop(0, rows // ROWS, group, 0)
+    n0 = lax.broadcasted_iota(jnp.int32, firsts.shape, 0) + (anchor_first - ABOVE)
+    reaction = lax.broadcasted_iota(jnp.int32, firsts.shape, 1)
+    change = by_reaction(reaction, lambda r: changes[0, r].astype(jnp.float32))
+    firsts[...] = counts_factor(
+        n0.astype(jnp.float32) - change, orders_by_reaction(reaction, 0, 1), float(extents[0])
+    )
+    real = (n0 >= 0) & (n0 < extents[0])
+    in_box = (n0 >= box[0, 0]) & (n0 < box[1, 0])
+    kinds[...] = jnp.where(real, jnp.where(in_box, 1, 0), 2)
+    table = [
+        math.exp(-mean_jumps) * mean_jumps**j / math.factorial(j) for j in range(series_length)
+    ]
+    for j in range(STEPS):
+        series[j] = jnp.float32(table[j])
+    for which in range(2):
+        tail = jnp.float32(0.0)
+        for j in range(STEPS + 1, series_length):
+            tail = tail + jnp.where(j <= truncation[which], jnp.float32(table[j]), 0.0)
+        series[STEPS + which] = jnp.float32(table[STEPS]) + tail
+    wait_all(stay_copies)
 
 
 def split_product(values, matrix):
@@ -189,22 +212,22 @@
 
 
 class Lattice:
-    def __init__(self, rows, which, itab, ftab, table_layers, weights, free, stay, p, acc, moved_layers):
+    def __init__(self, rows, which, tables, weights, free, stay, p, acc, moved_layers):
         self.rows, self.plane = rows, 2 * rows
-        self.which, self.itab, self.ftab = which, itab, ftab
+        self.which = which
+        self.offsets, self.series, self.firsts, self.kinds = tables
         self.weights, self.free, self.stay = weights, free, stay
         self.p, self.acc, self.moved_layers = p, acc, moved_layers
-        self.weight_base = (table_layers + 4) * REACTIONS
-        self.never = jnp.full((ROWS, LANES), itab[KINDS], jnp.int32) < 0
+        self.never = jnp.full((ROWS, LANES), self.kinds[0, 0], jnp.int32) < 0
 
     def moved(self, turn, row):
         return PAD + (turn + 1) * self.moved_layers * self.plane + row
 
     def kind(self, table):
-        return self.itab[KINDS + 2 + table]
+        return self.kinds[ABOVE + table, 0]
 
     def first(self, table, r):
-        return self.ftab[(table + 2) * REACTIONS + r]
+        return self.firsts[ABOVE + table, r]
 
     def mask(self, kind, h, row0, count):
         at = pl.multiple_of(kind * self.plane + h * self.rows + row0, 8)
@@ -219,7 +242,7 @@
             self.p[pl.ds(at, rows), :] = part
             if totals is not None:
                 at = pl.multiple_of(totals * self.plane + h * rows, 8)
-                self.acc[pl.ds(at, rows), :] = part * self.ftab[self.weight_base]
+                self.acc[pl.ds(at, rows), :] = part * self.series[0]
             masked = part * self.mask(kind, h, 0, rows)
             at = target * self.plane + h * rows
             for turn in (0, -1, 1):
@@ -243,7 +266,7 @@
             totals = None if segment.totals is None else segment.totals * self.plane + row0
             shift = segment.source * self.plane + row0
             sources = [
-                [self.itab[self.which * 12 + r * 2 + h] + shift for h in range(2)]
+                [self.offsets[self.which * 12 + r * 2 + h] + shift for h in range(2)]
                 for r in range(REACTIONS)
             ]
             for u in range(segment.count):
@@ -257,18 +280,22 @@
         if rolled is not None:
             value = jnp.where(self.never, rolled, value)
         value = value * self.stay[pl.ds(at, ROWS), :]
+        terms = [value]
         for r in range(REACTIONS):
             arriving = source[pl.ds(sources[r][h] + u * self.plane, ROWS), :]
-            value = value + arriving * coefficients[r][h] * firsts[r]
-        return at, value
-
-    def advance(self, k, source, target, blocks, layout, has_totals=None):
-        weight = self.ftab[self.weight_base + k]
+            terms.append(arriving * coefficients[r][h] * firsts[r])
+        while len(terms) > 1:
+            pairs = [terms[i : i + 2] for i in range(0, len(terms), 2)]
+            terms = [pair[0] + pair[1] if len(pair) == 2 else pair[0] for pair in pairs]
+        return at, terms[0]
+
+    def advance(self, k, source, target, blocks, layout, totals_by_layer=None):
+        weight = self.series[k]
         plane, rows = self.plane, self.rows
         counts = [segment.count for segment in layout(0)]
         size = sum(counts)
         offsets = [(s, u) for s, count in enumerate(counts) for u in range(count)]
-        lag = min(5, size // 3)
+        lag = min(6, size // 2)
 
         def center_row(before, index, h):
             s, u = offsets[index]
@@ -308,17 +335,18 @@
                     for h in range(2):
                         at, value = self.value(
                             source, place, h, coefficients, firsts,
-                            rolled[ready][1][h] if ready >= 0 else None,
+                            rolled[ready][1][1] if ready >= 0 and h == 1 else None,
                         )
                         self.p[pl.ds(at, ROWS), :] = value
                         masked = value * self.mask(kind, h, row0, ROWS)
                         row = target0 + u * plane + h * rows
                         target[pl.ds(pl.multiple_of(self.moved(0, row), 8), ROWS), :] = masked
-                        if has_totals is None or has_totals[index]:
-                            row = pl.multiple_of(totals0 + u * plane + h * rows, 8)
-                            self.acc[pl.ds(row, ROWS), :] = (
-                                self.acc[pl.ds(row, ROWS), :] + value * weight
-                            )
+                        if totals_by_layer is None or totals_by_layer[index]:
+                            at = pl.ds(pl.multiple_of(totals0 + u * plane + h * rows, 8), ROWS)
+                            total = value * weight
+                            if totals_by_layer is None or totals_by_layer[index] == "add":
+                                total = total + self.acc[at, :]
+                            self.acc[at, :] = total
                     while stored <= ready:
                         store_layer(before, stored, rolled[stored])
                         stored += 1
@@ -337,9 +365,9 @@
         for index in range(size):
             store_layer(last, index, roll_layer(last, index))
 
-    def finish(self, source, blocks, layout):
-        weight_density = self.ftab[self.weight_base + STEPS]
-        weight_totals = self.ftab[self.weight_base + STEPS + 1]
+    def finish(self, source, blocks, layout, more=None, fresh=None):
+        weight_density = self.series[STEPS]
+        weight_totals = self.series[STEPS + 1]
 
         def group(g, sums):
             row0 = pl.multiple_of(g * ROWS + HALO, 8)
@@ -347,7 +375,7 @@
 
             def block(b, sums):
                 mass, hit = sums
-                for place in self.places(layout(b), row0):
+                for index, place in enumerate(self.places(layout(b), row0)):
                     segment, u, _, _, totals0, _ = place
                     table = segment.table + u
                     kind = self.kind(table)
@@ -355,7 +383,9 @@
                     for h in range(2):
                         _, value = self.value(source, place, h, coefficients, firsts)
                         row = pl.multiple_of(totals0 + u * self.plane + h * self.rows, 8)
-                        so_far = self.acc[pl.ds(row, ROWS), :]
+                        so_far = (self.acc if more is None else more)[pl.ds(row, ROWS), :]
+                        if more is not None and not fresh[index]:
+                            so_far = so_far + self.acc[pl.ds(row, ROWS), :]
                         totals = so_far + value * weight_totals
                         mass = mass + totals
                         hit = hit + totals * (1.0 - self.mask(kind, h, row0, ROWS))
@@ -396,8 +426,7 @@
     lax.fori_loop(0, count // size, several, 0)
 
 
-def sends_kernel(axis, dim, source, *refs):
-    first, second, stage, sems = refs[-4:]
+def start_sends(axis, dim, source, stage, sems):
     odd = lax.axis_index(axis) & 1
     last = source.shape[dim] - HALO
     copies = []
@@ -405,16 +434,25 @@
         at = pl.ds(pl.multiple_of(start, HALO), HALO)
         piece = source.at[at] if dim == 0 else source.at[:, at]
         copies.append(pltpu.make_async_copy(piece, stage.at[i], sems.at[i]))
-    copy_all(copies)
-    outs = []
-    for i, out in enumerate((first, second)):
-        copies[i].wait()
-        outs.append(pltpu.make_async_copy(stage.at[i], out, sems.at[2 + i]))
-        outs[-1].start()
-    wait_all(outs)
-
-
-def corners_kernel(first_in, second_in, itab, first, second):
+    return copy_all(copies)
+
+
+def finish_sends(loads, stage, outs, sems):
+    stores = []
+    for i, out in enumerate(outs):
+        loads[i].wait()
+        stores.append(pltpu.make_async_copy(stage.at[i], out, sems.at[2 + i]))
+        stores[-1].start()
+    return stores
+
+
+def sends_kernel(axis, dim, source, *refs):
+    first, second, stage, sems = refs[-4:]
+    loads = start_sends(axis, dim, source, stage, sems)
+    wait_all(finish_sends(loads, stage, (first, second), sems))
+
+
+def corners_kernel(first_in, second_in, offsets, first, second):
     odd = lax.axis_index("gx") & 1
     last = first_in.shape[0] - HALO
     swapped = (lax.axis_index("gy") & 1) == 0
@@ -427,7 +465,7 @@
 
 def interior_kernel(
     dims,
-    density, first_side, second_side, stay_all, weights, free, itab, ftab,
+    density, first_side, second_side, stay_all, weights, free, offsets, series, firsts, kinds,
     occupancy, q_edges, p_edges, acc_edges, sums,
     p, acc, q0, q1, stay, block, staged, sem_in, sem_stay, sem_edges, sem_out,
 ):
@@ -438,7 +476,7 @@
     chunks = block_first // chunk
     even = (lax.axis_index("gy") & 1) == 0
     lattice = Lattice(
-        rows, 0, itab, ftab, block_first + 2 * HALO, weights, free, stay, p, acc, block_first
+        rows, 0, (offsets, series, firsts, kinds), weights, free, stay, p, acc, block_first
     )
     loads = copy_all(
         [
@@ -537,9 +575,9 @@
 def edges_kernel(
     dims, devices,
     first_halo, second_halo, first_corner, second_corner, stay_all, q_edges, p_edges, acc_edges, sums_in,
-    weights, free, itab, ftab, occupancy_in,
+    weights, free, offsets, series, firsts, kinds, occupancy_in,
     occupancy, row_out,
-    p, acc, q0, q1, q2, q3, stay, staged, sem_q, sem_p, sem_other, sem_out,
+    p, acc, q0, q1, q2, q3, stay, earlier, staged, sem_q, sem_p, sem_other, sem_out,
 ):
     block_first, block_second, _, _ = dims
     rows = block_second + 2 * HALO
@@ -547,9 +585,9 @@
     q = (q0, q1, q2, q3)
     right_table = block_first - 2
     lattice = Lattice(
-        rows, 1, itab, ftab, block_first + 2 * HALO, weights, free, stay, p, acc, 2 * SIDE_MOVED
-    )
-    early, imports = [], []
+        rows, 1, (offsets, series, firsts, kinds), weights, free, stay, p, acc, 2 * SIDE_MOVED
+    )
+    early, late, imports = [], [], []
     p_imports = [[] for _ in range(STEPS)]
     for side in range(2):
         first = 2
@@ -560,10 +598,10 @@
                 sem_other.at[side],
             )
         )
-        early.append(
+        late.append(
             pltpu.make_async_copy(
                 acc_edges.at[side],
-                acc.at[pl.ds(side * HALO * plane, HALO * plane)],
+                earlier.at[pl.ds(side * HALO * plane, HALO * plane)],
                 sem_other.at[2 + side],
             )
         )
@@ -591,6 +629,7 @@
     copy_all(p_imports[0])
     for k in range(1, STEPS):
         copy_all(imports[k] + p_imports[k])
+    copy_all(late)
     spread = parity_matrix(False)
     even = (lax.axis_index("gx") & 1) == 0
     for side in range(2):
@@ -626,10 +665,14 @@
 
     for k in range(1, STEPS):
         wait_all(imports[k - 1] + p_imports[k - 1])
-        own = [u >= HALO - 2 * k for u in range(HALO)] + [u < 2 * k for u in range(HALO)]
+        own = [
+            None if u < HALO - 2 * k else "new" if u >= HALO - 2 else "add" for u in range(HALO)
+        ]
+        own += own[::-1]
         lattice.advance(k, q[k - 1], q[k], 1, layout_of(k), own)
-    wait_all(imports[STEPS - 1] + p_imports[STEPS - 1])
-    mass, hit = lattice.finish(q[STEPS - 1], 1, layout_of(STEPS))
+    wait_all(imports[STEPS - 1] + p_imports[STEPS - 1] + late)
+    fresh = [u >= HALO - 2 for u in range(HALO)]
+    mass, hit = lattice.finish(q[STEPS - 1], 1, layout_of(STEPS), earlier, fresh + fresh[::-1])
     gather = parity_matrix(True)
     outs = []
     for side in range(2):
@@ -679,8 +722,7 @@
     vmem = pl.BlockSpec(memory_space=pltpu.VMEM)
     hbm = pl.BlockSpec(memory_space=pl.ANY)
     params = pltpu.CompilerParams(vmem_limit_bytes=VMEM_LIMIT)
-    chunk = largest_divisor(layers, 8)
-
+    light = pl.CostEstimate(flops=1000, bytes_accessed=1000, transcendentals=0)
     def sends(axis, dim, *after):
         shape = tuple(HALO if d == dim else size for d, size in enumerate(density.shape))
         return pl.pallas_call(
@@ -690,6 +732,7 @@
             out_specs=(hbm, hbm),
             scratch_shapes=[pltpu.VMEM((2,) + shape, f32), pltpu.SemaphoreType.DMA((4,))],
             compiler_params=params,
+            cost_estimate=light,
             name="sends",
         )(density, *after)
 
@@ -697,29 +740,29 @@
     first_side, second_side = exchange(side_sends, "gy", count_second)
     first_halo, second_halo = exchange(sends("gx", 0, side_sends[0]), "gx", count_first)
 
-    stay, weights, free, itab, ftab = pl.pallas_call(
+    table_rows = -(-(layers + 2 * ABOVE) // 8) * 8
+    stay, weights, free, *tables = pl.pallas_call(
         functools.partial(tables_kernel, dims),
-        grid=(layers // chunk,),
         out_shape=(
-            jax.ShapeDtypeStruct((layers, 2, rows, LANES), f32),
+            jax.ShapeDtypeStruct((layers * plane, LANES), f32),
             jax.ShapeDtypeStruct((12 * rows, LANES), f32),
             jax.ShapeDtypeStruct((6 * rows, LANES), f32),
-            jax.ShapeDtypeStruct((KINDS + layers + 4,), jnp.int32),
-            jax.ShapeDtypeStruct(((layers + 4) * REACTIONS + 8,), f32),
+            jax.ShapeDtypeStruct((24,), jnp.int32),
+            jax.ShapeDtypeStruct((STEPS + 2,), f32),
+            jax.ShapeDtypeStruct((table_rows, LANES), f32),
+            jax.ShapeDtypeStruct((table_rows, LANES), jnp.int32),
         ),
         in_specs=[smem] * 4,
-        out_specs=(
-            pl.BlockSpec((chunk, 2, rows, LANES), lambda i: (i, 0, 0, 0)),
-            pl.BlockSpec((12 * rows, LANES), lambda i: (0, 0)),
-            pl.BlockSpec((6 * rows, LANES), lambda i: (0, 0)),
-            smem,
-            smem,
-        ),
-        scratch_shapes=[pltpu.VMEM((12 * rows, LANES), f32)],
+        out_specs=(hbm, vmem, vmem, smem, smem, vmem, vmem),
+        scratch_shapes=[
+            pltpu.VMEM((layers * plane, LANES), f32),
+            pltpu.SemaphoreType.DMA((layers // largest_divisor(layers, 8),)),
+        ],
         compiler_params=params,
+        cost_estimate=light,
         name="tables",
-    )(reaction_rates, state_changes, target_box, truncation)
-    stay = stay.reshape(layers * plane, LANES)
+    )(reaction_rates, state_changes.T, target_box, truncation)
+    offsets = tables[0]
 
     corner = jax.ShapeDtypeStruct((HALO, 2 * HALO, species_third), f32)
     corner_sends = pl.pallas_call(
@@ -728,8 +771,9 @@
         in_specs=[vmem, vmem, smem],
         out_specs=(vmem, vmem),
         compiler_params=params,
+        cost_estimate=light,
         name="corners",
-    )(first_side, second_side, itab)
+    )(first_side, second_side, offsets)
     first_corner, second_corner = exchange(corner_sends, "gx", count_first)
 
     def scratch(own, totals, moved, steps):
@@ -749,7 +793,7 @@
             jax.ShapeDtypeStruct((2, HALO * plane, LANES), f32),
             jax.ShapeDtypeStruct((2 * ROWS, LANES), f32),
         ),
-        in_specs=[hbm, vmem, vmem, hbm, vmem, vmem, smem, smem],
+        in_specs=[hbm, vmem, vmem, hbm, vmem, vmem] + [smem] * 4,
         out_specs=(hbm, hbm, hbm, hbm, vmem),
         scratch_shapes=scratch(block_first, block_first, block_first, 2)
         + [
@@ -761,9 +805,9 @@
             pltpu.SemaphoreType.DMA,
         ],
         compiler_params=params,
-        cost_estimate=pl.CostEstimate(flops=400_000_000, bytes_accessed=40_000_000, transcendentals=0),
+        cost_estimate=light,
         name="interior",
-    )(density, first_side, second_side, stay, weights, free, itab, ftab)
+    )(density, first_side, second_side, stay, weights, free, *tables)
 
     occupancy, row = pl.pallas_call(
         functools.partial(edges_kernel, dims, devices),
@@ -771,22 +815,23 @@
             jax.ShapeDtypeStruct(density.shape, f32),
             jax.ShapeDtypeStruct((devices, LANES), f32),
         ),
-        in_specs=[vmem] * 4 + [hbm] * 4 + [vmem] * 3 + [smem] * 2 + [hbm],
+        in_specs=[vmem] * 4 + [hbm] * 4 + [vmem] * 3 + [smem] * 4 + [hbm],
         out_specs=(hbm, vmem),
         scratch_shapes=scratch(2 * SIDE, 2 * HALO, 2 * SIDE_MOVED, STEPS)
         + [
+            pltpu.VMEM((2 * HALO * plane, LANES), f32),
             pltpu.VMEM((2 * HALO, block_second, species_third), f32),
             pltpu.SemaphoreType.DMA((24,)),
             pltpu.SemaphoreType.DMA((8,)),
             pltpu.SemaphoreType.DMA((4,)),
             pltpu.SemaphoreType.DMA((2,)),
         ],
-        input_output_aliases={13: 0},
+        input_output_aliases={15: 0},
         compiler_params=params,
         name="edges",
     )(
         first_halo, second_halo, first_corner, second_corner, stay, q_edges, p_edges, acc_edges, sums,
-        weights, free, itab, ftab, occupancy,
+        weights, free, *tables, occupancy,
     )
     rows_in = lax.all_to_all(row, ("gx", "gy"), 0, 0, tiled=True)
     summary = jnp.sum(rows_in[:, :2], axis=0) * (1.0 / math.prod(extents))

time: 98.7 us -> 91.1 us (0.923)
  Pallas kernels: 71 us -> 63.5 us
    pallas_call x1, Pallas kernels: 10.2 us -> 5.85 us  [body(): pl.pallas_call(functools.partial(tables_kernel, dims), out_shape=(jax.Sha...]
    pallas_call x1, Pallas kernels: 25.5 us -> 23.7 us  [body(): pl.pallas_call(functools.partial(edges_kernel, dims, devices), out_shape=...]
    pallas_call x1, Pallas kernels: 29.2 us -> 27.8 us  [body(): pl.pallas_call(functools.partial(interior_kernel, dims), out_shape=(jax.S...]
    unnamed x15 -> x12, local copies, waits for them, and re-layouts: 2.48 us -> 1.68 us
  transfers between devices with their start and end apart: 6 -> 6, of which waited for: 0 -> 1; matrix products, arithmetic and copies ran while one was open for 1% -> 0% of each run, Pallas kernels for 42% -> 39%
where the time goes in v3:
time: 91.1 us; the launch traced here: 90.7 us
  Pallas kernels  63.5 us (70%)
  blocking collectives  13.8 us (15%)
  starting transfers between devices  10 us (11%)
  local copies, waits for them, and re-layouts  1.68 us (2%)
    pallas_call x1, Pallas kernels, body(): pl.pallas_call(functools.partial(interior_kernel, dims), out_shape=(jax.S...  27.8 us
    pallas_call x1, Pallas kernels, body(): pl.pallas_call(functools.partial(edges_kernel, dims, devices), out_shape=...  23.7 us
    all_to_all x1, blocking collectives, body(): rows_in = lax.all_to_all(row, ('gx', 'gy'), 0, 0, tiled=True)  13.8 us
    ppermute x6, starting transfers between devices, exchange(): lax.ppermute(piece, axis, pairs + [(j, i) for i, j in pairs])  10 us
    pallas_call x1, Pallas kernels, body(): pl.pallas_call(functools.partial(tables_kernel, dims), out_shape=(jax.Sha...  5.85 us
    pallas_call x2, Pallas kernels, sends(): pl.pallas_call(functools.partial(sends_kernel, axis, dim), out_shape=(jax...  4.39 us
  transfers between devices with their start and end apart: 6, of which 1 were waited for; matrix products, arithmetic and copies ran while one was open for 0% of the time, Pallas kernels for 39%

profile of v3, /device:TPU:0, one launch (start us, length us, event | category | flops | bytes accessed | tf_op | source)
XLA Modules:
  0.0 90.7 jit_solution(12870548223841912802)
XLA Ops:
  0.6 1.8 %sends.2 = (f32[32,8,256]{2,1,0:T(8,128)}, f32[32,8,256]{2,1,0:T(8,128)}) custom-call(f32[32,128,256]{2,1,0:T(8,128)} %density.1), custom_call_target="tpu_custom_call" | custom-call | flops 1000 | bytes 1000 | tf_op jit(solution)/shard_map/sends/pallas_call | solution.py:728
  2.4 0.0 copy-start.3
  2.4 2.6 %sends.3 = (f32[8,128,256]{2,1,0:T(8,128)}, f32[8,128,256]{2,1,0:T(8,128)}) custom-call(f32[32,128,256]{2,1,0:T(8,128)} %density.1, f32[32,8,256]{2,1,0:T(8,128)} %get-tuple-element.22.refs_0_), custom_call_target="tpu_custom_call" | custom-call | flops 1000 | bytes 1000 | tf_op jit(solution)/shard_map/sends/pallas_call | solution.py:728
  5.0 0.5 collective-permute-start
  5.6 1.6 %collective-permute-start.1 = (f32[8,128,256]{2,1,0:T(8,128)}, f32[8,128,256]{2,1,0:T(8,128)}, u32[]{:S(2)}, u32[]{:S(2)}) collective-permute-start(f32[8,128,256]{2,1,0:T(8,128)} %get-tuple-element.24), channel_id=1, source_target_pairs={{4,8},{12,16},{20,24},{8,4},{16,12},{24,20},{5,9},{13,17},{21,25},... | collective-permute-start | bytes 3145736 | tf_op jit(solution)/shard_map/ppermute | solution.py:717
  7.2 0.7 collective-permute-start.3
  7.9 0.0 copy-done.3
  7.9 5.5 %collective-permute-start.2 = (f32[32,8,256]{2,1,0:T(8,128)S(1)}, f32[32,8,256]{2,1,0:T(8,128)S(1)}, u32[]{:S(2)}, u32[]{:S(2)}) collective-permute-start(f32[32,8,256]{2,1,0:T(8,128)S(1)} %copy-done.3), channel_id=1, source_target_pairs={{0,1},{2,3},{1,0},{3,2},{4,5},{6,7},{5,4},{7,6},{8,9},{10,11},{9,8... | collective-permute-start | bytes 786440 | tf_op jit(solution)/shard_map/ppermute | solution.py:717
  13.3 5.8 %tables.1 = (f32[13824,128]{1,0:T(8,128)}, f32[1728,128]{1,0:T(8,128)}, f32[864,128]{1,0:T(8,128)}, s32[24]{0:T(128)}, f32[6]{0:T(128)}, /*index=5*/f32[56,128]{1,0:T(8,128)}, s32[56,128]{1,0:T(8,128)}) custom-call(f32[6]{0:T(128)} %rates.1, s32[3,6]{1,0:T(4,128)} %bitcast.7, s32[2,3]{1,0:T(2,128)} %box.1, s32[2]{0:T(128)} %truncation.1), custom_call_target="tpu_custom_call" | custom-call | flops 1000 | bytes 1000 | tf_op jit(solution)/shard_map/tables/pallas_call | solution.py:744
  19.2 0.0 collective-permute-done.3.second_in.second_side
  19.2 0.0 copy-start.1
  19.2 0.4 collective-permute-done.2.first_in.first_side
  19.6 0.0 copy-start.2
  19.6 0.3 copy-done.1
  19.9 0.4 copy-done.2
  20.3 1.8 %corners.1 = (f32[8,16,256]{2,1,0:T(8,128)}, f32[8,16,256]{2,1,0:T(8,128)}) custom-call(f32[32,8,256]{2,1,0:T(8,128)} %copy-done.2, f32[32,8,256]{2,1,0:T(8,128)} %copy-done.1, s32[24]{0:T(128)} %get-tuple-element.26.offsets), custom_call_target="tpu_custom_call" | custom-call | flops 1000 | bytes 1000 | tf_op jit(solution)/shard_map/corners/pallas_call | solution.py:768
  22.0 1.1 %collective-permute-start.4 = (f32[8,16,256]{2,1,0:T(8,128)}, f32[8,16,256]{2,1,0:T(8,128)S(1)}, u32[]{:S(2)}, u32[]{:S(2)}) collective-permute-start(f32[8,16,256]{2,1,0:T(8,128)} %get-tuple-element.27), channel_id=1, source_target_pairs={{0,4},{8,12},{16,20},{24,28},{4,0},{12,8},{20,16},{28,24},{1,5},{9... | collective-permute-start | bytes 393224 | tf_op jit(solution)/shard_map/ppermute | solution.py:717
  23.1 0.7 collective-permute-start.5
  23.8 27.8 %interior.1 = (f32[32,128,256]{2,1,0:T(8,128)}, f32[4,2,3,1152,128]{4,3,2,1,0:T(8,128)}, f32[4,2,576,128]{3,2,1,0:T(8,128)}, f32[2,2304,128]{2,1,0:T(8,128)}, f32[32,128]{1,0:T(8,128)}) custom-call(f32[32,128,256]{2,1,0:T(8,128)} %density.1, f32[32,8,256]{2,1,0:T(8,128)} %copy-done.2, f32[32,8,256]{2,1,0:T(8,128)} %copy-done.1, ...), custom_call_target="tpu_custom_call" | custom-call | flops 1000 | bytes 1000 | tf_op jit(solution)/shard_map/interior/pallas_call | solution.py:787
  51.6 0.0 collective-permute-done.4.first_corner
  51.6 0.0 copy-start.4
  51.6 0.0 collective-permute-done.5.second_corner
  51.6 0.0 copy-start.5
  51.6 0.0 collective-permute-done.first_halo
  51.6 0.0 copy-start
  51.6 0.0 collective-permute-done.1.second_halo
  51.7 0.6 copy-done.4
  52.2 0.0 copy-done.5
  52.3 0.4 copy-done
  52.6 23.7 %edges.1 = (f32[32,128,256]{2,1,0:T(8,128)}, f32[32,128]{1,0:T(8,128)}) custom-call(f32[8,128,256]{2,1,0:T(8,128)} %copy-done, f32[8,128,256]{2,1,0:T(8,128)} %collective-permute-done.1.second_halo, f32[8,16,256]{2,1,0:T(8,128)} %copy-done.4, f32[8,16,256]{2,1,0:T(8,128)} %copy-done.5, ...), custom_call_target="tpu_custom_call", output_to_operand_aliasing={{0}: (15, {})} | custom-call | tf_op jit(solution)/shard_map/edges/pallas_call | solution.py:812
  76.4 13.8 %all_to_all.12 = f32[32,1,128]{2,1,0:T(1,128)S(1)} all-to-all(f32[32,1,128]{2,1,0:T(1,128)} %bitcast.6), channel_id=1, replica_groups=mesh['gx'=8,'gy'=4] {'gx','gy'}, dimensions={0} | all-to-all | bytes 32768 | tf_op jit(solution)/shard_map/all_to_all | solution.py:836
  90.2 0.5 broadcast_multiply_fusion
  (1 shorter events, 0.0 us)
Async XLA Ops:
  2.4 5.4 %copy-start.3 = (f32[32,8,256]{2,1,0:T(8,128)S(1)}, f32[32,8,256]{2,1,0:T(8,128)}, u32[]{:S(2)}) copy-start(f32[32,8,256]{2,1,0:T(8,128)} %get-tuple-element.22.refs_0_) | copy-start | bytes 786436
  5.0 46.6 %collective-permute-start = (f32[8,128,256]{2,1,0:T(8,128)}, f32[8,128,256]{2,1,0:T(8,128)S(1)}, u32[]{:S(2)}, u32[]{:S(2)}) collective-permute-start(f32[8,128,256]{2,1,0:T(8,128)} %get-tuple-element.23), channel_id=1, source_target_pairs={{0,4},{8,12},{16,20},{24,28},{4,0},{12,8},{20,16},{28,24},{1,5},{9... | collective-permute-start | bytes 3145736 | tf_op jit(solution)/shard_map/ppermute | solution.py:717
  5.6 46.1 %collective-permute-start.1 = (f32[8,128,256]{2,1,0:T(8,128)}, f32[8,128,256]{2,1,0:T(8,128)}, u32[]{:S(2)}, u32[]{:S(2)}) collective-permute-start(f32[8,128,256]{2,1,0:T(8,128)} %get-tuple-element.24), channel_id=1, source_target_pairs={{4,8},{12,16},{20,24},{8,4},{16,12},{24,20},{5,9},{13,17},{21,25},... | collective-permute-start | bytes 3145736 | tf_op jit(solution)/shard_map/ppermute | solution.py:717
  7.2 12.0 %collective-permute-start.3 = (f32[32,8,256]{2,1,0:T(8,128)}, f32[32,8,256]{2,1,0:T(8,128)S(1)}, u32[]{:S(2)}, u32[]{:S(2)}) collective-permute-start(f32[32,8,256]{2,1,0:T(8,128)} %get-tuple-element.25), channel_id=1, source_target_pairs={{1,2},{2,1},{5,6},{6,5},{9,10},{10,9},{13,14},{14,13},{17,18},{18,... | collective-permute-start | bytes 786440 | tf_op jit(solution)/shard_map/ppermute | solution.py:717
  7.9 11.7 %collective-permute-start.2 = (f32[32,8,256]{2,1,0:T(8,128)S(1)}, f32[32,8,256]{2,1,0:T(8,128)S(1)}, u32[]{:S(2)}, u32[]{:S(2)}) collective-permute-start(f32[32,8,256]{2,1,0:T(8,128)S(1)} %copy-done.3), channel_id=1, source_target_pairs={{0,1},{2,3},{1,0},{3,2},{4,5},{6,7},{5,4},{7,6},{8,9},{10,11},{9,8... | collective-permute-start | bytes 786440 | tf_op jit(solution)/shard_map/ppermute | solution.py:717
  19.2 0.7 copy-start.1
  19.6 0.7 copy-start.2
  22.0 29.5 %collective-permute-start.4 = (f32[8,16,256]{2,1,0:T(8,128)}, f32[8,16,256]{2,1,0:T(8,128)S(1)}, u32[]{:S(2)}, u32[]{:S(2)}) collective-permute-start(f32[8,16,256]{2,1,0:T(8,128)} %get-tuple-element.27), channel_id=1, source_target_pairs={{0,4},{8,12},{16,20},{24,28},{4,0},{12,8},{20,16},{28,24},{1,5},{9... | collective-permute-start | bytes 393224 | tf_op jit(solution)/shard_map/ppermute | solution.py:717
  23.1 28.5 %collective-permute-start.5 = (f32[8,16,256]{2,1,0:T(8,128)}, f32[8,16,256]{2,1,0:T(8,128)S(1)}, u32[]{:S(2)}, u32[]{:S(2)}) collective-permute-start(f32[8,16,256]{2,1,0:T(8,128)} %get-tuple-element.28), channel_id=1, source_target_pairs={{4,8},{12,16},{20,24},{8,4},{16,12},{24,20},{5,9},{13,17},{21,25},... | collective-permute-start | bytes 393224 | tf_op jit(solution)/shard_map/ppermute | solution.py:717
  51.6 0.6 copy-start.4
  51.6 0.7 copy-start.5
  51.6 1.0 %copy-start = (f32[8,128,256]{2,1,0:T(8,128)}, f32[8,128,256]{2,1,0:T(8,128)S(1)}, u32[]{:S(2)}) copy-start(f32[8,128,256]{2,1,0:T(8,128)S(1)} %collective-permute-done.first_halo) | copy-start | bytes 3145732

commit v4 on v3

--- a/solution.py
+++ b/solution.py
@@ -14,7 +14,7 @@
 LANES = 128
 ROWS = 16
 PAD = 8
-BODY_LAYERS = 14
+BODY_LAYERS = 28
 
 mean_jumps = 8.0
 headroom = 1.05
@@ -48,8 +48,21 @@
     anchor_first = lax.axis_index("gx") * block_first - HALO
     anchor_second = lax.axis_index("gy") * block_second - HALO
 
+    plain = jnp.int32(REACTIONS - 1)
+    for r in range(REACTIONS - 2, -1, -1):
+        plain = jnp.where(changes[0, r] == 2, r, plain)
+
+    def reaction_of(r):
+        return jnp.where(r == 0, plain, jnp.where(r == plain, 0, r))
+
+    def change(d, r):
+        return changes[d, reaction_of(r)]
+
+    def rate(r):
+        return rates[reaction_of(r)]
+
     def order(r, d):
-        return jnp.maximum(-changes[d, r], 0)
+        return jnp.maximum(-change(d, r), 0)
 
     def by_reaction(index, value, copies=1):
         found = jnp.zeros(index.shape, jnp.float32)
@@ -65,7 +78,7 @@
 
     corner = jnp.float32(0.0)
     for r in range(REACTIONS):
-        term = rates[r]
+        term = rate(r)
         for d in range(3):
             e = float(extents[d])
             s = order(r, d)
@@ -95,7 +108,7 @@
             orders_by_reaction(split_lane, 1, copies),
             float(extents[1]),
         )
-        * by_reaction(split_lane, lambda r: rates[r], copies)
+        * by_reaction(split_lane, lambda r: rate(r), copies)
         * inverse,
         0.0,
     )
@@ -144,11 +157,11 @@
         third = 2 * lane + h
 
         def coefficient(r, carry, h=h, third=third):
-            from_row = row - changes[1, r]
-            from_third = third - changes[2, r]
+            from_row = row - change(1, r)
+            from_third = third - change(2, r)
             moved = (
                 inverse
-                * rates[r]
+                * rate(r)
                 * counts_factor(from_row.astype(jnp.float32), order(r, 1), float(extents[1]))
                 * counts_factor(from_third.astype(jnp.float32), order(r, 2), float(extents[2]))
             )
@@ -161,18 +174,18 @@
     for which in range(2):
         for r in range(REACTIONS):
             for h in range(2):
-                source = h - changes[2, r]
+                source = h - change(2, r)
                 offsets[which * 12 + r * 2 + h] = (
                     PAD
-                    + (((source >> 1) + 1) * kernel_layers[which] - changes[0, r]) * plane
+                    + (((source >> 1) + 1) * kernel_layers[which] - change(0, r)) * plane
                     + (source & 1) * rows
-                    - changes[1, r]
+                    - change(1, r)
                 )
-    n0 = lax.broadcasted_iota(jnp.int32, firsts.shape, 0) + (anchor_first - ABOVE)
-    reaction = lax.broadcasted_iota(jnp.int32, firsts.shape, 1)
-    change = by_reaction(reaction, lambda r: changes[0, r].astype(jnp.float32))
+    n0 = lax.broadcasted_iota(jnp.int32, firsts.shape, 1) + (anchor_first - ABOVE)
+    reaction = lax.broadcasted_iota(jnp.int32, firsts.shape, 0)
+    moves = by_reaction(reaction, lambda r: change(0, r).astype(jnp.float32))
     firsts[...] = counts_factor(
-        n0.astype(jnp.float32) - change, orders_by_reaction(reaction, 0, 1), float(extents[0])
+        n0.astype(jnp.float32) - moves, orders_by_reaction(reaction, 0, 1), float(extents[0])
     )
     real = (n0 >= 0) & (n0 < extents[0])
     in_box = (n0 >= box[0, 0]) & (n0 < box[1, 0])
@@ -224,10 +237,10 @@
         return PAD + (turn + 1) * self.moved_layers * self.plane + row
 
     def kind(self, table):
-        return self.kinds[ABOVE + table, 0]
+        return self.kinds[0, ABOVE + table]
 
     def first(self, table, r):
-        return self.firsts[ABOVE + table, r]
+        return self.firsts[r, ABOVE + table]
 
     def mask(self, kind, h, row0, count):
         at = pl.multiple_of(kind * self.plane + h * self.rows + row0, 8)
@@ -283,7 +296,8 @@
         terms = [value]
         for r in range(REACTIONS):
             arriving = source[pl.ds(sources[r][h] + u * self.plane, ROWS), :]
-            terms.append(arriving * coefficients[r][h] * firsts[r])
+            term = arriving * coefficients[r][h]
+            terms.append(term if r == 0 else term * firsts[r])
         while len(terms) > 1:
             pairs = [terms[i : i + 2] for i in range(0, len(terms), 2)]
             terms = [pair[0] + pair[1] if len(pair) == 2 else pair[0] for pair in pairs]
@@ -328,7 +342,7 @@
                     segment, u, own, target0, totals0, _ = place
                     table = segment.table + u
                     kind = self.kind(table)
-                    firsts = [self.first(table, r) for r in range(REACTIONS)]
+                    firsts = [None] + [self.first(table, r) for r in range(1, REACTIONS)]
                     ready = -1
                     if index >= lag:
                         ready = ((index - lag + 1) * size + size - lag - 1) // (size - lag) - 1
@@ -379,7 +393,7 @@
                     segment, u, _, _, totals0, _ = place
                     table = segment.table + u
                     kind = self.kind(table)
-                    firsts = [self.first(table, r) for r in range(REACTIONS)]
+                    firsts = [None] + [self.first(table, r) for r in range(1, REACTIONS)]
                     for h in range(2):
                         _, value = self.value(source, place, h, coefficients, firsts)
                         row = pl.multiple_of(totals0 + u * self.plane + h * self.rows, 8)
@@ -426,30 +440,25 @@
     lax.fori_loop(0, count // size, several, 0)
 
 
-def start_sends(axis, dim, source, stage, sems):
-    odd = lax.axis_index(axis) & 1
-    last = source.shape[dim] - HALO
-    copies = []
-    for i, start in enumerate(((1 - odd) * last, odd * last)):
-        at = pl.ds(pl.multiple_of(start, HALO), HALO)
-        piece = source.at[at] if dim == 0 else source.at[:, at]
-        copies.append(pltpu.make_async_copy(piece, stage.at[i], sems.at[i]))
-    return copy_all(copies)
-
-
-def finish_sends(loads, stage, outs, sems):
-    stores = []
-    for i, out in enumerate(outs):
-        loads[i].wait()
-        stores.append(pltpu.make_async_copy(stage.at[i], out, sems.at[2 + i]))
-        stores[-1].start()
-    return stores
-
-
-def sends_kernel(axis, dim, source, *refs):
-    first, second, stage, sems = refs[-4:]
-    loads = start_sends(axis, dim, source, stage, sems)
-    wait_all(finish_sends(loads, stage, (first, second), sems))
+def sends_kernel(source, *refs):
+    outs, stages, sems = refs[:4], refs[4:6], refs[6]
+    loads, stores = [], []
+    for j, (axis, dim) in enumerate((("gy", 1), ("gx", 0))):
+        odd = lax.axis_index(axis) & 1
+        last = source.shape[dim] - HALO
+        for i, start in enumerate(((1 - odd) * last, odd * last)):
+            at = pl.ds(pl.multiple_of(start, HALO), HALO)
+            piece = source.at[at] if dim == 0 else source.at[:, at]
+            loads.append(pltpu.make_async_copy(piece, stages[j].at[i], sems.at[2 * j + i]))
+    copy_all(loads)
+    for j in range(2):
+        for i in range(2):
+            loads[2 * j + i].wait()
+            stores.append(
+                pltpu.make_async_copy(stages[j].at[i], outs[2 * j + i], sems.at[4 + 2 * j + i])
+            )
+            stores[-1].start()
+    wait_all(stores)
 
 
 def corners_kernel(first_in, second_in, offsets, first, second):
@@ -465,9 +474,9 @@
 
 def interior_kernel(
     dims,
-    density, first_side, second_side, stay_all, weights, free, offsets, series, firsts, kinds,
+    density, first_side, second_side, stay_all, weights_all, free, offsets, series, firsts, kinds,
     occupancy, q_edges, p_edges, acc_edges, sums,
-    p, acc, q0, q1, stay, block, staged, sem_in, sem_stay, sem_edges, sem_out,
+    p, acc, q0, q1, stay, block, staged, sem_in, sem_late, weights, sem_edges, sem_out,
 ):
     block_first, block_second, _, _ = dims
     rows = block_second + 2 * HALO
@@ -478,18 +487,20 @@
     lattice = Lattice(
         rows, 0, (offsets, series, firsts, kinds), weights, free, stay, p, acc, block_first
     )
-    loads = copy_all(
-        [
-            pltpu.make_async_copy(
-                density.at[pl.ds(c * chunk, chunk)], block.at[pl.ds(c * chunk, chunk)], sem_in.at[c]
-            )
-            for c in range(chunks)
-        ]
-    )
-    stay_copy = pltpu.make_async_copy(
-        stay_all.at[pl.ds(HALO * plane, block_first * plane)], stay, sem_stay
-    )
-    stay_copy.start()
+    loads = [
+        pltpu.make_async_copy(
+            density.at[pl.ds(c * chunk, chunk)], block.at[pl.ds(c * chunk, chunk)], sem_in.at[c]
+        )
+        for c in range(chunks)
+    ]
+    copy_all(loads)
+    late = [
+        pltpu.make_async_copy(
+            stay_all.at[pl.ds(HALO * plane, block_first * plane)], stay, sem_late.at[0]
+        ),
+        pltpu.make_async_copy(weights_all, weights, sem_late.at[1]),
+    ]
+    copy_all(late)
     spread = parity_matrix(False)
     for c in range(chunks):
         loads[c].wait()
@@ -504,8 +515,8 @@
                 q0, split_product(values, spread), local, local + HALO, local, local
             )
 
-        in_groups(chunk, 4, layer)
-    stay_copy.wait()
+        in_groups(chunk, 8, layer)
+    wait_all(late)
 
     edges = []
 
@@ -561,10 +572,21 @@
     sums[pl.ds(0, ROWS), :] = mass
     sums[pl.ds(ROWS, ROWS), :] = hit
     gather = parity_matrix(True)
-    in_groups(inner, 4, lambda i: lattice.restore(HALO + i, staged, i, gather))
-    out = pltpu.make_async_copy(staged, occupancy.at[pl.ds(HALO, inner)], sem_out)
-    out.start()
-    out.wait()
+    outs = []
+    part = largest_divisor(inner, 8)
+    for c in range(inner // part):
+        in_groups(
+            part, 4, lambda i, c=c: lattice.restore(HALO + c * part + i, staged, c * part + i, gather)
+        )
+        outs.append(
+            pltpu.make_async_copy(
+                staged.at[pl.ds(c * part, part)],
+                occupancy.at[pl.ds(HALO + c * part, part)],
+                sem_out.at[c],
+            )
+        )
+        outs[-1].start()
+    wait_all(outs)
     wait_all(edges)
 
 
@@ -575,11 +597,11 @@
 def edges_kernel(
     dims, devices,
     first_halo, second_halo, first_corner, second_corner, stay_all, q_edges, p_edges, acc_edges, sums_in,
-    weights, free, offsets, series, firsts, kinds, occupancy_in,
+    weights_all, free, offsets, series, firsts, kinds, occupancy_in,
     occupancy, row_out,
-    p, acc, q0, q1, q2, q3, stay, earlier, staged, sem_q, sem_p, sem_other, sem_out,
+    p, acc, q0, q1, q2, q3, stay, earlier, weights, staged, sem_q, sem_p, sem_other, sem_out,
 ):
-    block_first, block_second, _, _ = dims
+    block_first, block_second, extents, _ = dims
     rows = block_second + 2 * HALO
     plane = 2 * rows
     q = (q0, q1, q2, q3)
@@ -624,12 +646,8 @@
                         sem_q.at[(k * 2 + side) * 3 + turn + 1],
                     )
                 )
-    copy_all(imports[0])
-    copy_all(early)
-    copy_all(p_imports[0])
-    for k in range(1, STEPS):
-        copy_all(imports[k] + p_imports[k])
-    copy_all(late)
+    early.append(pltpu.make_async_copy(weights_all, weights, sem_other.at[4]))
+    copy_all(imports[0] + early + p_imports[0])
     spread = parity_matrix(False)
     even = (lax.axis_index("gx") & 1) == 0
     for side in range(2):
@@ -665,6 +683,9 @@
 
     for k in range(1, STEPS):
         wait_all(imports[k - 1] + p_imports[k - 1])
+        copy_all(imports[k] + p_imports[k])
+        if k == STEPS - 1:
+            copy_all(late)
         own = [
             None if u < HALO - 2 * k else "new" if u >= HALO - 2 else "add" for u in range(HALO)
         ]
@@ -689,8 +710,9 @@
             )
         )
         outs[-1].start()
-    mass = jnp.sum(mass + sums_in[pl.ds(0, ROWS), :])
-    hit = jnp.sum(hit + sums_in[pl.ds(ROWS, ROWS), :])
+    share = 1.0 / math.prod(extents)
+    mass = jnp.sum(mass + sums_in[pl.ds(0, ROWS), :]) * share
+    hit = jnp.sum(hit + sums_in[pl.ds(ROWS, ROWS), :]) * share
     lane = lax.broadcasted_iota(jnp.int32, (devices, LANES), 1)
     row_out[...] = jnp.where(lane == 0, hit, jnp.where(lane == 1, mass, 0.0))
     wait_all(outs)
@@ -723,24 +745,27 @@
     hbm = pl.BlockSpec(memory_space=pl.ANY)
     params = pltpu.CompilerParams(vmem_limit_bytes=VMEM_LIMIT)
     light = pl.CostEstimate(flops=1000, bytes_accessed=1000, transcendentals=0)
-    def sends(axis, dim, *after):
-        shape = tuple(HALO if d == dim else size for d, size in enumerate(density.shape))
-        return pl.pallas_call(
-            functools.partial(sends_kernel, axis, dim),
-            out_shape=(jax.ShapeDtypeStruct(shape, f32),) * 2,
-            in_specs=[hbm] * (1 + len(after)),
-            out_specs=(hbm, hbm),
-            scratch_shapes=[pltpu.VMEM((2,) + shape, f32), pltpu.SemaphoreType.DMA((4,))],
-            compiler_params=params,
-            cost_estimate=light,
-            name="sends",
-        )(density, *after)
-
-    side_sends = sends("gy", 1)
-    first_side, second_side = exchange(side_sends, "gy", count_second)
-    first_halo, second_halo = exchange(sends("gx", 0, side_sends[0]), "gx", count_first)
-
-    table_rows = -(-(layers + 2 * ABOVE) // 8) * 8
+    side_shape = (block_first, HALO, species_third)
+    halo_shape = (HALO, block_second, species_third)
+    sends = pl.pallas_call(
+        sends_kernel,
+        out_shape=(jax.ShapeDtypeStruct(side_shape, f32),) * 2
+        + (jax.ShapeDtypeStruct(halo_shape, f32),) * 2,
+        in_specs=[hbm],
+        out_specs=(hbm,) * 4,
+        scratch_shapes=[
+            pltpu.VMEM((2,) + side_shape, f32),
+            pltpu.VMEM((2,) + halo_shape, f32),
+            pltpu.SemaphoreType.DMA((8,)),
+        ],
+        compiler_params=params,
+        cost_estimate=light,
+        name="sends",
+    )(density)
+    first_side, second_side = exchange(sends[:2], "gy", count_second)
+    first_halo, second_halo = exchange(sends[2:], "gx", count_first)
+
+    table_lanes = -(-(layers + 2 * ABOVE) // LANES) * LANES
     stay, weights, free, *tables = pl.pallas_call(
         functools.partial(tables_kernel, dims),
         out_shape=(
@@ -749,8 +774,8 @@
             jax.ShapeDtypeStruct((6 * rows, LANES), f32),
             jax.ShapeDtypeStruct((24,), jnp.int32),
             jax.ShapeDtypeStruct((STEPS + 2,), f32),
-            jax.ShapeDtypeStruct((table_rows, LANES), f32),
-            jax.ShapeDtypeStruct((table_rows, LANES), jnp.int32),
+            jax.ShapeDtypeStruct((8, table_lanes), f32),
+            jax.ShapeDtypeStruct((8, table_lanes), jnp.int32),
         ),
         in_specs=[smem] * 4,
         out_specs=(hbm, vmem, vmem, smem, smem, vmem, vmem),
@@ -793,16 +818,17 @@
             jax.ShapeDtypeStruct((2, HALO * plane, LANES), f32),
             jax.ShapeDtypeStruct((2 * ROWS, LANES), f32),
         ),
-        in_specs=[hbm, vmem, vmem, hbm, vmem, vmem] + [smem] * 4,
+        in_specs=[hbm, vmem, vmem, hbm, hbm, vmem] + [smem] * 4,
         out_specs=(hbm, hbm, hbm, hbm, vmem),
         scratch_shapes=scratch(block_first, block_first, block_first, 2)
         + [
             pltpu.VMEM((block_first, block_second, species_third), f32),
             pltpu.VMEM((block_first - 2 * HALO, block_second, species_third), f32),
             pltpu.SemaphoreType.DMA((chunks,)),
-            pltpu.SemaphoreType.DMA,
+            pltpu.SemaphoreType.DMA((2,)),
+            pltpu.VMEM((12 * rows, LANES), f32),
             pltpu.SemaphoreType.DMA((34,)),
-            pltpu.SemaphoreType.DMA,
+            pltpu.SemaphoreType.DMA((block_first // HALO,)),
         ],
         compiler_params=params,
         cost_estimate=light,
@@ -815,15 +841,16 @@
             jax.ShapeDtypeStruct(density.shape, f32),
             jax.ShapeDtypeStruct((devices, LANES), f32),
         ),
-        in_specs=[vmem] * 4 + [hbm] * 4 + [vmem] * 3 + [smem] * 4 + [hbm],
+        in_specs=[vmem] * 4 + [hbm] * 4 + [vmem, hbm, vmem] + [smem] * 4 + [hbm],
         out_specs=(hbm, vmem),
         scratch_shapes=scratch(2 * SIDE, 2 * HALO, 2 * SIDE_MOVED, STEPS)
         + [
             pltpu.VMEM((2 * HALO * plane, LANES), f32),
+            pltpu.VMEM((12 * rows, LANES), f32),
             pltpu.VMEM((2 * HALO, block_second, species_third), f32),
             pltpu.SemaphoreType.DMA((24,)),
             pltpu.SemaphoreType.DMA((8,)),
-            pltpu.SemaphoreType.DMA((4,)),
+            pltpu.SemaphoreType.DMA((5,)),
             pltpu.SemaphoreType.DMA((2,)),
         ],
         input_output_aliases={15: 0},
@@ -834,7 +861,7 @@
         weights, free, *tables, occupancy,
     )
     rows_in = lax.all_to_all(row, ("gx", "gy"), 0, 0, tiled=True)
-    summary = jnp.sum(rows_in[:, :2], axis=0) * (1.0 / math.prod(extents))
+    summary = jnp.sum(rows_in[:, :2], axis=0)
     return occupancy, summary
 
 

time: 91.1 us -> 85.9 us (0.943)
  Pallas kernels: 63.5 us -> 57 us
  blocking collectives: 13.8 us -> 17.5 us
  starting transfers between devices: 10 us -> 7.73 us
    all_to_all x1, blocking collectives: 13.8 us -> 17.5 us  [body(): rows_in = lax.all_to_all(row, ('gx', 'gy'), 0, 0, tiled=True)]
    pallas_call x1, Pallas kernels: 23.7 us -> 20.5 us  [body(): pl.pallas_call(functools.partial(edges_kernel, dims, devices), out_shape=...]
    ppermute x6, starting transfers between devices: 10 us -> 7.73 us  [exchange(): lax.ppermute(piece, axis, pairs + [(j, i) for i, j in pairs])]
    pallas_call x1, Pallas kernels: 27.8 us -> 26 us  [body(): pl.pallas_call(functools.partial(interior_kernel, dims), out_shape=(jax.S...]
    pallas_call x2 -> x1, Pallas kernels: 4.39 us -> 2.8 us  [body(): pl.pallas_call(sends_kernel, out_shape=(jax.ShapeDtypeStruct(side_shape,...]
  transfers between devices with their start and end apart: 6 -> 6, of which waited for: 1 -> 0; matrix products, arithmetic and copies ran while one was open for 0% -> 0% of each run, Pallas kernels for 39% -> 39%
where the time goes in v4:
time: 85.9 us; the launch traced here: 85.3 us
  Pallas kernels  57 us (66%)
  blocking collectives  17.5 us (20%)
  starting transfers between devices  7.73 us (9%)
  local copies, waits for them, and re-layouts  1.78 us (2%)
    pallas_call x1, Pallas kernels, body(): pl.pallas_call(functools.partial(interior_kernel, dims), out_shape=(jax.S...  26 us
    pallas_call x1, Pallas kernels, body(): pl.pallas_call(functools.partial(edges_kernel, dims, devices), out_shape=...  20.5 us
    all_to_all x1, blocking collectives, body(): rows_in = lax.all_to_all(row, ('gx', 'gy'), 0, 0, tiled=True)  17.5 us
    ppermute x6, starting transfers between devices, exchange(): lax.ppermute(piece, axis, pairs + [(j, i) for i, j in pairs])  7.73 us
    pallas_call x1, Pallas kernels, body(): pl.pallas_call(functools.partial(tables_kernel, dims), out_shape=(jax.Sha...  5.95 us
    pallas_call x1, Pallas kernels, body(): pl.pallas_call(sends_kernel, out_shape=(jax.ShapeDtypeStruct(side_shape,...  2.8 us
    unnamed x10, local copies, waits for them, and re-layouts  1.78 us
    pallas_call x1, Pallas kernels, body(): pl.pallas_call(corners_kernel, out_shape=(corner, corner), in_specs=[vmem...  1.76 us
  transfers between devices with their start and end apart: 6, of which 0 were waited for; matrix products, arithmetic and copies ran while one was open for 0% of the time, Pallas kernels for 39%

profile of v4, /device:TPU:0, one launch (start us, length us, event | category | flops | bytes accessed | tf_op | source)
XLA Modules:
  0.0 85.3 jit_solution(15400335884409979306)
XLA Ops:
  0.6 2.8 %sends.1 = (f32[32,8,256]{2,1,0:T(8,128)}, f32[32,8,256]{2,1,0:T(8,128)}, f32[8,128,256]{2,1,0:T(8,128)}, f32[8,128,256]{2,1,0:T(8,128)}) custom-call(f32[32,128,256]{2,1,0:T(8,128)} %density.1), custom_call_target="tpu_custom_call" | custom-call | flops 1000 | bytes 1000 | tf_op jit(solution)/shard_map/sends/pallas_call | solution.py:750
  3.4 0.5 collective-permute-start
  4.0 1.6 %collective-permute-start.1 = (f32[8,128,256]{2,1,0:T(8,128)}, f32[8,128,256]{2,1,0:T(8,128)}, u32[]{:S(2)}, u32[]{:S(2)}) collective-permute-start(f32[8,128,256]{2,1,0:T(8,128)} %get-tuple-element.23), channel_id=1, source_target_pairs={{4,8},{12,16},{20,24},{8,4},{16,12},{24,20},{5,9},{13,17},{21,25},... | collective-permute-start | bytes 3145736 | tf_op jit(solution)/shard_map/ppermute | solution.py:739
  5.6 2.6 %collective-permute-start.2 = (f32[32,8,256]{2,1,0:T(8,128)}, f32[32,8,256]{2,1,0:T(8,128)S(1)}, u32[]{:S(2)}, u32[]{:S(2)}) collective-permute-start(f32[32,8,256]{2,1,0:T(8,128)} %get-tuple-element.24), channel_id=1, source_target_pairs={{0,1},{2,3},{1,0},{3,2},{4,5},{6,7},{5,4},{7,6},{8,9},{10,11},{9,8... | collective-permute-start | bytes 786440 | tf_op jit(solution)/shard_map/ppermute | solution.py:739
  8.2 0.7 collective-permute-start.3
  8.8 5.9 %tables.1 = (f32[13824,128]{1,0:T(8,128)}, f32[1728,128]{1,0:T(8,128)}, f32[864,128]{1,0:T(8,128)}, s32[24]{0:T(128)}, f32[6]{0:T(128)}, /*index=5*/f32[8,128]{1,0:T(8,128)}, s32[8,128]{1,0:T(8,128)}) custom-call(f32[6]{0:T(128)} %rates.1, s32[3,6]{1,0:T(4,128)} %bitcast.7, s32[2,3]{1,0:T(2,128)} %box.1, s32[2]{0:T(128)} %truncation.1), custom_call_target="tpu_custom_call" | custom-call | flops 1000 | bytes 1000 | tf_op jit(solution)/shard_map/tables/pallas_call | solution.py:769
  14.8 0.0 collective-permute-done.2.first_in.first_side
  14.8 0.0 copy-start.1
  14.8 0.0 collective-permute-done.3.second_in.second_side
  14.8 0.0 copy-start.2
  14.8 0.7 copy-done.1
  15.5 0.1 copy-done.2
  15.6 1.8 %corners.1 = (f32[8,16,256]{2,1,0:T(8,128)}, f32[8,16,256]{2,1,0:T(8,128)}) custom-call(f32[32,8,256]{2,1,0:T(8,128)} %copy-done.1, f32[32,8,256]{2,1,0:T(8,128)} %copy-done.2, s32[24]{0:T(128)} %get-tuple-element.26.offsets), custom_call_target="tpu_custom_call" | custom-call | flops 1000 | bytes 1000 | tf_op jit(solution)/shard_map/corners/pallas_call | solution.py:793
  17.4 1.7 %collective-permute-start.4 = (f32[8,16,256]{2,1,0:T(8,128)}, f32[8,16,256]{2,1,0:T(8,128)S(1)}, u32[]{:S(2)}, u32[]{:S(2)}) collective-permute-start(f32[8,16,256]{2,1,0:T(8,128)} %get-tuple-element.27), channel_id=1, source_target_pairs={{0,4},{8,12},{16,20},{24,28},{4,0},{12,8},{20,16},{28,24},{1,5},{9... | collective-permute-start | bytes 393224 | tf_op jit(solution)/shard_map/ppermute | solution.py:739
  19.1 0.7 collective-permute-start.5
  19.7 26.0 %interior.1 = (f32[32,128,256]{2,1,0:T(8,128)}, f32[4,2,3,1152,128]{4,3,2,1,0:T(8,128)}, f32[4,2,576,128]{3,2,1,0:T(8,128)}, f32[2,2304,128]{2,1,0:T(8,128)}, f32[32,128]{1,0:T(8,128)}) custom-call(f32[32,128,256]{2,1,0:T(8,128)} %density.1, f32[32,8,256]{2,1,0:T(8,128)} %copy-done.1, f32[32,8,256]{2,1,0:T(8,128)} %copy-done.2, ...), custom_call_target="tpu_custom_call" | custom-call | flops 1000 | bytes 1000 | tf_op jit(solution)/shard_map/interior/pallas_call | solution.py:812
  45.7 0.0 collective-permute-done.4.first_corner
  45.7 0.0 copy-start.3
  45.7 0.0 collective-permute-done.5.second_corner
  45.7 0.0 copy-start.4
  45.7 0.0 collective-permute-done.first_halo
  45.7 0.0 copy-start
  45.8 0.0 collective-permute-done.1.second_halo
  45.8 0.6 copy-done.3
  46.3 0.1 copy-done.4
  46.4 0.4 copy-done
  46.8 20.5 %edges.1 = (f32[32,128,256]{2,1,0:T(8,128)}, f32[32,128]{1,0:T(8,128)}) custom-call(f32[8,128,256]{2,1,0:T(8,128)} %copy-done, f32[8,128,256]{2,1,0:T(8,128)} %collective-permute-done.1.second_halo, f32[8,16,256]{2,1,0:T(8,128)} %copy-done.3, f32[8,16,256]{2,1,0:T(8,128)} %copy-done.4, ...), custom_call_target="tpu_custom_call", output_to_operand_aliasing={{0}: (15, {})} | custom-call | tf_op jit(solution)/shard_map/edges/pallas_call | solution.py:838
  67.3 17.5 %all_to_all.12 = f32[32,1,128]{2,1,0:T(1,128)S(1)} all-to-all(f32[32,1,128]{2,1,0:T(1,128)} %bitcast.6), channel_id=1, replica_groups=mesh['gx'=8,'gy'=4] {'gx','gy'}, dimensions={0} | all-to-all | bytes 32768 | tf_op jit(solution)/shard_map/all_to_all | solution.py:863
  84.8 0.5 slice_reduce_fusion
Async XLA Ops:
  3.4 42.3 %collective-permute-start = (f32[8,128,256]{2,1,0:T(8,128)}, f32[8,128,256]{2,1,0:T(8,128)S(1)}, u32[]{:S(2)}, u32[]{:S(2)}) collective-permute-start(f32[8,128,256]{2,1,0:T(8,128)} %get-tuple-element.22), channel_id=1, source_target_pairs={{0,4},{8,12},{16,20},{24,28},{4,0},{12,8},{20,16},{28,24},{1,5},{9... | collective-permute-start | bytes 3145736 | tf_op jit(solution)/shard_map/ppermute | solution.py:739
  4.0 41.8 %collective-permute-start.1 = (f32[8,128,256]{2,1,0:T(8,128)}, f32[8,128,256]{2,1,0:T(8,128)}, u32[]{:S(2)}, u32[]{:S(2)}) collective-permute-start(f32[8,128,256]{2,1,0:T(8,128)} %get-tuple-element.23), channel_id=1, source_target_pairs={{4,8},{12,16},{20,24},{8,4},{16,12},{24,20},{5,9},{13,17},{21,25},... | collective-permute-start | bytes 3145736 | tf_op jit(solution)/shard_map/ppermute | solution.py:739
  5.6 9.2 %collective-permute-start.2 = (f32[32,8,256]{2,1,0:T(8,128)}, f32[32,8,256]{2,1,0:T(8,128)S(1)}, u32[]{:S(2)}, u32[]{:S(2)}) collective-permute-start(f32[32,8,256]{2,1,0:T(8,128)} %get-tuple-element.24), channel_id=1, source_target_pairs={{0,1},{2,3},{1,0},{3,2},{4,5},{6,7},{5,4},{7,6},{8,9},{10,11},{9,8... | collective-permute-start | bytes 786440 | tf_op jit(solution)/shard_map/ppermute | solution.py:739
  8.2 6.6 %collective-permute-start.3 = (f32[32,8,256]{2,1,0:T(8,128)}, f32[32,8,256]{2,1,0:T(8,128)S(1)}, u32[]{:S(2)}, u32[]{:S(2)}) collective-permute-start(f32[32,8,256]{2,1,0:T(8,128)} %get-tuple-element.25), channel_id=1, source_target_pairs={{1,2},{2,1},{5,6},{6,5},{9,10},{10,9},{13,14},{14,13},{17,18},{18,... | collective-permute-start | bytes 786440 | tf_op jit(solution)/shard_map/ppermute | solution.py:739
  14.8 0.7 copy-start.1
  14.8 0.8 copy-start.2
  17.4 28.3 %collective-permute-start.4 = (f32[8,16,256]{2,1,0:T(8,128)}, f32[8,16,256]{2,1,0:T(8,128)S(1)}, u32[]{:S(2)}, u32[]{:S(2)}) collective-permute-start(f32[8,16,256]{2,1,0:T(8,128)} %get-tuple-element.27), channel_id=1, source_target_pairs={{0,4},{8,12},{16,20},{24,28},{4,0},{12,8},{20,16},{28,24},{1,5},{9... | collective-permute-start | bytes 393224 | tf_op jit(solution)/shard_map/ppermute | solution.py:739
  19.1 26.7 %collective-permute-start.5 = (f32[8,16,256]{2,1,0:T(8,128)}, f32[8,16,256]{2,1,0:T(8,128)S(1)}, u32[]{:S(2)}, u32[]{:S(2)}) collective-permute-start(f32[8,16,256]{2,1,0:T(8,128)} %get-tuple-element.28), channel_id=1, source_target_pairs={{4,8},{12,16},{20,24},{8,4},{16,12},{24,20},{5,9},{13,17},{21,25},... | collective-permute-start | bytes 393224 | tf_op jit(solution)/shard_map/ppermute | solution.py:739
  45.7 0.6 copy-start.3
  45.7 0.7 copy-start.4
  45.7 1.0 %copy-start = (f32[8,128,256]{2,1,0:T(8,128)}, f32[8,128,256]{2,1,0:T(8,128)S(1)}, u32[]{:S(2)}) copy-start(f32[8,128,256]{2,1,0:T(8,128)S(1)} %collective-permute-done.first_halo) | copy-start | bytes 3145732

commit v5 on v4

--- a/solution.py
+++ b/solution.py
@@ -37,9 +37,9 @@
 
 
 def tables_kernel(
-    dims, rates, changes, box, truncation,
-    stay, weights, free, offsets, series, firsts, kinds,
-    staged, sem_stay,
+    dims, rates, changes, box, truncation, density, side_send,
+    stay, weights, free, offsets, series, firsts, kinds, first_send, second_send,
+    staged, sent, sem_stay, sem_sends,
 ):
     block_first, block_second, extents, kernel_layers = dims
     rows = block_second + 2 * HALO
@@ -47,6 +47,7 @@
     layers = block_first + 2 * HALO
     anchor_first = lax.axis_index("gx") * block_first - HALO
     anchor_second = lax.axis_index("gy") * block_second - HALO
+    send_loads = start_sends("gx", 0, density, sent, sem_sends)
 
     plain = jnp.int32(REACTIONS - 1)
     for r in range(REACTIONS - 2, -1, -1):
@@ -152,6 +153,8 @@
         at = pl.ds(c * chunk * plane, chunk * plane)
         stay_copies.append(pltpu.make_async_copy(staged.at[at], stay.at[at], sem_stay.at[c]))
         stay_copies[-1].start()
+        if c == 0:
+            send_stores = finish_sends(send_loads, sent, (first_send, second_send), sem_sends)
 
     for h in range(2):
         third = 2 * lane + h
@@ -200,6 +203,7 @@
         for j in range(STEPS + 1, series_length):
             tail = tail + jnp.where(j <= truncation[which], jnp.float32(table[j]), 0.0)
         series[STEPS + which] = jnp.float32(table[STEPS]) + tail
+    wait_all(send_stores)
     wait_all(stay_copies)
 
 
@@ -440,25 +444,29 @@
     lax.fori_loop(0, count // size, several, 0)
 
 
-def sends_kernel(source, *refs):
-    outs, stages, sems = refs[:4], refs[4:6], refs[6]
-    loads, stores = [], []
-    for j, (axis, dim) in enumerate((("gy", 1), ("gx", 0))):
-        odd = lax.axis_index(axis) & 1
-        last = source.shape[dim] - HALO
-        for i, start in enumerate(((1 - odd) * last, odd * last)):
-            at = pl.ds(pl.multiple_of(start, HALO), HALO)
-            piece = source.at[at] if dim == 0 else source.at[:, at]
-            loads.append(pltpu.make_async_copy(piece, stages[j].at[i], sems.at[2 * j + i]))
-    copy_all(loads)
-    for j in range(2):
-        for i in range(2):
-            loads[2 * j + i].wait()
-            stores.append(
-                pltpu.make_async_copy(stages[j].at[i], outs[2 * j + i], sems.at[4 + 2 * j + i])
-            )
-            stores[-1].start()
-    wait_all(stores)
+def start_sends(axis, dim, source, stage, sems):
+    odd = lax.axis_index(axis) & 1
+    last = source.shape[dim] - HALO
+    loads = []
+    for i, start in enumerate(((1 - odd) * last, odd * last)):
+        at = pl.ds(pl.multiple_of(start, HALO), HALO)
+        piece = source.at[at] if dim == 0 else source.at[:, at]
+        loads.append(pltpu.make_async_copy(piece, stage.at[i], sems.at[i]))
+    return copy_all(loads)
+
+
+def finish_sends(loads, stage, outs, sems):
+    stores = []
+    for i, out in enumerate(outs):
+        loads[i].wait()
+        stores.append(pltpu.make_async_copy(stage.at[i], out, sems.at[2 + i]))
+        stores[-1].start()
+    return stores
+
+
+def sends_kernel(source, first, second, stage, sems):
+    loads = start_sends("gy", 1, source, stage, sems)
+    wait_all(finish_sends(loads, stage, (first, second), sems))
 
 
 def corners_kernel(first_in, second_in, offsets, first, second):
@@ -744,29 +752,24 @@
     vmem = pl.BlockSpec(memory_space=pltpu.VMEM)
     hbm = pl.BlockSpec(memory_space=pl.ANY)
     params = pltpu.CompilerParams(vmem_limit_bytes=VMEM_LIMIT)
+    heavy = pl.CostEstimate(flops=200_000_000_000, bytes_accessed=400_000_000, transcendentals=0)
     light = pl.CostEstimate(flops=1000, bytes_accessed=1000, transcendentals=0)
     side_shape = (block_first, HALO, species_third)
     halo_shape = (HALO, block_second, species_third)
-    sends = pl.pallas_call(
+    side_sends = pl.pallas_call(
         sends_kernel,
-        out_shape=(jax.ShapeDtypeStruct(side_shape, f32),) * 2
-        + (jax.ShapeDtypeStruct(halo_shape, f32),) * 2,
+        out_shape=(jax.ShapeDtypeStruct(side_shape, f32),) * 2,
         in_specs=[hbm],
-        out_specs=(hbm,) * 4,
-        scratch_shapes=[
-            pltpu.VMEM((2,) + side_shape, f32),
-            pltpu.VMEM((2,) + halo_shape, f32),
-            pltpu.SemaphoreType.DMA((8,)),
-        ],
+        out_specs=(hbm,) * 2,
+        scratch_shapes=[pltpu.VMEM((2,) + side_shape, f32), pltpu.SemaphoreType.DMA((4,))],
         compiler_params=params,
         cost_estimate=light,
         name="sends",
     )(density)
-    first_side, second_side = exchange(sends[:2], "gy", count_second)
-    first_halo, second_halo = exchange(sends[2:], "gx", count_first)
+    first_side, second_side = exchange(side_sends, "gy", count_second)
 
     table_lanes = -(-(layers + 2 * ABOVE) // LANES) * LANES
-    stay, weights, free, *tables = pl.pallas_call(
+    stay, weights, free, *tables, first_send, second_send = pl.pallas_call(
         functools.partial(tables_kernel, dims),
         out_shape=(
             jax.ShapeDtypeStruct((layers * plane, LANES), f32),
@@ -776,17 +779,22 @@
             jax.ShapeDtypeStruct((STEPS + 2,), f32),
             jax.ShapeDtypeStruct((8, table_lanes), f32),
             jax.ShapeDtypeStruct((8, table_lanes), jnp.int32),
+            jax.ShapeDtypeStruct(halo_shape, f32),
+            jax.ShapeDtypeStruct(halo_shape, f32),
         ),
-        in_specs=[smem] * 4,
-        out_specs=(hbm, vmem, vmem, smem, smem, vmem, vmem),
+        in_specs=[smem] * 4 + [hbm, hbm],
+        out_specs=(hbm, vmem, vmem, smem, smem, vmem, vmem, hbm, hbm),
         scratch_shapes=[
             pltpu.VMEM((layers * plane, LANES), f32),
+            pltpu.VMEM((2,) + halo_shape, f32),
             pltpu.SemaphoreType.DMA((layers // largest_divisor(layers, 8),)),
+            pltpu.SemaphoreType.DMA((4,)),
         ],
         compiler_params=params,
         cost_estimate=light,
         name="tables",
-    )(reaction_rates, state_changes.T, target_box, truncation)
+    )(reaction_rates, state_changes.T, target_box, truncation, density, side_sends[0])
+    first_halo, second_halo = exchange((first_send, second_send), "gx", count_first)
     offsets = tables[0]
 
     corner = jax.ShapeDtypeStruct((HALO, 2 * HALO, species_third), f32)
@@ -831,7 +839,7 @@
             pltpu.SemaphoreType.DMA((block_first // HALO,)),
         ],
         compiler_params=params,
-        cost_estimate=light,
+        cost_estimate=heavy,
         name="interior",
     )(density, first_side, second_side, stay, weights, free, *tables)
 

time: 85.9 us -> 82.9 us (0.965)
  blocking collectives: 17.5 us -> 12 us
  starting transfers between devices: 7.73 us -> 11.5 us
  local copies, waits for them, and re-layouts: 1.78 us -> 0.79 us
    all_to_all x1, blocking collectives: 17.5 us -> 12 us  [body(): rows_in = lax.all_to_all(row, ('gx', 'gy'), 0, 0, tiled=True)]
    ppermute x6, starting transfers between devices: 7.73 us -> 11.5 us  [exchange(): lax.ppermute(piece, axis, pairs + [(j, i) for i, j in pairs])]
    pallas_call x1, Pallas kernels: 2.8 us -> 1.79 us  [body(): pl.pallas_call(sends_kernel, out_shape=(jax.ShapeDtypeStruct(side_shape,...]
    unnamed x10 -> x4, local copies, waits for them, and re-layouts: 1.78 us -> 0.79 us
  transfers between devices with their start and end apart: 6 -> 6, of which waited for: 0 -> 0; matrix products, arithmetic and copies ran while one was open for 0% -> 0% of each run, Pallas kernels for 39% -> 42%
where the time goes in v5:
time: 82.9 us; the launch traced here: 82.3 us
  Pallas kernels  56.8 us (69%)
  blocking collectives  12 us (14%)
  starting transfers between devices  11.5 us (14%)
    pallas_call x1, Pallas kernels, body(): pl.pallas_call(functools.partial(interior_kernel, dims), out_shape=(jax.S...  26.1 us
    pallas_call x1, Pallas kernels, body(): pl.pallas_call(functools.partial(edges_kernel, dims, devices), out_shape=...  20.4 us
    all_to_all x1, blocking collectives, body(): rows_in = lax.all_to_all(row, ('gx', 'gy'), 0, 0, tiled=True)  12 us
    ppermute x6, starting transfers between devices, exchange(): lax.ppermute(piece, axis, pairs + [(j, i) for i, j in pairs])  11.5 us
    pallas_call x1, Pallas kernels, body(): pl.pallas_call(functools.partial(tables_kernel, dims), out_shape=(jax.Sha...  6.77 us
    pallas_call x1, Pallas kernels, body(): pl.pallas_call(sends_kernel, out_shape=(jax.ShapeDtypeStruct(side_shape,...  1.79 us
    pallas_call x1, Pallas kernels, body(): pl.pallas_call(corners_kernel, out_shape=(corner, corner), in_specs=[vmem...  1.77 us
  transfers between devices with their start and end apart: 6, of which 0 were waited for; matrix products, arithmetic and copies ran while one was open for 0% of the time, Pallas kernels for 42%

profile of v5, /device:TPU:0, one launch (start us, length us, event | category | flops | bytes accessed | tf_op | source)
XLA Modules:
  0.0 82.3 jit_solution(1503164144239174216)
XLA Ops:
  0.6 1.8 %sends.1 = (f32[32,8,256]{2,1,0:T(8,128)}, f32[32,8,256]{2,1,0:T(8,128)}) custom-call(f32[32,128,256]{2,1,0:T(8,128)} %density.3), custom_call_target="tpu_custom_call" | custom-call | flops 1000 | bytes 1000 | tf_op jit(solution)/shard_map/sends/pallas_call | solution.py:759
  2.4 0.7 collective-permute-start.3
  3.1 5.9 %collective-permute-start.2 = (f32[32,8,256]{2,1,0:T(8,128)}, f32[32,8,256]{2,1,0:T(8,128)S(1)}, u32[]{:S(2)}, u32[]{:S(2)}) collective-permute-start(f32[32,8,256]{2,1,0:T(8,128)} %get-tuple-element.22.side_send), channel_id=1, source_target_pairs={{0,1},{2,3},{1,0},{3,2},{4,5},{6,7},{5,4},{7,6},{8,9},{10,11},{9,8... | collective-permute-start | bytes 786440 | tf_op jit(solution)/shard_map/ppermute | solution.py:747
  9.0 6.8 %tables.1 = (f32[13824,128]{1,0:T(8,128)}, f32[1728,128]{1,0:T(8,128)}, f32[864,128]{1,0:T(8,128)}, s32[24]{0:T(128)}, f32[6]{0:T(128)}, /*index=5*/f32[8,128]{1...) custom-call(f32[6]{0:T(128)} %rates.1, s32[3,6]{1,0:T(4,128)} %bitcast.7, s32[2,3]{1,0:T(2,128)} %box.1, ...), custom_call_target="tpu_custom_call" | custom-call | flops 1000 | bytes 1000 | tf_op jit(solution)/shard_map/tables/pallas_call | solution.py:772
  15.8 0.1 collective-permute-start
  15.9 1.6 %collective-permute-start.1 = (f32[8,128,256]{2,1,0:T(8,128)}, f32[8,128,256]{2,1,0:T(8,128)}, u32[]{:S(2)}, u32[]{:S(2)}) collective-permute-start(f32[8,128,256]{2,1,0:T(8,128)} %get-tuple-element.24), channel_id=1, source_target_pairs={{4,8},{12,16},{20,24},{8,4},{16,12},{24,20},{5,9},{13,17},{21,25},... | collective-permute-start | bytes 3145736 | tf_op jit(solution)/shard_map/ppermute | solution.py:747
  17.5 0.0 collective-permute-done.3.second_in.second_side
  17.5 0.0 copy-start
  17.5 0.0 collective-permute-done.2.first_in.first_side
  17.5 0.0 copy-start.1
  17.5 0.7 copy-done
  18.2 0.1 copy-done.1
  18.3 1.8 %corners.1 = (f32[8,16,256]{2,1,0:T(8,128)}, f32[8,16,256]{2,1,0:T(8,128)}) custom-call(f32[32,8,256]{2,1,0:T(8,128)} %copy-done.1, f32[32,8,256]{2,1,0:T(8,128)} %copy-done, s32[24]{0:T(128)} %get-tuple-element.26.offsets), custom_call_target="tpu_custom_call" | custom-call | flops 1000 | bytes 1000 | tf_op jit(solution)/shard_map/corners/pallas_call | solution.py:801
  20.1 1.9 %collective-permute-start.4 = (f32[8,16,256]{2,1,0:T(8,128)}, f32[8,16,256]{2,1,0:T(8,128)}, u32[]{:S(2)}, u32[]{:S(2)}) collective-permute-start(f32[8,16,256]{2,1,0:T(8,128)} %get-tuple-element.27), channel_id=1, source_target_pairs={{0,4},{8,12},{16,20},{24,28},{4,0},{12,8},{20,16},{28,24},{1,5},{9... | collective-permute-start | bytes 393224 | tf_op jit(solution)/shard_map/ppermute | solution.py:747
  22.0 1.3 %collective-permute-start.5 = (f32[8,16,256]{2,1,0:T(8,128)}, f32[8,16,256]{2,1,0:T(8,128)}, u32[]{:S(2)}, u32[]{:S(2)}) collective-permute-start(f32[8,16,256]{2,1,0:T(8,128)} %get-tuple-element.28), channel_id=1, source_target_pairs={{4,8},{12,16},{20,24},{8,4},{16,12},{24,20},{5,9},{13,17},{21,25},... | collective-permute-start | bytes 393224 | tf_op jit(solution)/shard_map/ppermute | solution.py:747
  23.3 26.1 %interior.1 = (f32[32,128,256]{2,1,0:T(8,128)}, f32[4,2,3,1152,128]{4,3,2,1,0:T(8,128)}, f32[4,2,576,128]{3,2,1,0:T(8,128)}, f32[2,2304,128]{2,1,0:T(8,128)}, f32[32,128]{1,0:T(8,128)}) custom-call(f32[32,128,256]{2,1,0:T(8,128)} %density.3, f32[32,8,256]{2,1,0:T(8,128)} %copy-done.1, f32[32,8,256]{2,1,0:T(8,128)} %copy-done, ...), custom_call_target="tpu_custom_call" | custom-call | flops 199999995904 | bytes 400000000 | tf_op jit(solution)/shard_map/interior/pallas_call | solution.py:820
  49.4 0.0 collective-permute-done.4.first_corner
  49.4 0.0 collective-permute-done.5.second_corner
  49.4 0.0 collective-permute-done.first_halo
  49.4 0.0 collective-permute-done.1.second_halo
  49.4 20.4 %edges.1 = (f32[32,128,256]{2,1,0:T(8,128)}, f32[32,128]{1,0:T(8,128)}) custom-call(f32[8,128,256]{2,1,0:T(8,128)} %collective-permute-done.first_halo, f32[8,128,256]{2,1,0:T(8,128)} %collective-permute-done.1.second_halo, f32[8,16,256]{2,1,0:T(8,128)} %collective-permute-done.4.first_corner, ...), custom_call_target="tpu_custom_call", output_to_operand_aliasing={{0}: (15, {})} | custom-call | tf_op jit(solution)/shard_map/edges/pallas_call | solution.py:846
  69.8 12.0 %all_to_all.12 = f32[32,1,128]{2,1,0:T(1,128)S(1)} all-to-all(f32[32,1,128]{2,1,0:T(1,128)} %bitcast.6), channel_id=1, replica_groups=mesh['gx'=8,'gy'=4] {'gx','gy'}, dimensions={0} | all-to-all | bytes 32768 | tf_op jit(solution)/shard_map/all_to_all | solution.py:871
  81.8 0.5 slice_reduce_fusion
Async XLA Ops:
  2.4 15.1 %collective-permute-start.3 = (f32[32,8,256]{2,1,0:T(8,128)}, f32[32,8,256]{2,1,0:T(8,128)S(1)}, u32[]{:S(2)}, u32[]{:S(2)}) collective-permute-start(f32[32,8,256]{2,1,0:T(8,128)} %get-tuple-element.25), channel_id=1, source_target_pairs={{1,2},{2,1},{5,6},{6,5},{9,10},{10,9},{13,14},{14,13},{17,18},{18,... | collective-permute-start | bytes 786440 | tf_op jit(solution)/shard_map/ppermute | solution.py:747
  3.1 14.4 %collective-permute-start.2 = (f32[32,8,256]{2,1,0:T(8,128)}, f32[32,8,256]{2,1,0:T(8,128)S(1)}, u32[]{:S(2)}, u32[]{:S(2)}) collective-permute-start(f32[32,8,256]{2,1,0:T(8,128)} %get-tuple-element.22.side_send), channel_id=1, source_target_pairs={{0,1},{2,3},{1,0},{3,2},{4,5},{6,7},{5,4},{7,6},{8,9},{10,11},{9,8... | collective-permute-start | bytes 786440 | tf_op jit(solution)/shard_map/ppermute | solution.py:747
  15.8 33.6 %collective-permute-start = (f32[8,128,256]{2,1,0:T(8,128)}, f32[8,128,256]{2,1,0:T(8,128)}, u32[]{:S(2)}, u32[]{:S(2)}) collective-permute-start(f32[8,128,256]{2,1,0:T(8,128)} %get-tuple-element.23), channel_id=1, source_target_pairs={{0,4},{8,12},{16,20},{24,28},{4,0},{12,8},{20,16},{28,24},{1,5},{9... | collective-permute-start | bytes 3145736 | tf_op jit(solution)/shard_map/ppermute | solution.py:747
  15.9 33.5 %collective-permute-start.1 = (f32[8,128,256]{2,1,0:T(8,128)}, f32[8,128,256]{2,1,0:T(8,128)}, u32[]{:S(2)}, u32[]{:S(2)}) collective-permute-start(f32[8,128,256]{2,1,0:T(8,128)} %get-tuple-element.24), channel_id=1, source_target_pairs={{4,8},{12,16},{20,24},{8,4},{16,12},{24,20},{5,9},{13,17},{21,25},... | collective-permute-start | bytes 3145736 | tf_op jit(solution)/shard_map/ppermute | solution.py:747
  17.5 0.7 copy-start
  17.5 0.8 copy-start.1
  20.1 29.3 %collective-permute-start.4 = (f32[8,16,256]{2,1,0:T(8,128)}, f32[8,16,256]{2,1,0:T(8,128)}, u32[]{:S(2)}, u32[]{:S(2)}) collective-permute-start(f32[8,16,256]{2,1,0:T(8,128)} %get-tuple-element.27), channel_id=1, source_target_pairs={{0,4},{8,12},{16,20},{24,28},{4,0},{12,8},{20,16},{28,24},{1,5},{9... | collective-permute-start | bytes 393224 | tf_op jit(solution)/shard_map/ppermute | solution.py:747
  22.0 27.4 %collective-permute-start.5 = (f32[8,16,256]{2,1,0:T(8,128)}, f32[8,16,256]{2,1,0:T(8,128)}, u32[]{:S(2)}, u32[]{:S(2)}) collective-permute-start(f32[8,16,256]{2,1,0:T(8,128)} %get-tuple-element.28), channel_id=1, source_target_pairs={{4,8},{12,16},{20,24},{8,4},{16,12},{24,20},{5,9},{13,17},{21,25},... | collective-permute-start | bytes 393224 | tf_op jit(solution)/shard_map/ppermute | solution.py:747

commit v6 on v5

--- a/solution.py
+++ b/solution.py
@@ -14,7 +14,7 @@
 LANES = 128
 ROWS = 16
 PAD = 8
-BODY_LAYERS = 28
+BODY_LAYERS = 14
 
 mean_jumps = 8.0
 headroom = 1.05
@@ -266,14 +266,9 @@
                 lanes = masked if turn == 0 else pltpu.roll(masked, 1 if turn < 0 else LANES - 1, 1)
                 q[pl.ds(pl.multiple_of(self.moved(turn, at), 8), rows), :] = lanes
 
-    def coefficients(self, row0):
-        return [
-            [
-                self.weights[pl.ds(pl.multiple_of((r * 2 + h) * self.rows + row0, 8), ROWS), :]
-                for h in range(2)
-            ]
-            for r in range(REACTIONS)
-        ]
+    def coefficient(self, row0, r, h):
+        at = pl.multiple_of((r * 2 + h) * self.rows + row0, 8)
+        return self.weights[pl.ds(at, ROWS), :]
 
     def places(self, segments, row0):
         found = []
@@ -300,7 +295,7 @@
         terms = [value]
         for r in range(REACTIONS):
             arriving = source[pl.ds(sources[r][h] + u * self.plane, ROWS), :]
-            term = arriving * coefficients[r][h]
+            term = arriving * coefficients(r, h)
             terms.append(term if r == 0 else term * firsts[r])
         while len(terms) > 1:
             pairs = [terms[i : i + 2] for i in range(0, len(terms), 2)]
@@ -336,7 +331,7 @@
 
         def group(g, before):
             row0 = pl.multiple_of(g * ROWS, ROWS)
-            coefficients = self.coefficients(row0)
+            coefficients = functools.partial(self.coefficient, row0)
 
             def block(b, before):
                 places = self.places(layout(b), row0)
@@ -389,7 +384,10 @@
 
         def group(g, sums):
             row0 = pl.multiple_of(g * ROWS + HALO, 8)
-            coefficients = self.coefficients(row0)
+            held = [[self.coefficient(row0, r, h) for h in range(2)] for r in range(REACTIONS)]
+
+            def coefficients(r, h):
+                return held[r][h]
 
             def block(b, sums):
                 mass, hit = sums
@@ -467,17 +465,6 @@
 def sends_kernel(source, first, second, stage, sems):
     loads = start_sends("gy", 1, source, stage, sems)
     wait_all(finish_sends(loads, stage, (first, second), sems))
-
-
-def corners_kernel(first_in, second_in, offsets, first, second):
-    odd = lax.axis_index("gx") & 1
-    last = first_in.shape[0] - HALO
-    swapped = (lax.axis_index("gy") & 1) == 0
-    for out, start in ((first, (1 - odd) * last), (second, odd * last)):
-        at = pl.ds(pl.multiple_of(start, HALO), HALO)
-        low, high = first_in[at], second_in[at]
-        out[:, pl.ds(0, HALO)] = jnp.where(swapped, high, low)
-        out[:, pl.ds(HALO, HALO)] = jnp.where(swapped, low, high)
 
 
 def interior_kernel(
@@ -620,14 +607,16 @@
     early, late, imports = [], [], []
     p_imports = [[] for _ in range(STEPS)]
     for side in range(2):
-        first = 2
-        early.append(
-            pltpu.make_async_copy(
-                stay_all.at[pl.ds(((0, right_table)[side] + first) * plane, (SIDE - 4) * plane)],
-                stay.at[pl.ds((side * SIDE + first) * plane, (SIDE - 4) * plane)],
-                sem_other.at[side],
-            )
-        )
+        for i, (first, count) in enumerate(
+            ((2, HALO), (2 + HALO, HALO - 2)) if side == 0 else ((HALO, HALO), (2, HALO - 2))
+        ):
+            (early if i == 0 else p_imports[1]).append(
+                pltpu.make_async_copy(
+                    stay_all.at[pl.ds(((0, right_table)[side] + first) * plane, count * plane)],
+                    stay.at[pl.ds((side * SIDE + first) * plane, count * plane)],
+                    sem_other.at[(0, 5)[i] + side],
+                )
+            )
         late.append(
             pltpu.make_async_copy(
                 acc_edges.at[side],
@@ -798,15 +787,16 @@
     offsets = tables[0]
 
     corner = jax.ShapeDtypeStruct((HALO, 2 * HALO, species_third), f32)
-    corner_sends = pl.pallas_call(
-        corners_kernel,
-        out_shape=(corner, corner),
-        in_specs=[vmem, vmem, smem],
-        out_specs=(vmem, vmem),
-        compiler_params=params,
-        cost_estimate=light,
-        name="corners",
-    )(first_side, second_side, offsets)
+    odd = jnp.where(tables[0][0] < -(10**9), 0, lax.axis_index("gx") & 1)
+    swapped = (lax.axis_index("gy") & 1) == 0
+    lower = jnp.where(swapped, second_side, first_side)
+    upper = jnp.where(swapped, first_side, second_side)
+    corner_sends = [
+        jnp.concatenate(
+            [lax.dynamic_slice_in_dim(x, start, HALO, axis=0) for x in (lower, upper)], axis=1
+        )
+        for start in ((1 - odd) * (block_first - HALO), odd * (block_first - HALO))
+    ]
     first_corner, second_corner = exchange(corner_sends, "gx", count_first)
 
     def scratch(own, totals, moved, steps):
@@ -858,7 +848,7 @@
             pltpu.VMEM((2 * HALO, block_second, species_third), f32),
             pltpu.SemaphoreType.DMA((24,)),
             pltpu.SemaphoreType.DMA((8,)),
-            pltpu.SemaphoreType.DMA((5,)),
+            pltpu.SemaphoreType.DMA((7,)),
             pltpu.SemaphoreType.DMA((2,)),
         ],
         input_output_aliases={15: 0},

time: 82.9 us -> 81.7 us (0.986)
  Pallas kernels: 56.8 us -> 54.4 us
  other arithmetic: 0.53 us -> 1.98 us
    pallas_call x1 -> x0, Pallas kernels: 1.77 us -> none  [body(): pl.pallas_call(corners_kernel, out_shape=(corner, corner), in_specs=[vmem...]
    concatenate x0 -> x2, other arithmetic: none -> 1.41 us  [body(): jnp.concatenate([lax.dynamic_slice_in_dim(x, start, HALO, axis=0) for x i...]
  transfers between devices with their start and end apart: 6 -> 6, of which waited for: 0 -> 0; matrix products, arithmetic and copies ran while one was open for 0% -> 2% of each run, Pallas kernels for 42% -> 40%
where the time goes in v6:
time: 81.7 us; the launch traced here: 81.2 us
  Pallas kernels  54.4 us (67%)
  blocking collectives  12 us (15%)
  starting transfers between devices  11.5 us (14%)
  other arithmetic  1.98 us (2%)
  between operations  1.42 us (2%)
    pallas_call x1, Pallas kernels, body(): pl.pallas_call(functools.partial(interior_kernel, dims), out_shape=(jax.S...  26.1 us
    pallas_call x1, Pallas kernels, body(): pl.pallas_call(functools.partial(edges_kernel, dims, devices), out_shape=...  19.7 us
    all_to_all x1, blocking collectives, body(): rows_in = lax.all_to_all(row, ('gx', 'gy'), 0, 0, tiled=True)  12 us
    ppermute x6, starting transfers between devices, exchange(): lax.ppermute(piece, axis, pairs + [(j, i) for i, j in pairs])  11.5 us
    pallas_call x1, Pallas kernels, body(): pl.pallas_call(functools.partial(tables_kernel, dims), out_shape=(jax.Sha...  6.77 us
    pallas_call x1, Pallas kernels, body(): pl.pallas_call(sends_kernel, out_shape=(jax.ShapeDtypeStruct(side_shape,...  1.79 us
  transfers between devices with their start and end apart: 6, of which 0 were waited for; matrix products, arithmetic and copies ran while one was open for 2% of the time, Pallas kernels for 40%

profile of v6, /device:TPU:0, one launch (start us, length us, event | category | flops | bytes accessed | tf_op | source)
XLA Modules:
  0.0 81.2 jit_solution(15914048865997944136)
XLA Ops:
  0.6 1.8 %sends.1 = (f32[32,8,256]{2,1,0:T(8,128)}, f32[32,8,256]{2,1,0:T(8,128)}) custom-call(f32[32,128,256]{2,1,0:T(8,128)} %density.3), custom_call_target="tpu_custom_call" | custom-call | flops 1000 | bytes 1000 | tf_op jit(solution)/shard_map/sends/pallas_call | solution.py:748
  2.4 0.7 collective-permute-start.2
  3.1 5.9 %collective-permute-start.3 = (f32[32,8,256]{2,1,0:T(8,128)}, f32[32,8,256]{2,1,0:T(8,128)S(1)}, u32[]{:S(2)}, u32[]{:S(2)}) collective-permute-start(f32[32,8,256]{2,1,0:T(8,128)} %get-tuple-element.20.side_send), channel_id=1, source_target_pairs={{0,1},{2,3},{1,0},{3,2},{4,5},{6,7},{5,4},{7,6},{8,9},{10,11},{9,8... | collective-permute-start | bytes 786440 | tf_op jit(solution)/shard_map/ppermute | solution.py:736
  9.0 6.8 %tables.1 = (f32[13824,128]{1,0:T(8,128)}, f32[1728,128]{1,0:T(8,128)}, f32[864,128]{1,0:T(8,128)}, s32[24]{0:T(128)}, f32[6]{0:T(128)}, /*index=5*/f32[8,128]{1...) custom-call(f32[6]{0:T(128)} %rates.1, s32[3,6]{1,0:T(4,128)} %bitcast.9, s32[2,3]{1,0:T(2,128)} %box.1, ...), custom_call_target="tpu_custom_call" | custom-call | flops 1000 | bytes 1000 | tf_op jit(solution)/shard_map/tables/pallas_call | solution.py:761
  15.8 0.1 collective-permute-start
  15.9 1.6 %collective-permute-start.1 = (f32[8,128,256]{2,1,0:T(8,128)}, f32[8,128,256]{2,1,0:T(8,128)}, u32[]{:S(2)}, u32[]{:S(2)}) collective-permute-start(f32[8,128,256]{2,1,0:T(8,128)} %get-tuple-element.22), channel_id=1, source_target_pairs={{4,8},{12,16},{20,24},{8,4},{16,12},{24,20},{5,9},{13,17},{21,25},... | collective-permute-start | bytes 3145736 | tf_op jit(solution)/shard_map/ppermute | solution.py:736
  18.2 0.0 collective-permute-done.2.second_side
  18.2 0.0 copy-start
  18.2 0.0 collective-permute-done.3.first_side
  18.2 0.0 copy-start.1
  18.3 0.7 pad_maximum_fusion
  19.0 1.9 %collective-permute-start.4 = (f32[8,16,256]{2,1,0:T(8,128)}, f32[8,16,256]{2,1,0:T(8,128)}, u32[]{:S(2)}, u32[]{:S(2)}) collective-permute-start(f32[8,16,256]{2,1,0:T(8,128)} %pad_maximum_fusion), channel_id=1, source_target_pairs={{0,4},{8,12},{16,20},{24,28},{4,0},{12,8},{20,16},{28,24},{1,5},{9... | collective-permute-start | bytes 393224 | tf_op jit(solution)/shard_map/ppermute | solution.py:736
  20.9 0.7 pad_maximum_fusion.1
  21.6 1.3 %collective-permute-start.5 = (f32[8,16,256]{2,1,0:T(8,128)}, f32[8,16,256]{2,1,0:T(8,128)}, u32[]{:S(2)}, u32[]{:S(2)}) collective-permute-start(f32[8,16,256]{2,1,0:T(8,128)} %pad_maximum_fusion.1), channel_id=1, source_target_pairs={{4,8},{12,16},{20,24},{8,4},{16,12},{24,20},{5,9},{13,17},{21,25},... | collective-permute-start | bytes 393224 | tf_op jit(solution)/shard_map/ppermute | solution.py:736
  22.9 0.0 copy-done
  22.9 0.0 copy-done.1
  22.9 26.1 %interior.1 = (f32[32,128,256]{2,1,0:T(8,128)}, f32[4,2,3,1152,128]{4,3,2,1,0:T(8,128)}, f32[4,2,576,128]{3,2,1,0:T(8,128)}, f32[2,2304,128]{2,1,0:T(8,128)}, f32[32,128]{1,0:T(8,128)}) custom-call(f32[32,128,256]{2,1,0:T(8,128)} %density.3, f32[32,8,256]{2,1,0:T(8,128)} %copy-done.1, f32[32,8,256]{2,1,0:T(8,128)} %copy-done, ...), custom_call_target="tpu_custom_call" | custom-call | flops 199999995904 | bytes 400000000 | tf_op jit(solution)/shard_map/interior/pallas_call | solution.py:810
  49.0 0.0 collective-permute-done.4.first_corner
  49.0 0.0 collective-permute-done.5.second_corner
  49.0 0.0 collective-permute-done.first_halo
  49.0 0.0 collective-permute-done.1.second_halo
  49.0 19.7 %edges.1 = (f32[32,128,256]{2,1,0:T(8,128)}, f32[32,128]{1,0:T(8,128)}) custom-call(f32[8,128,256]{2,1,0:T(8,128)} %collective-permute-done.first_halo, f32[8,128,256]{2,1,0:T(8,128)} %collective-permute-done.1.second_halo, f32[8,16,256]{2,1,0:T(8,128)} %collective-permute-done.4.first_corner, ...), custom_call_target="tpu_custom_call", output_to_operand_aliasing={{0}: (15, {})} | custom-call | tf_op jit(solution)/shard_map/edges/pallas_call | solution.py:836
  68.8 12.0 %all_to_all.12 = f32[32,1,128]{2,1,0:T(1,128)S(1)} all-to-all(f32[32,1,128]{2,1,0:T(1,128)} %bitcast.8), channel_id=1, replica_groups=mesh['gx'=8,'gy'=4] {'gx','gy'}, dimensions={0} | all-to-all | bytes 32768 | tf_op jit(solution)/shard_map/all_to_all | solution.py:861
  80.7 0.5 slice_reduce_fusion
  (2 shorter events, 0.1 us)
Async XLA Ops:
  2.4 15.7 %collective-permute-start.2 = (f32[32,8,256]{2,1,0:T(8,128)}, f32[32,8,256]{2,1,0:T(8,128)S(1)}, u32[]{:S(2)}, u32[]{:S(2)}) collective-permute-start(f32[32,8,256]{2,1,0:T(8,128)} %get-tuple-element.23), channel_id=1, source_target_pairs={{1,2},{2,1},{5,6},{6,5},{9,10},{10,9},{13,14},{14,13},{17,18},{18,... | collective-permute-start | bytes 786440 | tf_op jit(solution)/shard_map/ppermute | solution.py:736
  3.1 15.1 %collective-permute-start.3 = (f32[32,8,256]{2,1,0:T(8,128)}, f32[32,8,256]{2,1,0:T(8,128)S(1)}, u32[]{:S(2)}, u32[]{:S(2)}) collective-permute-start(f32[32,8,256]{2,1,0:T(8,128)} %get-tuple-element.20.side_send), channel_id=1, source_target_pairs={{0,1},{2,3},{1,0},{3,2},{4,5},{6,7},{5,4},{7,6},{8,9},{10,11},{9,8... | collective-permute-start | bytes 786440 | tf_op jit(solution)/shard_map/ppermute | solution.py:736
  15.8 33.2 %collective-permute-start = (f32[8,128,256]{2,1,0:T(8,128)}, f32[8,128,256]{2,1,0:T(8,128)}, u32[]{:S(2)}, u32[]{:S(2)}) collective-permute-start(f32[8,128,256]{2,1,0:T(8,128)} %get-tuple-element.21), channel_id=1, source_target_pairs={{0,4},{8,12},{16,20},{24,28},{4,0},{12,8},{20,16},{28,24},{1,5},{9... | collective-permute-start | bytes 3145736 | tf_op jit(solution)/shard_map/ppermute | solution.py:736
  15.9 33.2 %collective-permute-start.1 = (f32[8,128,256]{2,1,0:T(8,128)}, f32[8,128,256]{2,1,0:T(8,128)}, u32[]{:S(2)}, u32[]{:S(2)}) collective-permute-start(f32[8,128,256]{2,1,0:T(8,128)} %get-tuple-element.22), channel_id=1, source_target_pairs={{4,8},{12,16},{20,24},{8,4},{16,12},{24,20},{5,9},{13,17},{21,25},... | collective-permute-start | bytes 3145736 | tf_op jit(solution)/shard_map/ppermute | solution.py:736
  18.2 4.7 %copy-start = (f32[32,8,256]{2,1,0:T(8,128)}, f32[32,8,256]{2,1,0:T(8,128)S(1)}, u32[]{:S(2)}) copy-start(f32[32,8,256]{2,1,0:T(8,128)S(1)} %collective-permute-done.2.second_side) | copy-start | bytes 786436
  18.2 4.7 %copy-start.1 = (f32[32,8,256]{2,1,0:T(8,128)}, f32[32,8,256]{2,1,0:T(8,128)S(1)}, u32[]{:S(2)}) copy-start(f32[32,8,256]{2,1,0:T(8,128)S(1)} %collective-permute-done.3.first_side) | copy-start | bytes 786436
  19.0 30.0 %collective-permute-start.4 = (f32[8,16,256]{2,1,0:T(8,128)}, f32[8,16,256]{2,1,0:T(8,128)}, u32[]{:S(2)}, u32[]{:S(2)}) collective-permute-start(f32[8,16,256]{2,1,0:T(8,128)} %pad_maximum_fusion), channel_id=1, source_target_pairs={{0,4},{8,12},{16,20},{24,28},{4,0},{12,8},{20,16},{28,24},{1,5},{9... | collective-permute-start | bytes 393224 | tf_op jit(solution)/shard_map/ppermute | solution.py:736
  21.6 27.4 %collective-permute-start.5 = (f32[8,16,256]{2,1,0:T(8,128)}, f32[8,16,256]{2,1,0:T(8,128)}, u32[]{:S(2)}, u32[]{:S(2)}) collective-permute-start(f32[8,16,256]{2,1,0:T(8,128)} %pad_maximum_fusion.1), channel_id=1, source_target_pairs={{4,8},{12,16},{20,24},{8,4},{16,12},{24,20},{5,9},{13,17},{21,25},... | collective-permute-start | bytes 393224 | tf_op jit(solution)/shard_map/ppermute | solution.py:736
